TPU v7x, 1024 devices: a whole 8x8x8 slice. The times are simulated.
1024 devices in a mesh: vir: 64 (over y, x), occ: 8 (over z), rep: 2 (over core).
Axes of the slice: x: 8, y: 8, z: 8, core: 2. Of those that a mesh axis runs over, the one named last changes fastest.
Arguments:
- amplitudes: bfloat16 [64, 8, 64, 128, 128], P('vir', 'occ', None, 'rep'), may hold values from -6 to 6
- cycle_ints: bfloat16 [8, 1, 64, 128, 128], P('occ'), may hold values from -0.125 to 0.125
- cycle_src: int32 [64, 2], replicated, may hold values from 0 to 63
- cycle_wsel: int32 [64, 2], replicated, may hold values from 0 to 63
- ladder_src: int32 [64, 2], replicated, may hold values from 0 to 63
- owner_order: int32 [64], replicated, may hold values from 0 to 63, each once
- first_integral_blocks: bfloat16 [6, 64, 2, 128, 128], P(None, 'vir'), may hold values from -0.15625 to 0.15625
- right_ints: bfloat16 [6, 64, 2, 128, 128], P(None, 'vir'), may hold values from -0.5 to 0.5
Outputs:
- cycle_part: bfloat16 [64, 1, 64, 128, 128], P('vir', None, 'occ', 'rep')
- ladder_part: bfloat16 [64, 8, 64, 128, 128], P(None, 'occ', 'vir', 'rep')
All inputs are finite; a program needn't handle non-finite values.
Results may differ from a plain program's by a relative error of at most 0.0049.
Values may be sent and summed in bfloat16 or wider, within the bound.
No kernel may reach another device: no remote copies, remote signals or barrier semaphores. Data moves between devices by JAX's collectives and lax.ppermute only.
A program may use at most 64 MiB of HBM per device.

v0:
```python
import math

import jax
import jax.numpy as jnp
from jax import lax
from jax.sharding import PartitionSpec as P


def ladder_blocks(amp_tiles, first_virtual_tiles, right_tiles):
    item_count = amp_tiles.shape[0]
    block_size = math.gcd(item_count, 16)
    grouped = amp_tiles.reshape((item_count // block_size, block_size) + amp_tiles.shape[1:])

    def one_block(group_tiles):
        halved_contribution = jnp.einsum(
            "ipec,qpdc->iqped", group_tiles, right_tiles, preferred_element_type=jnp.float32
        )
        halved_contribution = halved_contribution.astype(jnp.bfloat16)
        return jnp.einsum(
            "yszr,wysrl->wzl",
            first_virtual_tiles,
            halved_contribution,
            preferred_element_type=jnp.float32,
        )

    summed = lax.map(one_block, grouped)
    return summed.reshape((item_count,) + summed.shape[2:])


def shards(
    amplitudes,
    cycle_ints,
    cycle_src,
    cycle_wsel,
    ladder_src,
    owner_order,
    first_integral_blocks,
    right_ints,
):
    held_tiles = amplitudes[0, 0]
    cycle_amps = jnp.take(held_tiles, cycle_src, axis=0)
    cycle_weights = jnp.take(cycle_ints[0], cycle_wsel, axis=1)
    cyclic_contributions = jnp.einsum(
        "spac,jspcb->jsab", cycle_amps, cycle_weights, preferred_element_type=jnp.float32
    )
    cycle_total = lax.psum_scatter(
        cyclic_contributions[None], "occ", scatter_dimension=2, tiled=True
    )
    cycle_part = cycle_total.astype(jnp.bfloat16)
    chosen = jnp.take(ladder_src, owner_order, axis=0)
    outgoing = jnp.take(held_tiles, chosen, axis=0)
    arriving_data = lax.all_to_all(outgoing, "vir", split_axis=0, concat_axis=0, tiled=True)
    first_virtual_tiles = first_integral_blocks[:, 0]
    right_tiles = right_ints[:, 0]
    replica = lax.axis_index("rep")
    row_count = arriving_data.shape[2]
    left_rows = lax.dynamic_slice_in_dim(first_virtual_tiles, replica * row_count, row_count, 3)
    partial_sums = ladder_blocks(arriving_data, left_rows, right_tiles)
    ladder_tiles = lax.psum_scatter(partial_sums, "rep", scatter_dimension=1, tiled=True).astype(
        jnp.bfloat16
    )
    ladder_part = ladder_tiles[:, None, None]
    return (cycle_part, ladder_part)


def solution(mesh):
    in_specs = (
        P("vir", "occ", None, "rep", None),
        P("occ", None, None, None, None),
        P(),
        P(),
        P(),
        P(),
        P(None, "vir", None, None, None),
        P(None, "vir", None, None, None),
    )
    out_specs = (P("vir", None, "occ", "rep", None), P(None, "occ", "vir", "rep", None))
    return jax.shard_map(shards, mesh=mesh, in_specs=in_specs, out_specs=out_specs, check_vma=False)
```

profile of v0, /device:TPU:1, one launch (start us, length us, event | category | flops | bytes accessed | tf_op | source)
XLA Modules:
  0.0 153.1 jit_solution(5837351131303747564)
XLA Ops:
  7.2 0.8 compare_select_fusion.3
  8.0 0.7 compare_and_fusion.2
  8.6 0.8 copy.21
  9.4 0.6 gather_fusion.1
  10.3 3.4 %gather_fusion.3 = bf16[128,64,128]{2,1,0:T(8,128)(2,1)} fusion(bf16[64,64,128]{2,1,0:T(8,128)(2,1)} %bitcast.64, s32[1024]{0:T(1024)S(1)} %pad_clamp_fusion), kind=kCustom, calls=%fused_computation.1.clone | custom fusion | bytes 4194816 | tf_op jit(solution)/shard_map/jit(_take)/gather | solution.py:51
  13.6 3.2 %broadcast_select_fusion = bf16[64,2,64,128]{3,2,1,0:T(8,128)(2,1)} fusion(bf16[64,2,64,128]{3,2,1,0:T(8,128)(2,1)} %bitcast.66, pred[64,2]{1,0:T(8,128)(4,1)S(1)} %get-tuple-element.41), kind=kLoop, calls=%fused_computation.20 | loop fusion | flops 1048576 | bytes 4194432 | tf_op jit(solution)/shard_map/jit(_take)/select_n | solution.py:51
  16.9 14.4 %all-to-all-start = ((bf16[64,2,64,128]{3,2,1,0:T(8,128)(2,1)}), bf16[64,2,64,128]{3,2,1,0:T(8,128)(2,1)}, u32[]{:S(2)}, u32[]{:S(2)}) async-start(bf16[64,2,64,128]{3,2,1,0:T(8,128)(2,1)} %broadcast_select_fusion), calls=%async_computation.1 | async-start | bytes 4194304 | tf_op jit(solution)/shard_map/all_to_all | solution.py:52
  31.5 0.1 reshape.77
  31.6 2.2 %gather_fusion.2 = bf16[128,64,128]{2,1,0:T(8,128)(2,1)} fusion(bf16[64,64,128]{2,1,0:T(8,128)(2,1)S(1)} %bitcast.65, s32[1024]{0:T(1024)S(1)} %pad_clamp_fusion.3), kind=kCustom, calls=%fused_computation.clone | custom fusion | bytes 4194816 | tf_op jit(solution)/shard_map/jit(_take)/gather | solution.py:41
  33.9 0.1 reshape.53
  34.3 3.0 %gather_fusion = bf16[128,128,128]{2,1,0:T(8,128)(2,1)} fusion(bf16[64,128,128]{2,1,0:T(8,128)(2,1)S(1)} %bitcast.63, s32[1024]{0:T(1024)S(1)} %pad_clamp_fusion.2), kind=kCustom, calls=%fused_computation.2 | custom fusion | bytes 8389120 | tf_op jit(solution)/shard_map/jit(_take)/gather | solution.py:42
  37.4 5.6 %fusion.23 = f32[1,1,64,64,128]{4,3,2,1,0:T(8,128)} fusion(bf16[64,2,128,128]{3,2,1,0:T(8,128)(2,1)} %bitcast.68, pred[64,2]{1,0:T(8,128)(4,1)S(1)} %copy.17, bf16[64,2,64,128]{3,2,1,0:T(8,128)(2,1)} %bitcast.69, pred[64,2]{1,0:T(8,128)(4,1)S(1)} %copy.19), kind=kOutput, calls=%fused_computation.22 | convolution fusion | flops 271581184 | bytes 8388864 | tf_op jit(solution)/shard_map/spac,jspcb->jsab/dot_general | solution.py:43
  43.0 0.9 copy-done.2
  43.9 0.2 constant_dynamic-slice_fusion
  44.1 0.2 copy.22
  44.3 31.7 %all-to-all-done = bf16[64,2,64,128]{3,2,1,0:T(8,128)(2,1)} async-done(((bf16[64,2,64,128]{3,2,1,0:T(8,128)(2,1)}), bf16[64,2,64,128]{3,2,1,0:T(8,128)(2,1)}, u32[]{:S(2)}, u32[]{:S(2)}) %all-to-all-start) | async-done | bytes 2097184 | tf_op jit(solution)/shard_map/all_to_all | solution.py:52
  76.0 27.0 %while.10 = (s32[]{:T(128)}, f32[4,16,128,128]{3,2,1,0:T(8,128)}, bf16[4,16,2,64,128]{4,3,2,1,0:T(8,128)(2,1)}, bf16[6,2,128,128]{3,2,1,0:T(8,128)(2,1)}, bf16[6,2,128,64]{2,3,0,1:T(8,128)(2,1)S(1)}, /*index=5*/s32[]{:T(128)}) while((s32[]{:T(128)}, f32[4,16,128,128]{3,2,1,0:T(8,128)}, bf16[4,16,2,64,128]{4,3,2,1,0:T(8,128)(2,1)}, ...), condition=%wide.region_2.4_spmd, body=%wide.region_1.3_spmd.sunk | while | flops 806879232 | bytes 6358085 | solution.py:26
  76.0 4.1 %fusion.42 = f32[1,16,128,128]{2,3,1,0:T(8,128)} fusion(bf16[4,16,2,64,128]{4,3,2,1,0:T(8,128)(2,1)} %get-tuple-element.88, s32[]{:T(128)} %get-tuple-element.80, bf16[6,2,128,64]{2,3,0,1:T(8,128)(2,1)S(1)} %get-tuple-element.90, bf16[6,2,128,128]{3,2,1,0:T(8,128)(2,1)} %get-tuple-element.89), kind=kOutput, calls=%fused_computation.8.clone.1 | convolution fusion | flops 806879232 | bytes 2163200 | tf_op jit(solution)/shard_map/while/body/eval_jaxpr/yszr,wysrl->wzl/dot_general | solution.py:19
  80.1 1.6 %copy.38 = f32[1,16,128,128]{3,2,1,0:T(8,128)S(1)} copy(f32[1,16,128,128]{2,3,1,0:T(8,128)} %fusion.42) | data formatting | bytes 2097152 | tf_op jit(solution)/shard_map/while/body/jit(dynamic_update_index_in_dim)/dynamic_update_slice | solution.py:26
  81.7 1.0 constant_dynamic-update-slice_fusion.2
  82.7 4.1 %fusion.42 = f32[1,16,128,128]{2,3,1,0:T(8,128)} fusion(bf16[4,16,2,64,128]{4,3,2,1,0:T(8,128)(2,1)} %get-tuple-element.88, s32[]{:T(128)} %get-tuple-element.80, bf16[6,2,128,64]{2,3,0,1:T(8,128)(2,1)S(1)} %get-tuple-element.90, bf16[6,2,128,128]{3,2,1,0:T(8,128)(2,1)} %get-tuple-element.89), kind=kOutput, calls=%fused_computation.8.clone.1 | convolution fusion | flops 806879232 | bytes 2163200 | tf_op jit(solution)/shard_map/while/body/eval_jaxpr/yszr,wysrl->wzl/dot_general | solution.py:19
  86.8 1.6 %copy.38 = f32[1,16,128,128]{3,2,1,0:T(8,128)S(1)} copy(f32[1,16,128,128]{2,3,1,0:T(8,128)} %fusion.42) | data formatting | bytes 2097152 | tf_op jit(solution)/shard_map/while/body/jit(dynamic_update_index_in_dim)/dynamic_update_slice | solution.py:26
  88.4 1.1 constant_dynamic-update-slice_fusion.2
  89.5 4.1 %fusion.42 = f32[1,16,128,128]{2,3,1,0:T(8,128)} fusion(bf16[4,16,2,64,128]{4,3,2,1,0:T(8,128)(2,1)} %get-tuple-element.88, s32[]{:T(128)} %get-tuple-element.80, bf16[6,2,128,64]{2,3,0,1:T(8,128)(2,1)S(1)} %get-tuple-element.90, bf16[6,2,128,128]{3,2,1,0:T(8,128)(2,1)} %get-tuple-element.89), kind=kOutput, calls=%fused_computation.8.clone.1 | convolution fusion | flops 806879232 | bytes 2163200 | tf_op jit(solution)/shard_map/while/body/eval_jaxpr/yszr,wysrl->wzl/dot_general | solution.py:19
  93.6 1.6 %copy.38 = f32[1,16,128,128]{3,2,1,0:T(8,128)S(1)} copy(f32[1,16,128,128]{2,3,1,0:T(8,128)} %fusion.42) | data formatting | bytes 2097152 | tf_op jit(solution)/shard_map/while/body/jit(dynamic_update_index_in_dim)/dynamic_update_slice | solution.py:26
  95.2 1.1 constant_dynamic-update-slice_fusion.2
  96.2 4.1 %fusion.42 = f32[1,16,128,128]{2,3,1,0:T(8,128)} fusion(bf16[4,16,2,64,128]{4,3,2,1,0:T(8,128)(2,1)} %get-tuple-element.88, s32[]{:T(128)} %get-tuple-element.80, bf16[6,2,128,64]{2,3,0,1:T(8,128)(2,1)S(1)} %get-tuple-element.90, bf16[6,2,128,128]{3,2,1,0:T(8,128)(2,1)} %get-tuple-element.89), kind=kOutput, calls=%fused_computation.8.clone.1 | convolution fusion | flops 806879232 | bytes 2163200 | tf_op jit(solution)/shard_map/while/body/eval_jaxpr/yszr,wysrl->wzl/dot_general | solution.py:19
  100.4 1.6 %copy.38 = f32[1,16,128,128]{3,2,1,0:T(8,128)S(1)} copy(f32[1,16,128,128]{2,3,1,0:T(8,128)} %fusion.42) | data formatting | bytes 2097152 | tf_op jit(solution)/shard_map/while/body/jit(dynamic_update_index_in_dim)/dynamic_update_slice | solution.py:26
  101.9 1.1 constant_dynamic-update-slice_fusion.2
  103.0 1.6 %convert_element_type.12 = bf16[1,1,8,64,128]{4,3,2,1,0:T(8,128)(2,1)} convert(f32[1,1,8,64,128]{4,3,2,1,0:T(8,128)} %reduce-scatter.3.cloned.1.call-done) | non-fusion elementwise | flops 65536 | bytes 393216 | tf_op jit(solution)/shard_map/convert_element_type | solution.py:49
  104.7 38.8 %reduce-scatter.5.cloned.1.call-done = f32[64,64,128]{2,1,0:T(8,128)} async-done(((f32[64,128,128]{2,1,0:T(8,128)}), f32[64,64,128]{2,1,0:T(8,128)}) %reduce-scatter.5.cloned.1.call-update) | async-done | bytes 2097168 | tf_op jit(solution)/shard_map/reduce_scatter | solution.py:59
  143.5 2.8 %convert_bitcast_fusion = bf16[64,1,1,64,128]{4,3,2,1,0:T(8,128)(2,1)} fusion(f32[64,64,128]{2,1,0:T(8,128)} %reduce-scatter.5.cloned.1.call-done), kind=kLoop, calls=%fused_computation.24 | loop fusion | flops 524288 | bytes 3145728 | tf_op jit(solution)/shard_map/broadcast_in_dim | solution.py:62
  (29 shorter events, 0.9 us)
Async XLA Ops:
  7.2 27.2 %copy-start = (bf16[1,1,64,128,128]{4,3,2,1,0:T(8,128)(2,1)S(1)}, bf16[1,1,64,128,128]{4,3,2,1,0:T(8,128)(2,1)}, u32[]{:S(2)}) copy-start(bf16[1,1,64,128,128]{4,3,2,1,0:T(8,128)(2,1)} %param.13) | copy-start | bytes 6291460
  16.9 14.5 %copy-start.4 = (s32[64,2]{0,1:T(2,128)S(1)}, s32[64,2]{0,1:T(2,128)}, u32[]{:S(2)}) copy-start(s32[64,2]{0,1:T(2,128)} %param.14) | copy-start | bytes 1540
  16.9 14.8 %copy-start.1 = (bf16[1,1,64,64,128]{4,3,2,1,0:T(8,128)(2,1)S(1)}, bf16[1,1,64,64,128]{4,3,2,1,0:T(8,128)(2,1)}, u32[]{:S(2)}) copy-start(bf16[1,1,64,64,128]{4,3,2,1,0:T(8,128)(2,1)} %param.12) | copy-start | bytes 3145732
  16.9 59.1 %all-to-all-start = ((bf16[64,2,64,128]{3,2,1,0:T(8,128)(2,1)}), bf16[64,2,64,128]{3,2,1,0:T(8,128)(2,1)}, u32[]{:S(2)}, u32[]{:S(2)}) async-start(bf16[64,2,64,128]{3,2,1,0:T(8,128)(2,1)} %broadcast_select_fusion), calls=%async_computation.1 | async-start | bytes 4194304 | tf_op jit(solution)/shard_map/all_to_all | solution.py:52
  31.3 71.7 %reduce-scatter.3.cloned.1.call-start = ((), (), s32[]{:S(2)}) async-start(), calls=%async_computation.3 | async-start | bytes 2359296 | tf_op jit(solution)/shard_map/reduce_scatter | solution.py:46
  31.6 2.2 %copy-start.3 = (s32[64,2]{0,1:T(2,128)S(1)}, s32[64,2]{0,1:T(2,128)}, u32[]{:S(2)}) copy-start(s32[64,2]{0,1:T(2,128)} %param.15) | copy-start | bytes 1540
  42.9 1.0 copy-start.2
  43.0 100.5 %reduce-scatter.5.cloned.1.call-start = ((), (), s32[]{:S(2)}) async-start(), calls=%async_computation.4 | async-start | bytes 6291456 | tf_op jit(solution)/shard_map/reduce_scatter | solution.py:59
Sparse Core Ops, SparseCore 0:
  43.1 56.0 reduce-scatter.2
  103.1 40.3 reduce-scatter.4
where the time goes:
time: 154 us; the launch traced here: 153 us
  waiting for transfers between devices  70.6 us (46%)
  local copies, waits for them, and re-layouts  22.6 us (15%)
  matrix products  22 us (14%)
  starting transfers between devices  14.5 us (9%)
  between operations  14.2 us (9%)
  other arithmetic  9.21 us (6%)
    reduce_scatter x1, waiting for transfers between devices, shards(): lax.psum_scatter(partial_sums, 'rep', scatter_dimension=1, tiled=True)  38.8 us
    all_to_all x1, waiting for transfers between devices, shards(): lax.all_to_all(outgoing, 'vir', split_axis=0, concat_axis=0, tiled=True)  31.7 us
    dot_general x4, matrix products, one_block(): jnp.einsum('yszr,wysrl->wzl', first_virtual_tiles, halved_contribution, p...  16.5 us
    all_to_all x1, starting transfers between devices, shards(): lax.all_to_all(outgoing, 'vir', split_axis=0, concat_axis=0, tiled=True)  14.4 us
    dynamic_update_slice x8, local copies, waits for them, and re-layouts, ladder_blocks(): summed = lax.map(one_block, grouped)  10.5 us
    dot_general x1, matrix products, shards(): jnp.einsum('spac,jspcb->jsab', cycle_amps, cycle_weights, preferred_eleme...  5.58 us
    gather x1, local copies, waits for them, and re-layouts, shards(): outgoing = jnp.take(held_tiles, chosen, axis=0)  3.38 us
    select_n x1, other arithmetic, shards(): outgoing = jnp.take(held_tiles, chosen, axis=0)  3.22 us
  transfers between devices with their start and end apart: 3, of which 2 were waited for; matrix products, arithmetic and copies ran while one was open for 26% of the time, Pallas kernels for 0%

commit v1 on v0

v1 whole, which is shorter than its diff:
```python
import jax
import jax.numpy as jnp
from jax import lax
from jax.experimental import pallas as pl
from jax.experimental.pallas import tpu as pltpu
from jax.sharding import PartitionSpec as P

GROUP = 16


def gather_kernel(order_ref, src_ref, tiles_ref, out_ref):
    count, terms = out_ref.shape[0], out_ref.shape[1]

    def one(m, carry):
        slot = order_ref[m]
        for p in range(terms):
            out_ref[m, p] = tiles_ref[src_ref[p, slot]]
        return carry

    lax.fori_loop(0, count, one, 0, unroll=8)


def whole(shape):
    return pl.BlockSpec(shape, lambda g, *_: (0,) * len(shape))


def gather_tiles(order, src, tiles):
    terms, count = src.shape
    out_shape = (count, terms) + tiles.shape[1:]
    return pl.pallas_call(
        gather_kernel,
        grid_spec=pltpu.PrefetchScalarGridSpec(
            num_scalar_prefetch=2,
            grid=(1,),
            in_specs=[whole(tiles.shape)],
            out_specs=whole(out_shape),
        ),
        out_shape=jax.ShapeDtypeStruct(out_shape, tiles.dtype),
        compiler_params=pltpu.CompilerParams(vmem_limit_bytes=8 << 20),
        cost_estimate=pl.CostEstimate(flops=0, bytes_accessed=4 << 20, transcendentals=0),
        name="outgoing_tiles",
    )(order, src, tiles)


def cycle_kernel(me_ref, src_ref, wsel_ref, amps_ref, ints_ref, *out_refs):
    terms, holders, share = src_ref.shape[0], len(out_refs), out_refs[0].shape[0]
    me = me_ref[0]
    for step, out_ref in enumerate(out_refs):
        base = lax.rem(me + step, holders) * share

        def one(t, carry):
            s = base + t
            left = jnp.concatenate([amps_ref[src_ref[p, s]] for p in range(terms)], axis=1)
            right = jnp.concatenate([ints_ref[wsel_ref[p, s]] for p in range(terms)], axis=0)
            total = jnp.dot(left, right, preferred_element_type=jnp.float32)
            out_ref[t] = total.astype(out_ref.dtype)
            return carry

        lax.fori_loop(0, share, one, 0, unroll=4)


def cycle_partials(me, holders, src, wsel, amps, ints):
    share = src.shape[1] // holders
    out_shape = (share,) + amps.shape[1:]
    return pl.pallas_call(
        cycle_kernel,
        grid_spec=pltpu.PrefetchScalarGridSpec(
            num_scalar_prefetch=3,
            grid=(1,),
            in_specs=[whole(amps.shape), whole(ints.shape)],
            out_specs=[whole(out_shape)] * holders,
        ),
        out_shape=[jax.ShapeDtypeStruct(out_shape, jnp.bfloat16)] * holders,
        compiler_params=pltpu.CompilerParams(vmem_limit_bytes=12 << 20),
        cost_estimate=pl.CostEstimate(flops=2 * 64 * 64 * 256 * 128, bytes_accessed=4 << 20, transcendentals=0),
        name="cycle_partials",
    )(me, src, wsel, amps, ints)


def ladder_kernel(amps_ref, left_ref, right_ref, own_ref, other_ref):
    group, terms, rows, width = amps_ref.shape
    vectors = right_ref.shape[1] // width
    half = own_ref.shape[1]
    left = left_ref[...]
    sub = 4
    for start in range(0, group, sub):
        halves = []
        for p in range(terms):
            tiles = amps_ref[start : start + sub, p].reshape(sub * rows, width)
            product = lax.dot_general(
                tiles, right_ref[p], (((1,), (1,)), ((), ())), preferred_element_type=jnp.float32
            )
            halves.append(product.astype(jnp.bfloat16))
        for first in range(0, sub, 2):
            columns = []
            for i in (first, first + 1):
                columns.append(
                    jnp.concatenate(
                        [
                            halves[p][i * rows : (i + 1) * rows, q * width : (q + 1) * width]
                            for p in range(terms)
                            for q in range(vectors)
                        ],
                        axis=0,
                    )
                )
            summed = jnp.dot(left, jnp.concatenate(columns, axis=1), preferred_element_type=jnp.float32)
            for place in range(2):
                tile = summed[:, place * width : (place + 1) * width]
                own_ref[start + first + place] = tile[:half]
                other_ref[start + first + place] = tile[half:].astype(other_ref.dtype)


def ladder_partials(amps, left, right):
    items, terms, rows, width = amps.shape
    half = left.shape[0] // 2
    return pl.pallas_call(
        ladder_kernel,
        grid=(items // GROUP,),
        in_specs=[
            pl.BlockSpec((GROUP, terms, rows, width), lambda g: (g, 0, 0, 0)),
            pl.BlockSpec(left.shape, lambda g: (0, 0)),
            pl.BlockSpec(right.shape, lambda g: (0, 0, 0)),
        ],
        out_specs=[
            pl.BlockSpec((GROUP, half, width), lambda g: (g, 0, 0)),
            pl.BlockSpec((GROUP, half, width), lambda g: (g, 0, 0)),
        ],
        out_shape=[
            jax.ShapeDtypeStruct((items, half, width), jnp.float32),
            jax.ShapeDtypeStruct((items, half, width), jnp.bfloat16),
        ],
        compiler_params=pltpu.CompilerParams(vmem_limit_bytes=12 << 20),
        cost_estimate=pl.CostEstimate(flops=32 << 27, bytes_accessed=6 << 20, transcendentals=0),
        name="ladder_partials",
    )(amps, left, right)


def sum_kernel(*refs):
    out_ref = refs[-1]
    total = refs[0][...].astype(jnp.float32)
    for part_ref in refs[1:-1]:
        total = total + part_ref[...].astype(jnp.float32)
    out_ref[...] = total.astype(out_ref.dtype)


def sum_parts(parts):
    size = parts[0].size
    return pl.pallas_call(
        sum_kernel,
        in_specs=[pl.BlockSpec(memory_space=pltpu.VMEM)] * len(parts),
        out_specs=pl.BlockSpec(memory_space=pltpu.VMEM),
        out_shape=jax.ShapeDtypeStruct(parts[0].shape, parts[0].dtype),
        cost_estimate=pl.CostEstimate(flops=8 * size, bytes_accessed=18 * size, transcendentals=0),
        name="sum_parts",
    )(*parts)


def shards(
    amplitudes,
    cycle_ints,
    cycle_src,
    cycle_wsel,
    ladder_src,
    owner_order,
    first_integral_blocks,
    right_ints,
):
    held_tiles = amplitudes[0, 0]
    tile_count, row_count, width = held_tiles.shape

    outgoing = gather_tiles(owner_order, ladder_src.T, held_tiles)
    arriving = lax.all_to_all(outgoing, "vir", split_axis=0, concat_axis=0, tiled=True)

    holders = lax.axis_size("occ")
    me = lax.axis_index("occ").astype(jnp.int32).reshape(1)
    partials = cycle_partials(me, holders, cycle_src.T, cycle_wsel.T, held_tiles, cycle_ints[0, 0])
    parts = [partials[0]]
    for step in sorted(range(1, holders), key=lambda step: (abs(step - holders // 2), step)):
        ring = [(k, (k + step) % holders) for k in range(holders)]
        parts.append(lax.ppermute(partials[step], "occ", ring))
    cycle_part = sum_parts(parts)
    arriving, cycle_part = lax.optimization_barrier((arriving, cycle_part))
    cycle_part = cycle_part[None, None]

    replica = lax.axis_index("rep")
    left = lax.dynamic_slice_in_dim(first_integral_blocks[:, 0], replica * row_count, row_count, 3)
    left = jnp.transpose(left, (2, 1, 0, 3)).reshape(width, -1)
    own_rows = lax.dynamic_slice_in_dim(left, replica * row_count, row_count, 0)
    other_rows = lax.dynamic_slice_in_dim(left, (1 - replica) * row_count, row_count, 0)
    left = jnp.concatenate([own_rows, other_rows], axis=0)
    right = jnp.transpose(right_ints[:, 0], (1, 0, 2, 3)).reshape(right_ints.shape[2], -1, width)

    own, other = ladder_partials(arriving, left, right)
    received = lax.ppermute(other, "rep", [(0, 1), (1, 0)])
    ladder_part = (own + received.astype(jnp.float32)).astype(jnp.bfloat16)[:, None, None]
    return (cycle_part, ladder_part)


def solution(mesh):
    in_specs = (
        P("vir", "occ", None, "rep", None),
        P("occ", None, None, None, None),
        P(),
        P(),
        P(),
        P(),
        P(None, "vir", None, None, None),
        P(None, "vir", None, None, None),
    )
    out_specs = (P("vir", None, "occ", "rep", None), P(None, "occ", "vir", "rep", None))
    return jax.shard_map(shards, mesh=mesh, in_specs=in_specs, out_specs=out_specs, check_vma=False)
```

time: 154 us -> 87 us (0.56)
  waiting for transfers between devices: 70.6 us -> 6.23 us
  starting transfers between devices: 14.5 us -> 55.9 us
  matrix products: 22 us -> 0 us
  local copies, waits for them, and re-layouts: 22.6 us -> 6.05 us
  Pallas kernels: 0 us -> 16 us
  between operations: 14.2 us -> 0.93 us
  other arithmetic: 9.21 us -> 1.32 us
    ppermute x0 -> x8, starting transfers between devices: none -> 41.3 us  [the longest x7 37.8 us: shards(): parts.append(lax.ppermute(partials[step], 'occ', ring))]
    reduce_scatter x2 -> x0, waiting for transfers between devices: 38.8 us -> none  [the longest x1 38.8 us: shards(): lax.psum_scatter(partial_sums, 'rep', scatter_dimension=1, tiled=True)]
    all_to_all x1, waiting for transfers between devices: 31.7 us -> 0.01 us  [shards(): lax.all_to_all(outgoing, 'vir', split_axis=0, concat_axis=0, tiled=True)]
    dot_general x5 -> x0, matrix products: 22 us -> none  [the longest x4 16.5 us: one_block(): jnp.einsum('yszr,wysrl->wzl', first_virtual_tiles, halved_contribution, p...]
    pallas_call x0 -> x4, Pallas kernels: none -> 16 us  [the longest x1 7.65 us: ladder_partials(): pl.pallas_call(ladder_kernel, grid=(items // GROUP,), in_specs=[pl.BlockS...]
    dynamic_update_slice x8 -> x0, local copies, waits for them, and re-layouts: 10.5 us -> none  [ladder_blocks(): summed = lax.map(one_block, grouped)]
    gather x4 -> x0, local copies, waits for them, and re-layouts: 9.16 us -> none  [the longest x1 3.38 us: shards(): outgoing = jnp.take(held_tiles, chosen, axis=0)]
    ppermute x0 -> x8, waiting for transfers between devices: none -> 6.23 us  [the longest x7 3.97 us: shards(): parts.append(lax.ppermute(partials[step], 'occ', ring))]
  transfers between devices with their start and end apart: 3 -> 9, of which waited for: 2 -> 3; matrix products, arithmetic and copies ran while one was open for 26% -> 1% of each run, Pallas kernels for 0% -> 7%
where the time goes in v1:
time: 87 us; the launch traced here: 86.4 us
  starting transfers between devices  55.9 us (64%)
  Pallas kernels  16 us (18%)
  waiting for transfers between devices  6.23 us (7%)
  local copies, waits for them, and re-layouts  6.05 us (7%)
  other arithmetic  1.32 us (2%)
  between operations  0.93 us (1%)
    ppermute x7, starting transfers between devices, shards(): parts.append(lax.ppermute(partials[step], 'occ', ring))  37.8 us
    all_to_all x1, starting transfers between devices, shards(): lax.all_to_all(outgoing, 'vir', split_axis=0, concat_axis=0, tiled=True)  14.6 us
    pallas_call x1, Pallas kernels, ladder_partials(): pl.pallas_call(ladder_kernel, grid=(items // GROUP,), in_specs=[pl.BlockS...  7.65 us
    unnamed x40, local copies, waits for them, and re-layouts  5.49 us
    pallas_call x1, Pallas kernels, cycle_partials(): pl.pallas_call(cycle_kernel, grid_spec=pltpu.PrefetchScalarGridSpec(num_s...  4.14 us
    ppermute x7, waiting for transfers between devices, shards(): parts.append(lax.ppermute(partials[step], 'occ', ring))  3.97 us
    ppermute x1, starting transfers between devices, shards(): received = lax.ppermute(other, 'rep', [(0, 1), (1, 0)])  3.49 us
    ppermute x1, waiting for transfers between devices, shards(): received = lax.ppermute(other, 'rep', [(0, 1), (1, 0)])  2.26 us
  transfers between devices with their start and end apart: 9, of which 3 were waited for; matrix products, arithmetic and copies ran while one was open for 1% of the time, Pallas kernels for 7%

profile of v1, /device:TPU:1, one launch (start us, length us, event | category | flops | bytes accessed | tf_op | source)
XLA Modules:
  0.0 86.4 jit_solution(17437559309564193575)
XLA Ops:
  0.6 0.0 copy-start
  0.6 0.0 copy-start.1
  0.7 1.3 %copy-done.1 = bf16[1,1,64,64,128]{4,3,2,1,0:T(8,128)(2,1)S(1)} copy-done((bf16[1,1,64,64,128]{4,3,2,1,0:T(8,128)(2,1)S(1)}, bf16[1,1,64,64,128]{4,3,2,1,0:T(8,128)(2,1)}, u32[]{:S(2)}) %copy-start.1) | copy-done | bytes 1048600
  1.9 0.7 copy-done.5
  2.6 0.7 copy-done.8
  3.3 2.1 %outgoing_tiles.1 = bf16[64,2,64,128]{3,2,1,0:T(8,128)(2,1)} custom-call(s32[64]{0:T(128)S(1)} %copy-done.8, s32[2,64]{1,0:T(2,128)S(1)} %bitcast.25, bf16[64,64,128]{2,1,0:T(8,128)(2,1)S(1)} %bitcast.21), custom_call_target="tpu_custom_call" | custom-call | bytes 4194304 | tf_op jit(solution)/shard_map/outgoing_tiles/pallas_call | solution.py:30
  5.4 14.6 %all-to-all-start = ((bf16[64,2,64,128]{3,2,1,0:T(8,128)(2,1)}), bf16[64,2,64,128]{3,2,1,0:T(8,128)(2,1)}, u32[]{:S(2)}, u32[]{:S(2)}) async-start(bf16[64,2,64,128]{3,2,1,0:T(8,128)(2,1)} %outgoing_tiles.1), calls=%async_computation | async-start | bytes 4194304 | tf_op jit(solution)/shard_map/all_to_all | solution.py:173
  20.0 4.1 %cycle_partials.1 = (bf16[8,64,128]{2,1,0:T(8,128)(2,1)S(1)}, bf16[8,64,128]{2,1,0:T(8,128)(2,1)S(1)}, bf16[8,64,128]{2,1,0:T(8,128)(2,1)}, bf16[8,64,128]{2,1,0...) custom-call(s32[1]{0:T(128)} %bitcast.2.me_ref, ...), custom_call_target="tpu_custom_call" | custom-call | flops 268435456 | bytes 4194304 | tf_op jit(solution)/shard_map/cycle_partials/pallas_call | solution.py:65
  24.2 0.7 copy-done.4
  24.8 0.6 copy-done.9
  25.5 0.7 copy-done.10
  26.1 14.4 %collective-permute-start = (bf16[8,64,128]{2,1,0:T(8,128)(2,1)}, bf16[8,64,128]{2,1,0:T(8,128)(2,1)S(1)}, u32[]{:S(2)}, u32[]{:S(2)}) collective-permute-start(bf16[8,64,128]{2,1,0:T(8,128)(2,1)} %get-tuple-element.15), channel_id=1, source_target_pairs={{0,8},{2,10},{4,12},{6,14},{8,0},{10,2},{12,4},{14,6},{1,9},{3,11}... | collective-permute-start | bytes 393224 | tf_op jit(solution)/shard_map/ppermute | solution.py:181
  40.5 7.6 %collective-permute-start.1 = (bf16[8,64,128]{2,1,0:T(8,128)(2,1)}, bf16[8,64,128]{2,1,0:T(8,128)(2,1)S(1)}, u32[]{:S(2)}, u32[]{:S(2)}) collective-permute-start(bf16[8,64,128]{2,1,0:T(8,128)(2,1)} %get-tuple-element.16), channel_id=1, source_target_pairs={{0,6},{2,8},{4,10},{6,12},{8,14},{10,0},{12,2},{14,4},{1,7},{3,9},... | collective-permute-start | bytes 393224 | tf_op jit(solution)/shard_map/ppermute | solution.py:181
  48.2 1.9 %collective-permute-start.2 = (bf16[8,64,128]{2,1,0:T(8,128)(2,1)}, bf16[8,64,128]{2,1,0:T(8,128)(2,1)S(1)}, u32[]{:S(2)}, u32[]{:S(2)}) collective-permute-start(bf16[8,64,128]{2,1,0:T(8,128)(2,1)} %get-tuple-element.17), channel_id=1, source_target_pairs={{0,10},{2,12},{4,14},{6,0},{8,2},{10,4},{12,6},{14,8},{1,11},{3,13... | collective-permute-start | bytes 393224 | tf_op jit(solution)/shard_map/ppermute | solution.py:181
  50.1 4.5 %collective-permute-start.3 = (bf16[8,64,128]{2,1,0:T(8,128)(2,1)}, bf16[8,64,128]{2,1,0:T(8,128)(2,1)S(1)}, u32[]{:S(2)}, u32[]{:S(2)}) collective-permute-start(bf16[8,64,128]{2,1,0:T(8,128)(2,1)} %get-tuple-element.18), channel_id=1, source_target_pairs={{0,4},{2,6},{4,8},{6,10},{8,12},{10,14},{12,0},{14,2},{1,5},{3,7},... | collective-permute-start | bytes 393224 | tf_op jit(solution)/shard_map/ppermute | solution.py:181
  54.7 2.8 %collective-permute-start.4 = (bf16[8,64,128]{2,1,0:T(8,128)(2,1)}, bf16[8,64,128]{2,1,0:T(8,128)(2,1)S(1)}, u32[]{:S(2)}, u32[]{:S(2)}) collective-permute-start(bf16[8,64,128]{2,1,0:T(8,128)(2,1)} %get-tuple-element.19), channel_id=1, source_target_pairs={{0,12},{2,14},{4,0},{6,2},{8,4},{10,6},{12,8},{14,10},{1,13},{3,15... | collective-permute-start | bytes 393224 | tf_op jit(solution)/shard_map/ppermute | solution.py:181
  57.5 0.2 dynamic-slice_bitcast_fusion
  57.7 0.2 copy.13
  57.9 2.7 %collective-permute-start.5 = (bf16[8,64,128]{2,1,0:T(8,128)(2,1)}, bf16[8,64,128]{2,1,0:T(8,128)(2,1)S(1)}, u32[]{:S(2)}, u32[]{:S(2)}) collective-permute-start(bf16[8,64,128]{2,1,0:T(8,128)(2,1)} %copy-done.10), channel_id=1, source_target_pairs={{0,2},{2,4},{4,6},{6,8},{8,10},{10,12},{12,14},{14,0},{1,3},{3,5},... | collective-permute-start | bytes 393224 | tf_op jit(solution)/shard_map/ppermute | solution.py:181
  60.7 0.0 copy-start.13
  60.7 3.8 %collective-permute-start.6 = (bf16[8,64,128]{2,1,0:T(8,128)(2,1)}, bf16[8,64,128]{2,1,0:T(8,128)(2,1)S(1)}, u32[]{:S(2)}, u32[]{:S(2)}) collective-permute-start(bf16[8,64,128]{2,1,0:T(8,128)(2,1)} %copy-done.9), channel_id=1, source_target_pairs={{0,14},{2,0},{4,2},{6,4},{8,6},{10,8},{12,10},{14,12},{1,15},{3,1}... | collective-permute-start | bytes 393224 | tf_op jit(solution)/shard_map/ppermute | solution.py:181
  64.5 0.2 constant_dynamic-slice_fusion.1
  64.6 0.1 copy.19
  64.8 0.1 copy.20
  65.0 0.5 collective-permute-done.4.refs_5_
  65.5 3.5 %collective-permute-done.6.refs_7_ = bf16[8,64,128]{2,1,0:T(8,128)(2,1)S(1)} collective-permute-done((bf16[8,64,128]{2,1,0:T(8,128)(2,1)}, bf16[8,64,128]{2,1,0:T(8,128)(2,1)S(1)}, u32[]{:S(2)}, u32[]{:S(2)}) %collective-permute-start.6) | collective-permute-done | bytes 131104 | tf_op jit(solution)/shard_map/ppermute | solution.py:181
  69.0 0.6 copy-done.18
  69.6 2.1 %sum_parts.1 = bf16[8,64,128]{2,1,0:T(8,128)(2,1)} custom-call(bf16[8,64,128]{2,1,0:T(8,128)(2,1)} %copy-done.4, bf16[8,64,128]{2,1,0:T(8,128)(2,1)} %copy-done.12, bf16[8,64,128]{2,1,0:T(8,128)(2,1)} %copy-done.13, bf16[8,64,128]{2,1,0:T(8,128)(2,1)} %copy-done.14, bf16[8,64,128]{2,1,0:T(8,128)(2,1)} %copy-done.15, bf16[8,64,128]{2,1,0:T(8,128)(2,1)} %copy-done.16, ...), custom_call_target="tpu_custom_call" | custom-call | flops 524288 | bytes 1179648 | tf_op jit(solution)/shard_map/sum_parts/pallas_call | solution.py:149
  71.7 7.7 %ladder_partials.1 = (f32[64,64,128]{2,1,0:T(8,128)S(1)}, bf16[64,64,128]{2,1,0:T(8,128)(2,1)S(1)}) custom-call(bf16[64,2,64,128]{3,2,1,0:T(8,128)(2,1)} %all-to-all-done.amps_ref, bf16[128,768]{1,0:T(8,128)(2,1)S(1)} %pad_maximum_fusion.left_ref, bf16[2,768,128]{2,1,0:T(8,128)(2,1)S(1)} %bitcast.24), custom_call_target="tpu_custom_call" | custom-call | flops 4294967296 | bytes 6291456 | tf_op jit(solution)/shard_map/ladder_partials/pallas_call | solution.py:117
  79.4 3.5 %collective-permute-start.7 = (bf16[64,64,128]{2,1,0:T(8,128)(2,1)S(1)}, bf16[64,64,128]{2,1,0:T(8,128)(2,1)S(1)}, u32[]{:S(2)}, u32[]{:S(2)}) collective-permute-start(bf16[64,64,128]{2,1,0:T(8,128)(2,1)S(1)} %get-tuple-element.25), channel_id=1, source_target_pairs={{0,1},{1,0},{2,3},{3,2},{4,5},{5,4},{6,7},{7,6},{8,9},{9,8},{10,11... | collective-permute-start | bytes 3145736 | tf_op jit(solution)/shard_map/ppermute | solution.py:195
  82.9 2.3 %collective-permute-done.7 = bf16[64,64,128]{2,1,0:T(8,128)(2,1)S(1)} collective-permute-done((bf16[64,64,128]{2,1,0:T(8,128)(2,1)S(1)}, bf16[64,64,128]{2,1,0:T(8,128)(2,1)S(1)}, u32[]{:S(2)}, u32[]{:S(2)}) %collective-permute-start.7) | collective-permute-done | bytes 1048608 | tf_op jit(solution)/shard_map/ppermute | solution.py:195
  85.1 1.3 %fusion = bf16[64,1,1,64,128]{4,3,2,1,0:T(8,128)(2,1)} fusion(f32[64,64,128]{2,1,0:T(8,128)S(1)} %get-tuple-element.24, bf16[64,64,128]{2,1,0:T(8,128)(2,1)S(1)} %collective-permute-done.7), kind=kLoop, calls=%fused_computation.1 | loop fusion | flops 1572864 | bytes 4194304
  (36 shorter events, 0.1 us)
Async XLA Ops:
  0.6 56.9 %copy-start = (bf16[6,1,2,128,128]{4,3,2,1,0:T(8,128)(2,1)S(1)}, bf16[6,1,2,128,128]{4,3,2,1,0:T(8,128)(2,1)}, u32[]{:S(2)}) copy-start(bf16[6,1,2,128,128]{4,3,2,1,0:T(8,128)(2,1)} %param.14) | copy-start | bytes 1179652
  0.6 1.3 %copy-start.1 = (bf16[1,1,64,64,128]{4,3,2,1,0:T(8,128)(2,1)S(1)}, bf16[1,1,64,64,128]{4,3,2,1,0:T(8,128)(2,1)}, u32[]{:S(2)}) copy-start(bf16[1,1,64,64,128]{4,3,2,1,0:T(8,128)(2,1)} %param.8) | copy-start | bytes 3145732
  1.9 0.7 copy-start.5
  2.6 0.7 copy-start.8
  5.4 14.6 %copy-start.2 = (bf16[1,1,64,64,128]{4,3,2,1,0:T(8,128)(2,1)S(1)}, bf16[1,1,64,64,128]{4,3,2,1,0:T(8,128)(2,1)}, u32[]{:S(2)}) copy-start(bf16[1,1,64,64,128]{4,3,2,1,0:T(8,128)(2,1)} %param.8) | copy-start | bytes 3145732
  5.4 14.6 %copy-start.3 = (bf16[1,1,64,128,128]{4,3,2,1,0:T(8,128)(2,1)S(1)}, bf16[1,1,64,128,128]{4,3,2,1,0:T(8,128)(2,1)}, u32[]{:S(2)}) copy-start(bf16[1,1,64,128,128]{4,3,2,1,0:T(8,128)(2,1)} %param.9) | copy-start | bytes 6291460
  5.4 14.6 %copy-start.6 = (s32[64,2]{0,1:T(2,128)S(1)}, s32[64,2]{0,1:T(2,128)}, u32[]{:S(2)}) copy-start(s32[64,2]{0,1:T(2,128)} %param.10) | copy-start | bytes 1540
  5.4 14.6 %copy-start.7 = (s32[64,2]{0,1:T(2,128)S(1)}, s32[64,2]{0,1:T(2,128)}, u32[]{:S(2)}) copy-start(s32[64,2]{0,1:T(2,128)} %param.11) | copy-start | bytes 1540
  5.4 66.3 %all-to-all-start = ((bf16[64,2,64,128]{3,2,1,0:T(8,128)(2,1)}), bf16[64,2,64,128]{3,2,1,0:T(8,128)(2,1)}, u32[]{:S(2)}, u32[]{:S(2)}) async-start(bf16[64,2,64,128]{3,2,1,0:T(8,128)(2,1)} %outgoing_tiles.1), calls=%async_computation | async-start | bytes 4194304 | tf_op jit(solution)/shard_map/all_to_all | solution.py:173
  24.2 0.7 copy-start.4
  24.8 0.7 copy-start.9
  25.5 0.7 copy-start.10
  26.1 38.8 %copy-start.11 = (bf16[6,1,2,128,128]{4,3,2,1,0:T(8,128)(2,1)S(1)}, bf16[6,1,2,128,128]{4,3,2,1,0:T(8,128)(2,1)}, u32[]{:S(2)}) copy-start(bf16[6,1,2,128,128]{4,3,2,1,0:T(8,128)(2,1)} %param.15) | copy-start | bytes 1179652
  26.1 31.8 %collective-permute-start = (bf16[8,64,128]{2,1,0:T(8,128)(2,1)}, bf16[8,64,128]{2,1,0:T(8,128)(2,1)S(1)}, u32[]{:S(2)}, u32[]{:S(2)}) collective-permute-start(bf16[8,64,128]{2,1,0:T(8,128)(2,1)} %get-tuple-element.15), channel_id=1, source_target_pairs={{0,8},{2,10},{4,12},{6,14},{8,0},{10,2},{12,4},{14,6},{1,9},{3,11}... | collective-permute-start | bytes 393224 | tf_op jit(solution)/shard_map/ppermute | solution.py:181
  40.5 20.1 %collective-permute-start.1 = (bf16[8,64,128]{2,1,0:T(8,128)(2,1)}, bf16[8,64,128]{2,1,0:T(8,128)(2,1)S(1)}, u32[]{:S(2)}, u32[]{:S(2)}) collective-permute-start(bf16[8,64,128]{2,1,0:T(8,128)(2,1)} %get-tuple-element.16), channel_id=1, source_target_pairs={{0,6},{2,8},{4,10},{6,12},{8,14},{10,0},{12,2},{14,4},{1,7},{3,9},... | collective-permute-start | bytes 393224 | tf_op jit(solution)/shard_map/ppermute | solution.py:181
  48.2 16.8 %collective-permute-start.2 = (bf16[8,64,128]{2,1,0:T(8,128)(2,1)}, bf16[8,64,128]{2,1,0:T(8,128)(2,1)S(1)}, u32[]{:S(2)}, u32[]{:S(2)}) collective-permute-start(bf16[8,64,128]{2,1,0:T(8,128)(2,1)} %get-tuple-element.17), channel_id=1, source_target_pairs={{0,10},{2,12},{4,14},{6,0},{8,2},{10,4},{12,6},{14,8},{1,11},{3,13... | collective-permute-start | bytes 393224 | tf_op jit(solution)/shard_map/ppermute | solution.py:181
  50.1 14.9 %collective-permute-start.3 = (bf16[8,64,128]{2,1,0:T(8,128)(2,1)}, bf16[8,64,128]{2,1,0:T(8,128)(2,1)S(1)}, u32[]{:S(2)}, u32[]{:S(2)}) collective-permute-start(bf16[8,64,128]{2,1,0:T(8,128)(2,1)} %get-tuple-element.18), channel_id=1, source_target_pairs={{0,4},{2,6},{4,8},{6,10},{8,12},{10,14},{12,0},{14,2},{1,5},{3,7},... | collective-permute-start | bytes 393224 | tf_op jit(solution)/shard_map/ppermute | solution.py:181
  54.7 10.8 %collective-permute-start.4 = (bf16[8,64,128]{2,1,0:T(8,128)(2,1)}, bf16[8,64,128]{2,1,0:T(8,128)(2,1)S(1)}, u32[]{:S(2)}, u32[]{:S(2)}) collective-permute-start(bf16[8,64,128]{2,1,0:T(8,128)(2,1)} %get-tuple-element.19), channel_id=1, source_target_pairs={{0,12},{2,14},{4,0},{6,2},{8,4},{10,6},{12,8},{14,10},{1,13},{3,15... | collective-permute-start | bytes 393224 | tf_op jit(solution)/shard_map/ppermute | solution.py:181
  57.9 11.1 %copy-start.12 = (bf16[8,64,128]{2,1,0:T(8,128)(2,1)}, bf16[8,64,128]{2,1,0:T(8,128)(2,1)S(1)}, u32[]{:S(2)}) copy-start(bf16[8,64,128]{2,1,0:T(8,128)(2,1)S(1)} %collective-permute-done.refs_1_) | copy-start | bytes 393220
  57.9 7.6 %collective-permute-start.5 = (bf16[8,64,128]{2,1,0:T(8,128)(2,1)}, bf16[8,64,128]{2,1,0:T(8,128)(2,1)S(1)}, u32[]{:S(2)}, u32[]{:S(2)}) collective-permute-start(bf16[8,64,128]{2,1,0:T(8,128)(2,1)} %copy-done.10), channel_id=1, source_target_pairs={{0,2},{2,4},{4,6},{6,8},{8,10},{10,12},{12,14},{14,0},{1,3},{3,5},... | collective-permute-start | bytes 393224 | tf_op jit(solution)/shard_map/ppermute | solution.py:181
  60.7 8.3 %copy-start.13 = (bf16[8,64,128]{2,1,0:T(8,128)(2,1)}, bf16[8,64,128]{2,1,0:T(8,128)(2,1)S(1)}, u32[]{:S(2)}) copy-start(bf16[8,64,128]{2,1,0:T(8,128)(2,1)S(1)} %collective-permute-done.1.refs_2_) | copy-start | bytes 393220
  60.7 8.3 %collective-permute-start.6 = (bf16[8,64,128]{2,1,0:T(8,128)(2,1)}, bf16[8,64,128]{2,1,0:T(8,128)(2,1)S(1)}, u32[]{:S(2)}, u32[]{:S(2)}) collective-permute-start(bf16[8,64,128]{2,1,0:T(8,128)(2,1)} %copy-done.9), channel_id=1, source_target_pairs={{0,14},{2,0},{4,2},{6,4},{8,6},{10,8},{12,10},{14,12},{1,15},{3,1}... | collective-permute-start | bytes 393224 | tf_op jit(solution)/shard_map/ppermute | solution.py:181
  65.0 4.0 %copy-start.14 = (bf16[8,64,128]{2,1,0:T(8,128)(2,1)}, bf16[8,64,128]{2,1,0:T(8,128)(2,1)S(1)}, u32[]{:S(2)}) copy-start(bf16[8,64,128]{2,1,0:T(8,128)(2,1)S(1)} %collective-permute-done.2.refs_3_) | copy-start | bytes 393220
  65.0 4.0 %copy-start.15 = (bf16[8,64,128]{2,1,0:T(8,128)(2,1)}, bf16[8,64,128]{2,1,0:T(8,128)(2,1)S(1)}, u32[]{:S(2)}) copy-start(bf16[8,64,128]{2,1,0:T(8,128)(2,1)S(1)} %collective-permute-done.3.refs_4_) | copy-start | bytes 393220
  65.5 3.5 %copy-start.16 = (bf16[8,64,128]{2,1,0:T(8,128)(2,1)}, bf16[8,64,128]{2,1,0:T(8,128)(2,1)S(1)}, u32[]{:S(2)}) copy-start(bf16[8,64,128]{2,1,0:T(8,128)(2,1)S(1)} %collective-permute-done.4.refs_5_) | copy-start | bytes 393220
  65.5 3.5 %copy-start.17 = (bf16[8,64,128]{2,1,0:T(8,128)(2,1)}, bf16[8,64,128]{2,1,0:T(8,128)(2,1)S(1)}, u32[]{:S(2)}) copy-start(bf16[8,64,128]{2,1,0:T(8,128)(2,1)S(1)} %collective-permute-done.5.refs_6_) | copy-start | bytes 393220
  69.0 0.7 copy-start.18
  79.4 5.8 %collective-permute-start.7 = (bf16[64,64,128]{2,1,0:T(8,128)(2,1)S(1)}, bf16[64,64,128]{2,1,0:T(8,128)(2,1)S(1)}, u32[]{:S(2)}, u32[]{:S(2)}) collective-permute-start(bf16[64,64,128]{2,1,0:T(8,128)(2,1)S(1)} %get-tuple-element.25), channel_id=1, source_target_pairs={{0,1},{1,0},{2,3},{3,2},{4,5},{5,4},{6,7},{7,6},{8,9},{9,8},{10,11... | collective-permute-start | bytes 3145736 | tf_op jit(solution)/shard_map/ppermute | solution.py:195

commit v2 on v1

--- a/solution.py
+++ b/solution.py
@@ -6,10 +6,22 @@
 from jax.sharding import PartitionSpec as P
 
 GROUP = 16
-
-
-def gather_kernel(order_ref, src_ref, tiles_ref, out_ref):
+TOGETHER = 8
+SENDS = (4, 3, 5, 2, 6, 1, 7)
+SPLITS = 4
+
+
+def gather_kernel(order_hbm, src_hbm, tiles_hbm, out_hbm, order_ref, src_ref, tiles_ref, out_ref, sems):
     count, terms = out_ref.shape[0], out_ref.shape[1]
+    loads = [
+        pltpu.make_async_copy(order_hbm, order_ref, sems.at[0]),
+        pltpu.make_async_copy(src_hbm, src_ref, sems.at[1]),
+        pltpu.make_async_copy(tiles_hbm, tiles_ref, sems.at[2]),
+    ]
+    for load in loads:
+        load.start()
+    for load in loads:
+        load.wait()
 
     def one(m, carry):
         slot = order_ref[m]
@@ -17,7 +29,15 @@
             out_ref[m, p] = tiles_ref[src_ref[p, slot]]
         return carry
 
-    lax.fori_loop(0, count, one, 0, unroll=8)
+    share = count // SPLITS
+    stores = []
+    for part in range(SPLITS):
+        lax.fori_loop(part * share, (part + 1) * share, one, 0, unroll=8)
+        block = pl.ds(part * share, share)
+        stores.append(pltpu.make_async_copy(out_ref.at[block], out_hbm.at[block], sems.at[3 + part]))
+        stores[-1].start()
+    for store in stores:
+        store.wait()
 
 
 def whole(shape):
@@ -29,23 +49,28 @@
     out_shape = (count, terms) + tiles.shape[1:]
     return pl.pallas_call(
         gather_kernel,
-        grid_spec=pltpu.PrefetchScalarGridSpec(
-            num_scalar_prefetch=2,
-            grid=(1,),
-            in_specs=[whole(tiles.shape)],
-            out_specs=whole(out_shape),
-        ),
+        in_specs=[pl.BlockSpec(memory_space=pltpu.HBM)] * 3,
+        out_specs=pl.BlockSpec(memory_space=pltpu.HBM),
         out_shape=jax.ShapeDtypeStruct(out_shape, tiles.dtype),
+        scratch_shapes=[
+            pltpu.SMEM(order.shape, order.dtype),
+            pltpu.SMEM(src.shape, src.dtype),
+            pltpu.VMEM(tiles.shape, tiles.dtype),
+            pltpu.VMEM(out_shape, tiles.dtype),
+            pltpu.SemaphoreType.DMA((3 + SPLITS,)),
+        ],
         compiler_params=pltpu.CompilerParams(vmem_limit_bytes=8 << 20),
         cost_estimate=pl.CostEstimate(flops=0, bytes_accessed=4 << 20, transcendentals=0),
         name="outgoing_tiles",
     )(order, src, tiles)
 
 
-def cycle_kernel(me_ref, src_ref, wsel_ref, amps_ref, ints_ref, *out_refs):
-    terms, holders, share = src_ref.shape[0], len(out_refs), out_refs[0].shape[0]
+def cycle_kernel(me_ref, src_ref, wsel_ref, amps_ref, ints_ref, *refs):
+    *out_hbm, out_ref, sems = refs
+    terms, holders, share = src_ref.shape[0], out_ref.shape[0], out_ref.shape[1]
     me = me_ref[0]
-    for step, out_ref in enumerate(out_refs):
+    stores = []
+    for step in SENDS + (0,):
         base = lax.rem(me + step, holders) * share
 
         def one(t, carry):
@@ -53,10 +78,14 @@
             left = jnp.concatenate([amps_ref[src_ref[p, s]] for p in range(terms)], axis=1)
             right = jnp.concatenate([ints_ref[wsel_ref[p, s]] for p in range(terms)], axis=0)
             total = jnp.dot(left, right, preferred_element_type=jnp.float32)
-            out_ref[t] = total.astype(out_ref.dtype)
+            out_ref[step, t] = total.astype(out_ref.dtype)
             return carry
 
         lax.fori_loop(0, share, one, 0, unroll=4)
+        stores.append(pltpu.make_async_copy(out_ref.at[step], out_hbm[step], sems.at[step]))
+        stores[-1].start()
+    for store in stores:
+        store.wait()
 
 
 def cycle_partials(me, holders, src, wsel, amps, ints):
@@ -68,7 +97,11 @@
             num_scalar_prefetch=3,
             grid=(1,),
             in_specs=[whole(amps.shape), whole(ints.shape)],
-            out_specs=[whole(out_shape)] * holders,
+            out_specs=[pl.BlockSpec(memory_space=pltpu.HBM)] * holders,
+            scratch_shapes=[
+                pltpu.VMEM((holders,) + out_shape, jnp.bfloat16),
+                pltpu.SemaphoreType.DMA((holders,)),
+            ],
         ),
         out_shape=[jax.ShapeDtypeStruct(out_shape, jnp.bfloat16)] * holders,
         compiler_params=pltpu.CompilerParams(vmem_limit_bytes=12 << 20),
@@ -82,7 +115,7 @@
     vectors = right_ref.shape[1] // width
     half = own_ref.shape[1]
     left = left_ref[...]
-    sub = 4
+    sub = min(TOGETHER, group)
     for start in range(0, group, sub):
         halves = []
         for p in range(terms):
@@ -176,12 +209,11 @@
     me = lax.axis_index("occ").astype(jnp.int32).reshape(1)
     partials = cycle_partials(me, holders, cycle_src.T, cycle_wsel.T, held_tiles, cycle_ints[0, 0])
     parts = [partials[0]]
-    for step in sorted(range(1, holders), key=lambda step: (abs(step - holders // 2), step)):
+    for step in SENDS:
         ring = [(k, (k + step) % holders) for k in range(holders)]
         parts.append(lax.ppermute(partials[step], "occ", ring))
-    cycle_part = sum_parts(parts)
-    arriving, cycle_part = lax.optimization_barrier((arriving, cycle_part))
-    cycle_part = cycle_part[None, None]
+    arriving, *parts = lax.optimization_barrier((arriving, *parts))
+    cycle_part = sum_parts(parts)[None, None]
 
     replica = lax.axis_index("rep")
     left = lax.dynamic_slice_in_dim(first_integral_blocks[:, 0], replica * row_count, row_count, 3)

time: 87 us -> 86.8 us (level)
  starting transfers between devices: 55.9 us -> 57.9 us
  waiting for transfers between devices: 6.23 us -> 4.37 us
    ppermute x1, starting transfers between devices: 3.49 us -> 5.46 us  [shards(): received = lax.ppermute(other, 'rep', [(0, 1), (1, 0)])]
    ppermute x1, waiting for transfers between devices: 2.26 us -> 0.4 us  [shards(): received = lax.ppermute(other, 'rep', [(0, 1), (1, 0)])]
where the time goes in v2:
time: 86.8 us; the launch traced here: 86.3 us
  starting transfers between devices  57.9 us (67%)
  Pallas kernels  15.7 us (18%)
  local copies, waits for them, and re-layouts  6.05 us (7%)
  waiting for transfers between devices  4.37 us (5%)
  other arithmetic  1.31 us (2%)
  between operations  0.99 us (1%)
    ppermute x7, starting transfers between devices, shards(): parts.append(lax.ppermute(partials[step], 'occ', ring))  37.8 us
    all_to_all x1, starting transfers between devices, shards(): lax.all_to_all(outgoing, 'vir', split_axis=0, concat_axis=0, tiled=True)  14.6 us
    pallas_call x1, Pallas kernels, ladder_partials(): pl.pallas_call(ladder_kernel, grid=(items // GROUP,), in_specs=[pl.BlockS...  7.44 us
    unnamed x40, local copies, waits for them, and re-layouts  5.49 us
    ppermute x1, starting transfers between devices, shards(): received = lax.ppermute(other, 'rep', [(0, 1), (1, 0)])  5.46 us
    pallas_call x1, Pallas kernels, cycle_partials(): pl.pallas_call(cycle_kernel, grid_spec=pltpu.PrefetchScalarGridSpec(num_s...  4.16 us
    ppermute x7, waiting for transfers between devices, shards(): parts.append(lax.ppermute(partials[step], 'occ', ring))  3.97 us
    pallas_call x1, Pallas kernels, sum_parts(): pl.pallas_call(sum_kernel, in_specs=[pl.BlockSpec(memory_space=pltpu.VMEM...  2.08 us
  transfers between devices with their start and end apart: 9, of which 3 were waited for; matrix products, arithmetic and copies ran while one was open for 1% of the time, Pallas kernels for 7%

profile of v2, /device:TPU:1, one launch (start us, length us, event | category | flops | bytes accessed | tf_op | source)
XLA Modules:
  0.0 86.3 jit_solution(1044508367609891898)
XLA Ops:
  0.6 0.0 copy-start
  0.7 1.3 %copy-done.1 = bf16[1,1,64,64,128]{4,3,2,1,0:T(8,128)(2,1)S(1)} copy-done((bf16[1,1,64,64,128]{4,3,2,1,0:T(8,128)(2,1)S(1)}, bf16[1,1,64,64,128]{4,3,2,1,0:T(8,128)(2,1)}, u32[]{:S(2)}) %copy-start.1) | copy-done | bytes 1048600
  1.9 0.7 copy-done.5
  2.6 0.7 copy-done.8
  3.3 2.0 %outgoing_tiles.1 = bf16[64,2,64,128]{3,2,1,0:T(8,128)(2,1)} custom-call(s32[64]{0:T(128)S(1)} %copy-done.8, s32[2,64]{1,0:T(2,128)S(1)} %bitcast.25, bf16[64,64,128]{2,1,0:T(8,128)(2,1)S(1)} %bitcast.21), custom_call_target="tpu_custom_call" | custom-call | bytes 4194304 | tf_op jit(solution)/shard_map/outgoing_tiles/pallas_call | solution.py:50
  5.3 0.0 copy-start.6
  5.3 0.0 copy-start.7
  5.3 14.6 %all-to-all-start = ((bf16[64,2,64,128]{3,2,1,0:T(8,128)(2,1)}), bf16[64,2,64,128]{3,2,1,0:T(8,128)(2,1)}, u32[]{:S(2)}, u32[]{:S(2)}) async-start(bf16[64,2,64,128]{3,2,1,0:T(8,128)(2,1)} %outgoing_tiles.1), calls=%async_computation | async-start | bytes 4194304 | tf_op jit(solution)/shard_map/all_to_all | solution.py:206
  19.9 4.2 %cycle_partials.1 = (bf16[8,64,128]{2,1,0:T(8,128)(2,1)S(1)}, bf16[8,64,128]{2,1,0:T(8,128)(2,1)S(1)}, bf16[8,64,128]{2,1,0:T(8,128)(2,1)}, bf16[8,64,128]{2,1,0...) custom-call(s32[1]{0:T(128)} %bitcast.2.me_ref, ...), custom_call_target="tpu_custom_call" | custom-call | flops 268435456 | bytes 4194304 | tf_op jit(solution)/shard_map/cycle_partials/pallas_call | solution.py:94
  24.1 0.6 copy-done.4
  24.8 0.7 copy-done.9
  25.4 0.6 copy-done.10
  26.1 14.4 %collective-permute-start = (bf16[8,64,128]{2,1,0:T(8,128)(2,1)}, bf16[8,64,128]{2,1,0:T(8,128)(2,1)S(1)}, u32[]{:S(2)}, u32[]{:S(2)}) collective-permute-start(bf16[8,64,128]{2,1,0:T(8,128)(2,1)} %get-tuple-element.22), channel_id=1, source_target_pairs={{0,8},{2,10},{4,12},{6,14},{8,0},{10,2},{12,4},{14,6},{1,9},{3,11}... | collective-permute-start | bytes 393224 | tf_op jit(solution)/shard_map/ppermute | solution.py:214
  40.5 7.6 %collective-permute-start.1 = (bf16[8,64,128]{2,1,0:T(8,128)(2,1)}, bf16[8,64,128]{2,1,0:T(8,128)(2,1)S(1)}, u32[]{:S(2)}, u32[]{:S(2)}) collective-permute-start(bf16[8,64,128]{2,1,0:T(8,128)(2,1)} %get-tuple-element.23), channel_id=1, source_target_pairs={{0,6},{2,8},{4,10},{6,12},{8,14},{10,0},{12,2},{14,4},{1,7},{3,9},... | collective-permute-start | bytes 393224 | tf_op jit(solution)/shard_map/ppermute | solution.py:214
  48.1 1.9 %collective-permute-start.2 = (bf16[8,64,128]{2,1,0:T(8,128)(2,1)}, bf16[8,64,128]{2,1,0:T(8,128)(2,1)S(1)}, u32[]{:S(2)}, u32[]{:S(2)}) collective-permute-start(bf16[8,64,128]{2,1,0:T(8,128)(2,1)} %get-tuple-element.24), channel_id=1, source_target_pairs={{0,10},{2,12},{4,14},{6,0},{8,2},{10,4},{12,6},{14,8},{1,11},{3,13... | collective-permute-start | bytes 393224 | tf_op jit(solution)/shard_map/ppermute | solution.py:214
  50.1 4.6 %collective-permute-start.3 = (bf16[8,64,128]{2,1,0:T(8,128)(2,1)}, bf16[8,64,128]{2,1,0:T(8,128)(2,1)S(1)}, u32[]{:S(2)}, u32[]{:S(2)}) collective-permute-start(bf16[8,64,128]{2,1,0:T(8,128)(2,1)} %get-tuple-element.25), channel_id=1, source_target_pairs={{0,4},{2,6},{4,8},{6,10},{8,12},{10,14},{12,0},{14,2},{1,5},{3,7},... | collective-permute-start | bytes 393224 | tf_op jit(solution)/shard_map/ppermute | solution.py:214
  54.6 2.8 %collective-permute-start.4 = (bf16[8,64,128]{2,1,0:T(8,128)(2,1)}, bf16[8,64,128]{2,1,0:T(8,128)(2,1)S(1)}, u32[]{:S(2)}, u32[]{:S(2)}) collective-permute-start(bf16[8,64,128]{2,1,0:T(8,128)(2,1)} %get-tuple-element.26), channel_id=1, source_target_pairs={{0,12},{2,14},{4,0},{6,2},{8,4},{10,6},{12,8},{14,10},{1,13},{3,15... | collective-permute-start | bytes 393224 | tf_op jit(solution)/shard_map/ppermute | solution.py:214
  57.5 0.2 dynamic-slice_bitcast_fusion
  57.7 0.2 copy.13
  57.9 2.7 %collective-permute-start.5 = (bf16[8,64,128]{2,1,0:T(8,128)(2,1)}, bf16[8,64,128]{2,1,0:T(8,128)(2,1)S(1)}, u32[]{:S(2)}, u32[]{:S(2)}) collective-permute-start(bf16[8,64,128]{2,1,0:T(8,128)(2,1)} %copy-done.10), channel_id=1, source_target_pairs={{0,2},{2,4},{4,6},{6,8},{8,10},{10,12},{12,14},{14,0},{1,3},{3,5},... | collective-permute-start | bytes 393224 | tf_op jit(solution)/shard_map/ppermute | solution.py:214
  60.6 3.8 %collective-permute-start.6 = (bf16[8,64,128]{2,1,0:T(8,128)(2,1)}, bf16[8,64,128]{2,1,0:T(8,128)(2,1)S(1)}, u32[]{:S(2)}, u32[]{:S(2)}) collective-permute-start(bf16[8,64,128]{2,1,0:T(8,128)(2,1)} %copy-done.9), channel_id=1, source_target_pairs={{0,14},{2,0},{4,2},{6,4},{8,6},{10,8},{12,10},{14,12},{1,15},{3,1}... | collective-permute-start | bytes 393224 | tf_op jit(solution)/shard_map/ppermute | solution.py:214
  64.4 0.2 constant_dynamic-slice_fusion.1
  64.6 0.1 copy.19
  64.7 0.1 copy.20
  65.0 0.5 collective-permute-done.4.refs_5_
  65.5 3.5 %collective-permute-done.6.refs_7_ = bf16[8,64,128]{2,1,0:T(8,128)(2,1)S(1)} collective-permute-done((bf16[8,64,128]{2,1,0:T(8,128)(2,1)}, bf16[8,64,128]{2,1,0:T(8,128)(2,1)S(1)}, u32[]{:S(2)}, u32[]{:S(2)}) %collective-permute-start.6) | collective-permute-done | bytes 131104 | tf_op jit(solution)/shard_map/ppermute | solution.py:214
  69.0 0.6 copy-done.18
  69.6 7.4 %ladder_partials.1 = (f32[64,64,128]{2,1,0:T(8,128)S(1)}, bf16[64,64,128]{2,1,0:T(8,128)(2,1)}) custom-call(bf16[64,2,64,128]{3,2,1,0:T(8,128)(2,1)} %all-to-all-done.amps_ref, bf16[128,768]{1,0:T(8,128)(2,1)S(1)} %pad_maximum_fusion.left_ref, bf16[2,768,128]{2,1,0:T(8,128)(2,1)S(1)} %bitcast.24), custom_call_target="tpu_custom_call" | custom-call | flops 4294967296 | bytes 6291456 | tf_op jit(solution)/shard_map/ladder_partials/pallas_call | solution.py:150
  77.0 5.5 %collective-permute-start.7 = (bf16[64,64,128]{2,1,0:T(8,128)(2,1)}, bf16[64,64,128]{2,1,0:T(8,128)(2,1)S(1)}, u32[]{:S(2)}, u32[]{:S(2)}) collective-permute-start(bf16[64,64,128]{2,1,0:T(8,128)(2,1)} %get-tuple-element.39), channel_id=1, source_target_pairs={{0,1},{1,0},{2,3},{3,2},{4,5},{5,4},{6,7},{7,6},{8,9},{9,8},{10,11... | collective-permute-start | bytes 3145736 | tf_op jit(solution)/shard_map/ppermute | solution.py:227
  82.5 2.1 %sum_parts.1 = bf16[8,64,128]{2,1,0:T(8,128)(2,1)} custom-call(bf16[8,64,128]{2,1,0:T(8,128)(2,1)} %copy-done.4, bf16[8,64,128]{2,1,0:T(8,128)(2,1)} %copy-done.12, bf16[8,64,128]{2,1,0:T(8,128)(2,1)} %copy-done.13, bf16[8,64,128]{2,1,0:T(8,128)(2,1)} %copy-done.14, bf16[8,64,128]{2,1,0:T(8,128)(2,1)} %copy-done.15, bf16[8,64,128]{2,1,0:T(8,128)(2,1)} %copy-done.16, ...), custom_call_target="tpu_custom_call" | custom-call | flops 524288 | bytes 1179648 | tf_op jit(solution)/shard_map/sum_parts/pallas_call | solution.py:182
  84.6 0.4 collective-permute-done.7
  85.0 1.3 %fusion = bf16[64,1,1,64,128]{4,3,2,1,0:T(8,128)(2,1)} fusion(f32[64,64,128]{2,1,0:T(8,128)S(1)} %get-tuple-element.38, bf16[64,64,128]{2,1,0:T(8,128)(2,1)S(1)} %collective-permute-done.7), kind=kLoop, calls=%fused_computation.1 | loop fusion | flops 1572864 | bytes 4194304
  (36 shorter events, 0.1 us)
Async XLA Ops:
  0.6 56.8 %copy-start = (bf16[6,1,2,128,128]{4,3,2,1,0:T(8,128)(2,1)S(1)}, bf16[6,1,2,128,128]{4,3,2,1,0:T(8,128)(2,1)}, u32[]{:S(2)}) copy-start(bf16[6,1,2,128,128]{4,3,2,1,0:T(8,128)(2,1)} %param.14) | copy-start | bytes 1179652
  0.6 1.3 %copy-start.1 = (bf16[1,1,64,64,128]{4,3,2,1,0:T(8,128)(2,1)S(1)}, bf16[1,1,64,64,128]{4,3,2,1,0:T(8,128)(2,1)}, u32[]{:S(2)}) copy-start(bf16[1,1,64,64,128]{4,3,2,1,0:T(8,128)(2,1)} %param.8) | copy-start | bytes 3145732
  1.9 0.7 copy-start.5
  2.6 0.7 copy-start.8
  5.3 14.6 %copy-start.2 = (bf16[1,1,64,64,128]{4,3,2,1,0:T(8,128)(2,1)S(1)}, bf16[1,1,64,64,128]{4,3,2,1,0:T(8,128)(2,1)}, u32[]{:S(2)}) copy-start(bf16[1,1,64,64,128]{4,3,2,1,0:T(8,128)(2,1)} %param.8) | copy-start | bytes 3145732
  5.3 14.6 %copy-start.3 = (bf16[1,1,64,128,128]{4,3,2,1,0:T(8,128)(2,1)S(1)}, bf16[1,1,64,128,128]{4,3,2,1,0:T(8,128)(2,1)}, u32[]{:S(2)}) copy-start(bf16[1,1,64,128,128]{4,3,2,1,0:T(8,128)(2,1)} %param.9) | copy-start | bytes 6291460
  5.3 14.6 %copy-start.6 = (s32[64,2]{0,1:T(2,128)S(1)}, s32[64,2]{0,1:T(2,128)}, u32[]{:S(2)}) copy-start(s32[64,2]{0,1:T(2,128)} %param.10) | copy-start | bytes 1540
  5.3 14.6 %copy-start.7 = (s32[64,2]{0,1:T(2,128)S(1)}, s32[64,2]{0,1:T(2,128)}, u32[]{:S(2)}) copy-start(s32[64,2]{0,1:T(2,128)} %param.11) | copy-start | bytes 1540
  5.3 63.6 %all-to-all-start = ((bf16[64,2,64,128]{3,2,1,0:T(8,128)(2,1)}), bf16[64,2,64,128]{3,2,1,0:T(8,128)(2,1)}, u32[]{:S(2)}, u32[]{:S(2)}) async-start(bf16[64,2,64,128]{3,2,1,0:T(8,128)(2,1)} %outgoing_tiles.1), calls=%async_computation | async-start | bytes 4194304 | tf_op jit(solution)/shard_map/all_to_all | solution.py:206
  24.1 0.7 copy-start.4
  24.8 0.7 copy-start.9
  25.4 0.7 copy-start.10
  26.1 38.8 %copy-start.11 = (bf16[6,1,2,128,128]{4,3,2,1,0:T(8,128)(2,1)S(1)}, bf16[6,1,2,128,128]{4,3,2,1,0:T(8,128)(2,1)}, u32[]{:S(2)}) copy-start(bf16[6,1,2,128,128]{4,3,2,1,0:T(8,128)(2,1)} %param.15) | copy-start | bytes 1179652
  26.1 31.8 %collective-permute-start = (bf16[8,64,128]{2,1,0:T(8,128)(2,1)}, bf16[8,64,128]{2,1,0:T(8,128)(2,1)S(1)}, u32[]{:S(2)}, u32[]{:S(2)}) collective-permute-start(bf16[8,64,128]{2,1,0:T(8,128)(2,1)} %get-tuple-element.22), channel_id=1, source_target_pairs={{0,8},{2,10},{4,12},{6,14},{8,0},{10,2},{12,4},{14,6},{1,9},{3,11}... | collective-permute-start | bytes 393224 | tf_op jit(solution)/shard_map/ppermute | solution.py:214
  40.5 20.1 %collective-permute-start.1 = (bf16[8,64,128]{2,1,0:T(8,128)(2,1)}, bf16[8,64,128]{2,1,0:T(8,128)(2,1)S(1)}, u32[]{:S(2)}, u32[]{:S(2)}) collective-permute-start(bf16[8,64,128]{2,1,0:T(8,128)(2,1)} %get-tuple-element.23), channel_id=1, source_target_pairs={{0,6},{2,8},{4,10},{6,12},{8,14},{10,0},{12,2},{14,4},{1,7},{3,9},... | collective-permute-start | bytes 393224 | tf_op jit(solution)/shard_map/ppermute | solution.py:214
  48.1 16.8 %collective-permute-start.2 = (bf16[8,64,128]{2,1,0:T(8,128)(2,1)}, bf16[8,64,128]{2,1,0:T(8,128)(2,1)S(1)}, u32[]{:S(2)}, u32[]{:S(2)}) collective-permute-start(bf16[8,64,128]{2,1,0:T(8,128)(2,1)} %get-tuple-element.24), channel_id=1, source_target_pairs={{0,10},{2,12},{4,14},{6,0},{8,2},{10,4},{12,6},{14,8},{1,11},{3,13... | collective-permute-start | bytes 393224 | tf_op jit(solution)/shard_map/ppermute | solution.py:214
  50.1 14.9 %collective-permute-start.3 = (bf16[8,64,128]{2,1,0:T(8,128)(2,1)}, bf16[8,64,128]{2,1,0:T(8,128)(2,1)S(1)}, u32[]{:S(2)}, u32[]{:S(2)}) collective-permute-start(bf16[8,64,128]{2,1,0:T(8,128)(2,1)} %get-tuple-element.25), channel_id=1, source_target_pairs={{0,4},{2,6},{4,8},{6,10},{8,12},{10,14},{12,0},{14,2},{1,5},{3,7},... | collective-permute-start | bytes 393224 | tf_op jit(solution)/shard_map/ppermute | solution.py:214
  54.6 10.8 %collective-permute-start.4 = (bf16[8,64,128]{2,1,0:T(8,128)(2,1)}, bf16[8,64,128]{2,1,0:T(8,128)(2,1)S(1)}, u32[]{:S(2)}, u32[]{:S(2)}) collective-permute-start(bf16[8,64,128]{2,1,0:T(8,128)(2,1)} %get-tuple-element.26), channel_id=1, source_target_pairs={{0,12},{2,14},{4,0},{6,2},{8,4},{10,6},{12,8},{14,10},{1,13},{3,15... | collective-permute-start | bytes 393224 | tf_op jit(solution)/shard_map/ppermute | solution.py:214
  57.9 11.1 %copy-start.12 = (bf16[8,64,128]{2,1,0:T(8,128)(2,1)}, bf16[8,64,128]{2,1,0:T(8,128)(2,1)S(1)}, u32[]{:S(2)}) copy-start(bf16[8,64,128]{2,1,0:T(8,128)(2,1)S(1)} %collective-permute-done.refs_1_) | copy-start | bytes 393220
  57.9 7.6 %collective-permute-start.5 = (bf16[8,64,128]{2,1,0:T(8,128)(2,1)}, bf16[8,64,128]{2,1,0:T(8,128)(2,1)S(1)}, u32[]{:S(2)}, u32[]{:S(2)}) collective-permute-start(bf16[8,64,128]{2,1,0:T(8,128)(2,1)} %copy-done.10), channel_id=1, source_target_pairs={{0,2},{2,4},{4,6},{6,8},{8,10},{10,12},{12,14},{14,0},{1,3},{3,5},... | collective-permute-start | bytes 393224 | tf_op jit(solution)/shard_map/ppermute | solution.py:214
  60.6 8.3 %copy-start.13 = (bf16[8,64,128]{2,1,0:T(8,128)(2,1)}, bf16[8,64,128]{2,1,0:T(8,128)(2,1)S(1)}, u32[]{:S(2)}) copy-start(bf16[8,64,128]{2,1,0:T(8,128)(2,1)S(1)} %collective-permute-done.1.refs_2_) | copy-start | bytes 393220
  60.6 8.3 %collective-permute-start.6 = (bf16[8,64,128]{2,1,0:T(8,128)(2,1)}, bf16[8,64,128]{2,1,0:T(8,128)(2,1)S(1)}, u32[]{:S(2)}, u32[]{:S(2)}) collective-permute-start(bf16[8,64,128]{2,1,0:T(8,128)(2,1)} %copy-done.9), channel_id=1, source_target_pairs={{0,14},{2,0},{4,2},{6,4},{8,6},{10,8},{12,10},{14,12},{1,15},{3,1}... | collective-permute-start | bytes 393224 | tf_op jit(solution)/shard_map/ppermute | solution.py:214
  64.9 4.0 %copy-start.14 = (bf16[8,64,128]{2,1,0:T(8,128)(2,1)}, bf16[8,64,128]{2,1,0:T(8,128)(2,1)S(1)}, u32[]{:S(2)}) copy-start(bf16[8,64,128]{2,1,0:T(8,128)(2,1)S(1)} %collective-permute-done.2.refs_3_) | copy-start | bytes 393220
  64.9 4.0 %copy-start.15 = (bf16[8,64,128]{2,1,0:T(8,128)(2,1)}, bf16[8,64,128]{2,1,0:T(8,128)(2,1)S(1)}, u32[]{:S(2)}) copy-start(bf16[8,64,128]{2,1,0:T(8,128)(2,1)S(1)} %collective-permute-done.3.refs_4_) | copy-start | bytes 393220
  65.5 3.5 %copy-start.16 = (bf16[8,64,128]{2,1,0:T(8,128)(2,1)}, bf16[8,64,128]{2,1,0:T(8,128)(2,1)S(1)}, u32[]{:S(2)}) copy-start(bf16[8,64,128]{2,1,0:T(8,128)(2,1)S(1)} %collective-permute-done.4.refs_5_) | copy-start | bytes 393220
  65.5 3.5 %copy-start.17 = (bf16[8,64,128]{2,1,0:T(8,128)(2,1)}, bf16[8,64,128]{2,1,0:T(8,128)(2,1)S(1)}, u32[]{:S(2)}) copy-start(bf16[8,64,128]{2,1,0:T(8,128)(2,1)S(1)} %collective-permute-done.5.refs_6_) | copy-start | bytes 393220
  68.9 0.7 copy-start.18
  77.0 7.9 %collective-permute-start.7 = (bf16[64,64,128]{2,1,0:T(8,128)(2,1)}, bf16[64,64,128]{2,1,0:T(8,128)(2,1)S(1)}, u32[]{:S(2)}, u32[]{:S(2)}) collective-permute-start(bf16[64,64,128]{2,1,0:T(8,128)(2,1)} %get-tuple-element.39), channel_id=1, source_target_pairs={{0,1},{1,0},{2,3},{3,2},{4,5},{5,4},{6,7},{7,6},{8,9},{9,8},{10,11... | collective-permute-start | bytes 3145736 | tf_op jit(solution)/shard_map/ppermute | solution.py:227

commit v3 on v2

--- a/solution.py
+++ b/solution.py
@@ -40,6 +40,10 @@
         store.wait()
 
 
+def in_hbm(array):
+    return pltpu.with_memory_space_constraint(array, pltpu.HBM)
+
+
 def whole(shape):
     return pl.BlockSpec(shape, lambda g, *_: (0,) * len(shape))
 
@@ -51,7 +55,7 @@
         gather_kernel,
         in_specs=[pl.BlockSpec(memory_space=pltpu.HBM)] * 3,
         out_specs=pl.BlockSpec(memory_space=pltpu.HBM),
-        out_shape=jax.ShapeDtypeStruct(out_shape, tiles.dtype),
+        out_shape=pltpu.HBM(out_shape, tiles.dtype),
         scratch_shapes=[
             pltpu.SMEM(order.shape, order.dtype),
             pltpu.SMEM(src.shape, src.dtype),
@@ -62,7 +66,7 @@
         compiler_params=pltpu.CompilerParams(vmem_limit_bytes=8 << 20),
         cost_estimate=pl.CostEstimate(flops=0, bytes_accessed=4 << 20, transcendentals=0),
         name="outgoing_tiles",
-    )(order, src, tiles)
+    )(in_hbm(order), in_hbm(src), in_hbm(tiles))
 
 
 def cycle_kernel(me_ref, src_ref, wsel_ref, amps_ref, ints_ref, *refs):
@@ -103,7 +107,7 @@
                 pltpu.SemaphoreType.DMA((holders,)),
             ],
         ),
-        out_shape=[jax.ShapeDtypeStruct(out_shape, jnp.bfloat16)] * holders,
+        out_shape=[pltpu.HBM(out_shape, jnp.bfloat16)] * holders,
         compiler_params=pltpu.CompilerParams(vmem_limit_bytes=12 << 20),
         cost_estimate=pl.CostEstimate(flops=2 * 64 * 64 * 256 * 128, bytes_accessed=4 << 20, transcendentals=0),
         name="cycle_partials",

time: 86.8 us -> 86.3 us (level)
  local copies, waits for them, and re-layouts: 6.05 us -> 1.5 us
  starting transfers between devices: 57.9 us -> 59.8 us
  other arithmetic: 1.31 us -> 2.54 us
    unnamed x40 -> x28, local copies, waits for them, and re-layouts: 5.49 us -> 0.94 us
    ppermute x1, starting transfers between devices: 5.46 us -> 7.37 us  [shards(): received = lax.ppermute(other, 'rep', [(0, 1), (1, 0)])]
    unnamed x1, other arithmetic: 1.3 us -> 2.53 us
where the time goes in v3:
time: 86.3 us; the launch traced here: 85.7 us
  starting transfers between devices  59.8 us (69%)
  Pallas kernels  16.4 us (19%)
  waiting for transfers between devices  4.5 us (5%)
  other arithmetic  2.54 us (3%)
  local copies, waits for them, and re-layouts  1.5 us (2%)
  between operations  0.96 us (1%)
    ppermute x7, starting transfers between devices, shards(): parts.append(lax.ppermute(partials[step], 'occ', ring))  37.9 us
    all_to_all x1, starting transfers between devices, shards(): lax.all_to_all(outgoing, 'vir', split_axis=0, concat_axis=0, tiled=True)  14.6 us
    pallas_call x1, Pallas kernels, ladder_partials(): pl.pallas_call(ladder_kernel, grid=(items // GROUP,), in_specs=[pl.BlockS...  7.44 us
    ppermute x1, starting transfers between devices, shards(): received = lax.ppermute(other, 'rep', [(0, 1), (1, 0)])  7.37 us
    pallas_call x1, Pallas kernels, cycle_partials(): pl.pallas_call(cycle_kernel, grid_spec=pltpu.PrefetchScalarGridSpec(num_s...  4.21 us
    ppermute x7, waiting for transfers between devices, shards(): parts.append(lax.ppermute(partials[step], 'occ', ring))  3.97 us
    pallas_call x1, Pallas kernels, gather_tiles(): pl.pallas_call(gather_kernel, in_specs=[pl.BlockSpec(memory_space=pltpu.H...  2.7 us
    unnamed x1, other arithmetic  2.53 us
  transfers between devices with their start and end apart: 9, of which 3 were waited for; matrix products, arithmetic and copies ran while one was open for 1% of the time, Pallas kernels for 7%

profile of v3, /device:TPU:1, one launch (start us, length us, event | category | flops | bytes accessed | tf_op | source)
XLA Modules:
  0.0 85.7 jit_solution(6692153547447847662)
XLA Ops:
  0.6 0.0 copy-start
  0.6 2.7 %outgoing_tiles.1 = bf16[64,2,64,128]{3,2,1,0:T(8,128)(2,1)} custom-call(s32[64]{0:T(128)} %order_hbm.1, s32[2,64]{1,0:T(2,128)} %bitcast.30, bf16[64,64,128]{2,1,0:T(8,128)(2,1)} %bitcast.21), custom_call_target="tpu_custom_call" | custom-call | bytes 4194304 | tf_op jit(solution)/shard_map/outgoing_tiles/pallas_call | solution.py:54
  3.3 0.0 copy-start.1
  3.4 0.0 copy-start.2
  3.4 0.0 copy-start.3
  3.4 0.0 copy-start.4
  3.4 14.6 %all-to-all-start = ((bf16[64,2,64,128]{3,2,1,0:T(8,128)(2,1)}), bf16[64,2,64,128]{3,2,1,0:T(8,128)(2,1)}, u32[]{:S(2)}, u32[]{:S(2)}) async-start(bf16[64,2,64,128]{3,2,1,0:T(8,128)(2,1)} %outgoing_tiles.1), calls=%async_computation | async-start | bytes 4194304 | tf_op jit(solution)/shard_map/all_to_all | solution.py:210
  18.0 4.2 %cycle_partials.1 = (bf16[8,64,128]{2,1,0:T(8,128)(2,1)}, bf16[8,64,128]{2,1,0:T(8,128)(2,1)}, bf16[8,64,128]{2,1,0:T(8,128)(2,1)}, bf16[8,64,128]{2,1,0:T(8,128...) custom-call(s32[1]{0:T(128)} %bitcast.2.me_ref, ...), custom_call_target="tpu_custom_call" | custom-call | flops 268435456 | bytes 4194304 | tf_op jit(solution)/shard_map/cycle_partials/pallas_call | solution.py:98
  22.2 0.0 copy-start.5
  22.2 14.4 %collective-permute-start = (bf16[8,64,128]{2,1,0:T(8,128)(2,1)}, bf16[8,64,128]{2,1,0:T(8,128)(2,1)S(1)}, u32[]{:S(2)}, u32[]{:S(2)}) collective-permute-start(bf16[8,64,128]{2,1,0:T(8,128)(2,1)} %get-tuple-element.22), channel_id=1, source_target_pairs={{0,8},{2,10},{4,12},{6,14},{8,0},{10,2},{12,4},{14,6},{1,9},{3,11}... | collective-permute-start | bytes 393224 | tf_op jit(solution)/shard_map/ppermute | solution.py:218
  36.7 7.6 %collective-permute-start.1 = (bf16[8,64,128]{2,1,0:T(8,128)(2,1)}, bf16[8,64,128]{2,1,0:T(8,128)(2,1)S(1)}, u32[]{:S(2)}, u32[]{:S(2)}) collective-permute-start(bf16[8,64,128]{2,1,0:T(8,128)(2,1)} %get-tuple-element.23), channel_id=1, source_target_pairs={{0,6},{2,8},{4,10},{6,12},{8,14},{10,0},{12,2},{14,4},{1,7},{3,9},... | collective-permute-start | bytes 393224 | tf_op jit(solution)/shard_map/ppermute | solution.py:218
  44.3 1.9 %collective-permute-start.2 = (bf16[8,64,128]{2,1,0:T(8,128)(2,1)}, bf16[8,64,128]{2,1,0:T(8,128)(2,1)S(1)}, u32[]{:S(2)}, u32[]{:S(2)}) collective-permute-start(bf16[8,64,128]{2,1,0:T(8,128)(2,1)} %get-tuple-element.24), channel_id=1, source_target_pairs={{0,10},{2,12},{4,14},{6,0},{8,2},{10,4},{12,6},{14,8},{1,11},{3,13... | collective-permute-start | bytes 393224 | tf_op jit(solution)/shard_map/ppermute | solution.py:218
  46.2 4.6 %collective-permute-start.3 = (bf16[8,64,128]{2,1,0:T(8,128)(2,1)}, bf16[8,64,128]{2,1,0:T(8,128)(2,1)S(1)}, u32[]{:S(2)}, u32[]{:S(2)}) collective-permute-start(bf16[8,64,128]{2,1,0:T(8,128)(2,1)} %get-tuple-element.25), channel_id=1, source_target_pairs={{0,4},{2,6},{4,8},{6,10},{8,12},{10,14},{12,0},{14,2},{1,5},{3,7},... | collective-permute-start | bytes 393224 | tf_op jit(solution)/shard_map/ppermute | solution.py:218
  50.8 2.8 %collective-permute-start.4 = (bf16[8,64,128]{2,1,0:T(8,128)(2,1)}, bf16[8,64,128]{2,1,0:T(8,128)(2,1)S(1)}, u32[]{:S(2)}, u32[]{:S(2)}) collective-permute-start(bf16[8,64,128]{2,1,0:T(8,128)(2,1)} %get-tuple-element.26), channel_id=1, source_target_pairs={{0,12},{2,14},{4,0},{6,2},{8,4},{10,6},{12,8},{14,10},{1,13},{3,15... | collective-permute-start | bytes 393224 | tf_op jit(solution)/shard_map/ppermute | solution.py:218
  53.7 0.2 dynamic-slice_bitcast_fusion
  53.8 0.2 copy.13
  54.0 0.0 collective-permute-done.refs_1_
  54.1 2.7 %collective-permute-start.5 = (bf16[8,64,128]{2,1,0:T(8,128)(2,1)}, bf16[8,64,128]{2,1,0:T(8,128)(2,1)S(1)}, u32[]{:S(2)}, u32[]{:S(2)}) collective-permute-start(bf16[8,64,128]{2,1,0:T(8,128)(2,1)} %get-tuple-element.27), channel_id=1, source_target_pairs={{0,2},{2,4},{4,6},{6,8},{8,10},{10,12},{12,14},{14,0},{1,3},{3,5},... | collective-permute-start | bytes 393224 | tf_op jit(solution)/shard_map/ppermute | solution.py:218
  56.8 3.8 %collective-permute-start.6 = (bf16[8,64,128]{2,1,0:T(8,128)(2,1)}, bf16[8,64,128]{2,1,0:T(8,128)(2,1)S(1)}, u32[]{:S(2)}, u32[]{:S(2)}) collective-permute-start(bf16[8,64,128]{2,1,0:T(8,128)(2,1)} %get-tuple-element.28), channel_id=1, source_target_pairs={{0,14},{2,0},{4,2},{6,4},{8,6},{10,8},{12,10},{14,12},{1,15},{3,1}... | collective-permute-start | bytes 393224 | tf_op jit(solution)/shard_map/ppermute | solution.py:218
  60.6 0.2 constant_dynamic-slice_fusion.1
  60.8 0.1 copy.19
  60.9 0.1 copy.20
  61.1 0.0 collective-permute-done.2.refs_3_
  61.1 0.5 collective-permute-done.4.refs_5_
  61.6 0.0 collective-permute-done.5.refs_6_
  61.6 3.5 %collective-permute-done.6.refs_7_ = bf16[8,64,128]{2,1,0:T(8,128)(2,1)S(1)} collective-permute-done((bf16[8,64,128]{2,1,0:T(8,128)(2,1)}, bf16[8,64,128]{2,1,0:T(8,128)(2,1)S(1)}, u32[]{:S(2)}, u32[]{:S(2)}) %collective-permute-start.6) | collective-permute-done | bytes 131104 | tf_op jit(solution)/shard_map/ppermute | solution.py:218
  65.1 0.6 copy-done.12
  65.8 7.4 %ladder_partials.1 = (f32[64,64,128]{2,1,0:T(8,128)S(1)}, bf16[64,64,128]{2,1,0:T(8,128)(2,1)}) custom-call(bf16[64,2,64,128]{3,2,1,0:T(8,128)(2,1)} %all-to-all-done.amps_ref, bf16[128,768]{1,0:T(8,128)(2,1)S(1)} %pad_maximum_fusion.left_ref, bf16[2,768,128]{2,1,0:T(8,128)(2,1)S(1)} %bitcast.24), custom_call_target="tpu_custom_call" | custom-call | flops 4294967296 | bytes 6291456 | tf_op jit(solution)/shard_map/ladder_partials/pallas_call | solution.py:154
  73.2 7.4 %collective-permute-start.7 = (bf16[64,64,128]{2,1,0:T(8,128)(2,1)}, bf16[64,64,128]{2,1,0:T(8,128)(2,1)}, u32[]{:S(2)}, u32[]{:S(2)}) collective-permute-start(bf16[64,64,128]{2,1,0:T(8,128)(2,1)} %get-tuple-element.39), channel_id=1, source_target_pairs={{0,1},{1,0},{2,3},{3,2},{4,5},{5,4},{6,7},{7,6},{8,9},{9,8},{10,11... | collective-permute-start | bytes 3145736 | tf_op jit(solution)/shard_map/ppermute | solution.py:231
  80.6 2.1 %sum_parts.1 = bf16[8,64,128]{2,1,0:T(8,128)(2,1)} custom-call(bf16[8,64,128]{2,1,0:T(8,128)(2,1)} %get-tuple-element.29.refs_0_, bf16[8,64,128]{2,1,0:T(8,128)(2,1)} %copy-done.6, bf16[8,64,128]{2,1,0:T(8,128)(2,1)} %copy-done.7, bf16[8,64,128]{2,1,0:T(8,128)(2,1)} %copy-done.8, bf16[8,64,128]{2,1,0:T(8,128)(2,1)} %copy-done.9, ...), custom_call_target="tpu_custom_call" | custom-call | flops 524288 | bytes 1179648 | tf_op jit(solution)/shard_map/sum_parts/pallas_call | solution.py:186
  82.7 0.5 collective-permute-done.7
  83.2 2.5 %fusion = bf16[64,1,1,64,128]{4,3,2,1,0:T(8,128)(2,1)} fusion(f32[64,64,128]{2,1,0:T(8,128)S(1)} %get-tuple-element.38, bf16[64,64,128]{2,1,0:T(8,128)(2,1)} %collective-permute-done.7), kind=kLoop, calls=%fused_computation.1 | loop fusion | flops 1572864 | bytes 4194304
  (24 shorter events, 0.1 us)
Async XLA Ops:
  0.6 53.0 %copy-start = (bf16[6,1,2,128,128]{4,3,2,1,0:T(8,128)(2,1)S(1)}, bf16[6,1,2,128,128]{4,3,2,1,0:T(8,128)(2,1)}, u32[]{:S(2)}) copy-start(bf16[6,1,2,128,128]{4,3,2,1,0:T(8,128)(2,1)} %param.14) | copy-start | bytes 1179652
  3.3 14.6 %copy-start.1 = (bf16[1,1,64,64,128]{4,3,2,1,0:T(8,128)(2,1)S(1)}, bf16[1,1,64,64,128]{4,3,2,1,0:T(8,128)(2,1)}, u32[]{:S(2)}) copy-start(bf16[1,1,64,64,128]{4,3,2,1,0:T(8,128)(2,1)} %param.8) | copy-start | bytes 3145732
  3.4 14.6 %copy-start.2 = (bf16[1,1,64,128,128]{4,3,2,1,0:T(8,128)(2,1)S(1)}, bf16[1,1,64,128,128]{4,3,2,1,0:T(8,128)(2,1)}, u32[]{:S(2)}) copy-start(bf16[1,1,64,128,128]{4,3,2,1,0:T(8,128)(2,1)} %param.9) | copy-start | bytes 6291460
  3.4 14.6 %copy-start.3 = (s32[64,2]{0,1:T(2,128)S(1)}, s32[64,2]{0,1:T(2,128)}, u32[]{:S(2)}) copy-start(s32[64,2]{0,1:T(2,128)} %param.10) | copy-start | bytes 1540
  3.4 14.6 %copy-start.4 = (s32[64,2]{0,1:T(2,128)S(1)}, s32[64,2]{0,1:T(2,128)}, u32[]{:S(2)}) copy-start(s32[64,2]{0,1:T(2,128)} %param.11) | copy-start | bytes 1540
  3.4 61.7 %all-to-all-start = ((bf16[64,2,64,128]{3,2,1,0:T(8,128)(2,1)}), bf16[64,2,64,128]{3,2,1,0:T(8,128)(2,1)}, u32[]{:S(2)}, u32[]{:S(2)}) async-start(bf16[64,2,64,128]{3,2,1,0:T(8,128)(2,1)} %outgoing_tiles.1), calls=%async_computation | async-start | bytes 4194304 | tf_op jit(solution)/shard_map/all_to_all | solution.py:210
  22.2 38.8 %copy-start.5 = (bf16[6,1,2,128,128]{4,3,2,1,0:T(8,128)(2,1)S(1)}, bf16[6,1,2,128,128]{4,3,2,1,0:T(8,128)(2,1)}, u32[]{:S(2)}) copy-start(bf16[6,1,2,128,128]{4,3,2,1,0:T(8,128)(2,1)} %param.15) | copy-start | bytes 1179652
  22.2 31.8 %collective-permute-start = (bf16[8,64,128]{2,1,0:T(8,128)(2,1)}, bf16[8,64,128]{2,1,0:T(8,128)(2,1)S(1)}, u32[]{:S(2)}, u32[]{:S(2)}) collective-permute-start(bf16[8,64,128]{2,1,0:T(8,128)(2,1)} %get-tuple-element.22), channel_id=1, source_target_pairs={{0,8},{2,10},{4,12},{6,14},{8,0},{10,2},{12,4},{14,6},{1,9},{3,11}... | collective-permute-start | bytes 393224 | tf_op jit(solution)/shard_map/ppermute | solution.py:218
  36.7 20.1 %collective-permute-start.1 = (bf16[8,64,128]{2,1,0:T(8,128)(2,1)}, bf16[8,64,128]{2,1,0:T(8,128)(2,1)S(1)}, u32[]{:S(2)}, u32[]{:S(2)}) collective-permute-start(bf16[8,64,128]{2,1,0:T(8,128)(2,1)} %get-tuple-element.23), channel_id=1, source_target_pairs={{0,6},{2,8},{4,10},{6,12},{8,14},{10,0},{12,2},{14,4},{1,7},{3,9},... | collective-permute-start | bytes 393224 | tf_op jit(solution)/shard_map/ppermute | solution.py:218
  44.3 16.8 %collective-permute-start.2 = (bf16[8,64,128]{2,1,0:T(8,128)(2,1)}, bf16[8,64,128]{2,1,0:T(8,128)(2,1)S(1)}, u32[]{:S(2)}, u32[]{:S(2)}) collective-permute-start(bf16[8,64,128]{2,1,0:T(8,128)(2,1)} %get-tuple-element.24), channel_id=1, source_target_pairs={{0,10},{2,12},{4,14},{6,0},{8,2},{10,4},{12,6},{14,8},{1,11},{3,13... | collective-permute-start | bytes 393224 | tf_op jit(solution)/shard_map/ppermute | solution.py:218
  46.2 14.9 %collective-permute-start.3 = (bf16[8,64,128]{2,1,0:T(8,128)(2,1)}, bf16[8,64,128]{2,1,0:T(8,128)(2,1)S(1)}, u32[]{:S(2)}, u32[]{:S(2)}) collective-permute-start(bf16[8,64,128]{2,1,0:T(8,128)(2,1)} %get-tuple-element.25), channel_id=1, source_target_pairs={{0,4},{2,6},{4,8},{6,10},{8,12},{10,14},{12,0},{14,2},{1,5},{3,7},... | collective-permute-start | bytes 393224 | tf_op jit(solution)/shard_map/ppermute | solution.py:218
  50.8 10.8 %collective-permute-start.4 = (bf16[8,64,128]{2,1,0:T(8,128)(2,1)}, bf16[8,64,128]{2,1,0:T(8,128)(2,1)S(1)}, u32[]{:S(2)}, u32[]{:S(2)}) collective-permute-start(bf16[8,64,128]{2,1,0:T(8,128)(2,1)} %get-tuple-element.26), channel_id=1, source_target_pairs={{0,12},{2,14},{4,0},{6,2},{8,4},{10,6},{12,8},{14,10},{1,13},{3,15... | collective-permute-start | bytes 393224 | tf_op jit(solution)/shard_map/ppermute | solution.py:218
  54.0 19.2 %copy-start.6 = (bf16[8,64,128]{2,1,0:T(8,128)(2,1)}, bf16[8,64,128]{2,1,0:T(8,128)(2,1)S(1)}, u32[]{:S(2)}) copy-start(bf16[8,64,128]{2,1,0:T(8,128)(2,1)S(1)} %collective-permute-done.refs_1_) | copy-start | bytes 393220
  54.1 7.6 %collective-permute-start.5 = (bf16[8,64,128]{2,1,0:T(8,128)(2,1)}, bf16[8,64,128]{2,1,0:T(8,128)(2,1)S(1)}, u32[]{:S(2)}, u32[]{:S(2)}) collective-permute-start(bf16[8,64,128]{2,1,0:T(8,128)(2,1)} %get-tuple-element.27), channel_id=1, source_target_pairs={{0,2},{2,4},{4,6},{6,8},{8,10},{10,12},{12,14},{14,0},{1,3},{3,5},... | collective-permute-start | bytes 393224 | tf_op jit(solution)/shard_map/ppermute | solution.py:218
  56.8 16.4 %copy-start.7 = (bf16[8,64,128]{2,1,0:T(8,128)(2,1)}, bf16[8,64,128]{2,1,0:T(8,128)(2,1)S(1)}, u32[]{:S(2)}) copy-start(bf16[8,64,128]{2,1,0:T(8,128)(2,1)S(1)} %collective-permute-done.1.refs_2_) | copy-start | bytes 393220
  56.8 8.3 %collective-permute-start.6 = (bf16[8,64,128]{2,1,0:T(8,128)(2,1)}, bf16[8,64,128]{2,1,0:T(8,128)(2,1)S(1)}, u32[]{:S(2)}, u32[]{:S(2)}) collective-permute-start(bf16[8,64,128]{2,1,0:T(8,128)(2,1)} %get-tuple-element.28), channel_id=1, source_target_pairs={{0,14},{2,0},{4,2},{6,4},{8,6},{10,8},{12,10},{14,12},{1,15},{3,1}... | collective-permute-start | bytes 393224 | tf_op jit(solution)/shard_map/ppermute | solution.py:218
  61.1 12.1 %copy-start.8 = (bf16[8,64,128]{2,1,0:T(8,128)(2,1)}, bf16[8,64,128]{2,1,0:T(8,128)(2,1)S(1)}, u32[]{:S(2)}) copy-start(bf16[8,64,128]{2,1,0:T(8,128)(2,1)S(1)} %collective-permute-done.2.refs_3_) | copy-start | bytes 393220
  61.1 4.0 %copy-start.9 = (bf16[8,64,128]{2,1,0:T(8,128)(2,1)}, bf16[8,64,128]{2,1,0:T(8,128)(2,1)S(1)}, u32[]{:S(2)}) copy-start(bf16[8,64,128]{2,1,0:T(8,128)(2,1)S(1)} %collective-permute-done.3.refs_4_) | copy-start | bytes 393220
  61.6 3.5 %copy-start.10 = (bf16[8,64,128]{2,1,0:T(8,128)(2,1)}, bf16[8,64,128]{2,1,0:T(8,128)(2,1)S(1)}, u32[]{:S(2)}) copy-start(bf16[8,64,128]{2,1,0:T(8,128)(2,1)S(1)} %collective-permute-done.4.refs_5_) | copy-start | bytes 393220
  61.6 3.5 %copy-start.11 = (bf16[8,64,128]{2,1,0:T(8,128)(2,1)}, bf16[8,64,128]{2,1,0:T(8,128)(2,1)S(1)}, u32[]{:S(2)}) copy-start(bf16[8,64,128]{2,1,0:T(8,128)(2,1)S(1)} %collective-permute-done.5.refs_6_) | copy-start | bytes 393220
  65.1 0.6 copy-start.12
  73.2 10.0 %collective-permute-start.7 = (bf16[64,64,128]{2,1,0:T(8,128)(2,1)}, bf16[64,64,128]{2,1,0:T(8,128)(2,1)}, u32[]{:S(2)}, u32[]{:S(2)}) collective-permute-start(bf16[64,64,128]{2,1,0:T(8,128)(2,1)} %get-tuple-element.39), channel_id=1, source_target_pairs={{0,1},{1,0},{2,3},{3,2},{4,5},{5,4},{6,7},{7,6},{8,9},{9,8},{10,11... | collective-permute-start | bytes 3145736 | tf_op jit(solution)/shard_map/ppermute | solution.py:231

commit v4 on v3

--- a/solution.py
+++ b/solution.py
@@ -193,6 +193,34 @@
     )(*parts)
 
 
+def final_kernel(own_ref, received_ref, out_hbm, out_ref, sems):
+    items = out_ref.shape[0]
+    share = items // SPLITS
+    stores = []
+    for part in range(SPLITS):
+        block = pl.ds(part * share, share)
+        total = own_ref[block] + received_ref[block].astype(jnp.float32)
+        out_ref[block] = total.astype(out_ref.dtype)
+        stores.append(pltpu.make_async_copy(out_ref.at[block], out_hbm.at[block], sems.at[part]))
+        stores[-1].start()
+    for store in stores:
+        store.wait()
+
+
+def final_sum(own, received):
+    vmem = pl.BlockSpec(memory_space=pltpu.VMEM)
+    return pl.pallas_call(
+        final_kernel,
+        in_specs=[vmem, vmem],
+        out_specs=pl.BlockSpec(memory_space=pltpu.HBM),
+        out_shape=pltpu.HBM(own.shape, received.dtype),
+        scratch_shapes=[pltpu.VMEM(own.shape, received.dtype), pltpu.SemaphoreType.DMA((SPLITS,))],
+        compiler_params=pltpu.CompilerParams(vmem_limit_bytes=12 << 20),
+        cost_estimate=pl.CostEstimate(flops=own.size, bytes_accessed=8 * own.size, transcendentals=0),
+        name="final_sum",
+    )(own, received)
+
+
 def shards(
     amplitudes,
     cycle_ints,
@@ -229,7 +257,7 @@
 
     own, other = ladder_partials(arriving, left, right)
     received = lax.ppermute(other, "rep", [(0, 1), (1, 0)])
-    ladder_part = (own + received.astype(jnp.float32)).astype(jnp.bfloat16)[:, None, None]
+    ladder_part = final_sum(own, received)[:, None, None]
     return (cycle_part, ladder_part)
 
 

time: 86.3 us -> 84.6 us (0.980)
  other arithmetic: 2.54 us -> 0.02 us
  Pallas kernels: 16.4 us -> 17.5 us
    unnamed x1 -> x0, other arithmetic: 2.53 us -> none
    pallas_call x0 -> x1, Pallas kernels: none -> 1.04 us  [final_sum(): pl.pallas_call(final_kernel, in_specs=[vmem, vmem], out_specs=pl.BlockSpe...]
where the time goes in v4:
time: 84.6 us; the launch traced here: 84.1 us
  starting transfers between devices  59.8 us (71%)
  Pallas kernels  17.5 us (21%)
  waiting for transfers between devices  4.37 us (5%)
  local copies, waits for them, and re-layouts  1.47 us (2%)
  between operations  0.98 us (1%)
    ppermute x7, starting transfers between devices, shards(): parts.append(lax.ppermute(partials[step], 'occ', ring))  37.9 us
    all_to_all x1, starting transfers between devices, shards(): lax.all_to_all(outgoing, 'vir', split_axis=0, concat_axis=0, tiled=True)  14.6 us
    pallas_call x1, Pallas kernels, ladder_partials(): pl.pallas_call(ladder_kernel, grid=(items // GROUP,), in_specs=[pl.BlockS...  7.44 us
    ppermute x1, starting transfers between devices, shards(): received = lax.ppermute(other, 'rep', [(0, 1), (1, 0)])  7.38 us
    pallas_call x1, Pallas kernels, cycle_partials(): pl.pallas_call(cycle_kernel, grid_spec=pltpu.PrefetchScalarGridSpec(num_s...  4.21 us
    ppermute x7, waiting for transfers between devices, shards(): parts.append(lax.ppermute(partials[step], 'occ', ring))  3.97 us
    pallas_call x1, Pallas kernels, gather_tiles(): pl.pallas_call(gather_kernel, in_specs=[pl.BlockSpec(memory_space=pltpu.H...  2.7 us
    pallas_call x1, Pallas kernels, sum_parts(): pl.pallas_call(sum_kernel, in_specs=[pl.BlockSpec(memory_space=pltpu.VMEM...  2.08 us
  transfers between devices with their start and end apart: 9, of which 3 were waited for; matrix products, arithmetic and copies ran while one was open for 1% of the time, Pallas kernels for 7%

profile of v4, /device:TPU:1, one launch (start us, length us, event | category | flops | bytes accessed | tf_op | source)
XLA Modules:
  0.0 84.1 jit_solution(16221997086566574555)
XLA Ops:
  0.6 0.0 copy-start
  0.6 2.7 %outgoing_tiles.1 = bf16[64,2,64,128]{3,2,1,0:T(8,128)(2,1)} custom-call(s32[64]{0:T(128)} %order_hbm.1, s32[2,64]{1,0:T(2,128)} %bitcast.30, bf16[64,64,128]{2,1,0:T(8,128)(2,1)} %bitcast.20), custom_call_target="tpu_custom_call" | custom-call | bytes 4194304 | tf_op jit(solution)/shard_map/outgoing_tiles/pallas_call | solution.py:54
  3.3 0.0 copy-start.1
  3.4 0.0 copy-start.2
  3.4 0.0 copy-start.3
  3.4 0.0 copy-start.4
  3.4 14.6 %all-to-all-start = ((bf16[64,2,64,128]{3,2,1,0:T(8,128)(2,1)}), bf16[64,2,64,128]{3,2,1,0:T(8,128)(2,1)}, u32[]{:S(2)}, u32[]{:S(2)}) async-start(bf16[64,2,64,128]{3,2,1,0:T(8,128)(2,1)} %outgoing_tiles.1), calls=%async_computation | async-start | bytes 4194304 | tf_op jit(solution)/shard_map/all_to_all | solution.py:238
  18.0 4.2 %cycle_partials.1 = (bf16[8,64,128]{2,1,0:T(8,128)(2,1)}, bf16[8,64,128]{2,1,0:T(8,128)(2,1)}, bf16[8,64,128]{2,1,0:T(8,128)(2,1)}, bf16[8,64,128]{2,1,0:T(8,128...) custom-call(s32[1]{0:T(128)} %bitcast.2.me_ref, ...), custom_call_target="tpu_custom_call" | custom-call | flops 268435456 | bytes 4194304 | tf_op jit(solution)/shard_map/cycle_partials/pallas_call | solution.py:98
  22.2 0.0 copy-start.5
  22.2 14.4 %collective-permute-start = (bf16[8,64,128]{2,1,0:T(8,128)(2,1)}, bf16[8,64,128]{2,1,0:T(8,128)(2,1)S(1)}, u32[]{:S(2)}, u32[]{:S(2)}) collective-permute-start(bf16[8,64,128]{2,1,0:T(8,128)(2,1)} %get-tuple-element.22), channel_id=1, source_target_pairs={{0,8},{2,10},{4,12},{6,14},{8,0},{10,2},{12,4},{14,6},{1,9},{3,11}... | collective-permute-start | bytes 393224 | tf_op jit(solution)/shard_map/ppermute | solution.py:246
  36.7 7.6 %collective-permute-start.1 = (bf16[8,64,128]{2,1,0:T(8,128)(2,1)}, bf16[8,64,128]{2,1,0:T(8,128)(2,1)S(1)}, u32[]{:S(2)}, u32[]{:S(2)}) collective-permute-start(bf16[8,64,128]{2,1,0:T(8,128)(2,1)} %get-tuple-element.23), channel_id=1, source_target_pairs={{0,6},{2,8},{4,10},{6,12},{8,14},{10,0},{12,2},{14,4},{1,7},{3,9},... | collective-permute-start | bytes 393224 | tf_op jit(solution)/shard_map/ppermute | solution.py:246
  44.3 1.9 %collective-permute-start.2 = (bf16[8,64,128]{2,1,0:T(8,128)(2,1)}, bf16[8,64,128]{2,1,0:T(8,128)(2,1)S(1)}, u32[]{:S(2)}, u32[]{:S(2)}) collective-permute-start(bf16[8,64,128]{2,1,0:T(8,128)(2,1)} %get-tuple-element.24), channel_id=1, source_target_pairs={{0,10},{2,12},{4,14},{6,0},{8,2},{10,4},{12,6},{14,8},{1,11},{3,13... | collective-permute-start | bytes 393224 | tf_op jit(solution)/shard_map/ppermute | solution.py:246
  46.2 4.6 %collective-permute-start.3 = (bf16[8,64,128]{2,1,0:T(8,128)(2,1)}, bf16[8,64,128]{2,1,0:T(8,128)(2,1)S(1)}, u32[]{:S(2)}, u32[]{:S(2)}) collective-permute-start(bf16[8,64,128]{2,1,0:T(8,128)(2,1)} %get-tuple-element.25), channel_id=1, source_target_pairs={{0,4},{2,6},{4,8},{6,10},{8,12},{10,14},{12,0},{14,2},{1,5},{3,7},... | collective-permute-start | bytes 393224 | tf_op jit(solution)/shard_map/ppermute | solution.py:246
  50.8 2.8 %collective-permute-start.4 = (bf16[8,64,128]{2,1,0:T(8,128)(2,1)}, bf16[8,64,128]{2,1,0:T(8,128)(2,1)S(1)}, u32[]{:S(2)}, u32[]{:S(2)}) collective-permute-start(bf16[8,64,128]{2,1,0:T(8,128)(2,1)} %get-tuple-element.26), channel_id=1, source_target_pairs={{0,12},{2,14},{4,0},{6,2},{8,4},{10,6},{12,8},{14,10},{1,13},{3,15... | collective-permute-start | bytes 393224 | tf_op jit(solution)/shard_map/ppermute | solution.py:246
  53.7 0.2 dynamic-slice_bitcast_fusion
  53.8 0.2 copy.13
  54.0 0.0 collective-permute-done.refs_1_
  54.1 2.7 %collective-permute-start.5 = (bf16[8,64,128]{2,1,0:T(8,128)(2,1)}, bf16[8,64,128]{2,1,0:T(8,128)(2,1)S(1)}, u32[]{:S(2)}, u32[]{:S(2)}) collective-permute-start(bf16[8,64,128]{2,1,0:T(8,128)(2,1)} %get-tuple-element.27), channel_id=1, source_target_pairs={{0,2},{2,4},{4,6},{6,8},{8,10},{10,12},{12,14},{14,0},{1,3},{3,5},... | collective-permute-start | bytes 393224 | tf_op jit(solution)/shard_map/ppermute | solution.py:246
  56.8 3.8 %collective-permute-start.6 = (bf16[8,64,128]{2,1,0:T(8,128)(2,1)}, bf16[8,64,128]{2,1,0:T(8,128)(2,1)S(1)}, u32[]{:S(2)}, u32[]{:S(2)}) collective-permute-start(bf16[8,64,128]{2,1,0:T(8,128)(2,1)} %get-tuple-element.28), channel_id=1, source_target_pairs={{0,14},{2,0},{4,2},{6,4},{8,6},{10,8},{12,10},{14,12},{1,15},{3,1}... | collective-permute-start | bytes 393224 | tf_op jit(solution)/shard_map/ppermute | solution.py:246
  60.6 0.2 constant_dynamic-slice_fusion.1
  60.8 0.1 copy.19
  60.9 0.1 copy.20
  61.1 0.0 collective-permute-done.2.refs_3_
  61.1 0.5 collective-permute-done.4.refs_5_
  61.6 0.0 collective-permute-done.5.refs_6_
  61.6 3.5 %collective-permute-done.6.refs_7_ = bf16[8,64,128]{2,1,0:T(8,128)(2,1)S(1)} collective-permute-done((bf16[8,64,128]{2,1,0:T(8,128)(2,1)}, bf16[8,64,128]{2,1,0:T(8,128)(2,1)S(1)}, u32[]{:S(2)}, u32[]{:S(2)}) %collective-permute-start.6) | collective-permute-done | bytes 131104 | tf_op jit(solution)/shard_map/ppermute | solution.py:246
  65.2 0.6 copy-done.12
  65.8 7.4 %ladder_partials.1 = (f32[64,64,128]{2,1,0:T(8,128)S(1)}, bf16[64,64,128]{2,1,0:T(8,128)(2,1)}) custom-call(bf16[64,2,64,128]{3,2,1,0:T(8,128)(2,1)} %all-to-all-done.amps_ref, bf16[128,768]{1,0:T(8,128)(2,1)S(1)} %pad_maximum_fusion.left_ref, bf16[2,768,128]{2,1,0:T(8,128)(2,1)S(1)} %bitcast.23), custom_call_target="tpu_custom_call" | custom-call | flops 4294967296 | bytes 6291456 | tf_op jit(solution)/shard_map/ladder_partials/pallas_call | solution.py:154
  73.2 7.4 %collective-permute-start.7 = (bf16[64,64,128]{2,1,0:T(8,128)(2,1)}, bf16[64,64,128]{2,1,0:T(8,128)(2,1)S(1)}, u32[]{:S(2)}, u32[]{:S(2)}) collective-permute-start(bf16[64,64,128]{2,1,0:T(8,128)(2,1)} %get-tuple-element.39), channel_id=1, source_target_pairs={{0,1},{1,0},{2,3},{3,2},{4,5},{5,4},{6,7},{7,6},{8,9},{9,8},{10,11... | collective-permute-start | bytes 3145736 | tf_op jit(solution)/shard_map/ppermute | solution.py:259
  80.6 2.1 %sum_parts.1 = bf16[8,64,128]{2,1,0:T(8,128)(2,1)} custom-call(bf16[8,64,128]{2,1,0:T(8,128)(2,1)} %get-tuple-element.29.refs_0_, bf16[8,64,128]{2,1,0:T(8,128)(2,1)} %copy-done.6, bf16[8,64,128]{2,1,0:T(8,128)(2,1)} %copy-done.7, bf16[8,64,128]{2,1,0:T(8,128)(2,1)} %copy-done.8, bf16[8,64,128]{2,1,0:T(8,128)(2,1)} %copy-done.9, ...), custom_call_target="tpu_custom_call" | custom-call | flops 524288 | bytes 1179648 | tf_op jit(solution)/shard_map/sum_parts/pallas_call | solution.py:186
  82.7 0.4 collective-permute-done.7.received_ref
  83.1 1.0 %final_sum.1 = bf16[64,64,128]{2,1,0:T(8,128)(2,1)} custom-call(f32[64,64,128]{2,1,0:T(8,128)S(1)} %get-tuple-element.38.own_ref, bf16[64,64,128]{2,1,0:T(8,128)(2,1)S(1)} %collective-permute-done.7.received_ref), custom_call_target="tpu_custom_call" | custom-call | flops 524288 | bytes 4194304 | tf_op jit(solution)/shard_map/final_sum/pallas_call | solution.py:212
  (24 shorter events, 0.1 us)
Async XLA Ops:
  0.6 53.0 %copy-start = (bf16[6,1,2,128,128]{4,3,2,1,0:T(8,128)(2,1)S(1)}, bf16[6,1,2,128,128]{4,3,2,1,0:T(8,128)(2,1)}, u32[]{:S(2)}) copy-start(bf16[6,1,2,128,128]{4,3,2,1,0:T(8,128)(2,1)} %param.14) | copy-start | bytes 1179652
  3.3 14.6 %copy-start.1 = (bf16[1,1,64,64,128]{4,3,2,1,0:T(8,128)(2,1)S(1)}, bf16[1,1,64,64,128]{4,3,2,1,0:T(8,128)(2,1)}, u32[]{:S(2)}) copy-start(bf16[1,1,64,64,128]{4,3,2,1,0:T(8,128)(2,1)} %param.8) | copy-start | bytes 3145732
  3.4 14.6 %copy-start.2 = (bf16[1,1,64,128,128]{4,3,2,1,0:T(8,128)(2,1)S(1)}, bf16[1,1,64,128,128]{4,3,2,1,0:T(8,128)(2,1)}, u32[]{:S(2)}) copy-start(bf16[1,1,64,128,128]{4,3,2,1,0:T(8,128)(2,1)} %param.9) | copy-start | bytes 6291460
  3.4 14.6 %copy-start.3 = (s32[64,2]{0,1:T(2,128)S(1)}, s32[64,2]{0,1:T(2,128)}, u32[]{:S(2)}) copy-start(s32[64,2]{0,1:T(2,128)} %param.10) | copy-start | bytes 1540
  3.4 14.6 %copy-start.4 = (s32[64,2]{0,1:T(2,128)S(1)}, s32[64,2]{0,1:T(2,128)}, u32[]{:S(2)}) copy-start(s32[64,2]{0,1:T(2,128)} %param.11) | copy-start | bytes 1540
  3.4 61.7 %all-to-all-start = ((bf16[64,2,64,128]{3,2,1,0:T(8,128)(2,1)}), bf16[64,2,64,128]{3,2,1,0:T(8,128)(2,1)}, u32[]{:S(2)}, u32[]{:S(2)}) async-start(bf16[64,2,64,128]{3,2,1,0:T(8,128)(2,1)} %outgoing_tiles.1), calls=%async_computation | async-start | bytes 4194304 | tf_op jit(solution)/shard_map/all_to_all | solution.py:238
  22.2 38.8 %copy-start.5 = (bf16[6,1,2,128,128]{4,3,2,1,0:T(8,128)(2,1)S(1)}, bf16[6,1,2,128,128]{4,3,2,1,0:T(8,128)(2,1)}, u32[]{:S(2)}) copy-start(bf16[6,1,2,128,128]{4,3,2,1,0:T(8,128)(2,1)} %param.15) | copy-start | bytes 1179652
  22.2 31.8 %collective-permute-start = (bf16[8,64,128]{2,1,0:T(8,128)(2,1)}, bf16[8,64,128]{2,1,0:T(8,128)(2,1)S(1)}, u32[]{:S(2)}, u32[]{:S(2)}) collective-permute-start(bf16[8,64,128]{2,1,0:T(8,128)(2,1)} %get-tuple-element.22), channel_id=1, source_target_pairs={{0,8},{2,10},{4,12},{6,14},{8,0},{10,2},{12,4},{14,6},{1,9},{3,11}... | collective-permute-start | bytes 393224 | tf_op jit(solution)/shard_map/ppermute | solution.py:246
  36.7 20.1 %collective-permute-start.1 = (bf16[8,64,128]{2,1,0:T(8,128)(2,1)}, bf16[8,64,128]{2,1,0:T(8,128)(2,1)S(1)}, u32[]{:S(2)}, u32[]{:S(2)}) collective-permute-start(bf16[8,64,128]{2,1,0:T(8,128)(2,1)} %get-tuple-element.23), channel_id=1, source_target_pairs={{0,6},{2,8},{4,10},{6,12},{8,14},{10,0},{12,2},{14,4},{1,7},{3,9},... | collective-permute-start | bytes 393224 | tf_op jit(solution)/shard_map/ppermute | solution.py:246
  44.3 16.8 %collective-permute-start.2 = (bf16[8,64,128]{2,1,0:T(8,128)(2,1)}, bf16[8,64,128]{2,1,0:T(8,128)(2,1)S(1)}, u32[]{:S(2)}, u32[]{:S(2)}) collective-permute-start(bf16[8,64,128]{2,1,0:T(8,128)(2,1)} %get-tuple-element.24), channel_id=1, source_target_pairs={{0,10},{2,12},{4,14},{6,0},{8,2},{10,4},{12,6},{14,8},{1,11},{3,13... | collective-permute-start | bytes 393224 | tf_op jit(solution)/shard_map/ppermute | solution.py:246
  46.2 14.9 %collective-permute-start.3 = (bf16[8,64,128]{2,1,0:T(8,128)(2,1)}, bf16[8,64,128]{2,1,0:T(8,128)(2,1)S(1)}, u32[]{:S(2)}, u32[]{:S(2)}) collective-permute-start(bf16[8,64,128]{2,1,0:T(8,128)(2,1)} %get-tuple-element.25), channel_id=1, source_target_pairs={{0,4},{2,6},{4,8},{6,10},{8,12},{10,14},{12,0},{14,2},{1,5},{3,7},... | collective-permute-start | bytes 393224 | tf_op jit(solution)/shard_map/ppermute | solution.py:246
  50.8 10.8 %collective-permute-start.4 = (bf16[8,64,128]{2,1,0:T(8,128)(2,1)}, bf16[8,64,128]{2,1,0:T(8,128)(2,1)S(1)}, u32[]{:S(2)}, u32[]{:S(2)}) collective-permute-start(bf16[8,64,128]{2,1,0:T(8,128)(2,1)} %get-tuple-element.26), channel_id=1, source_target_pairs={{0,12},{2,14},{4,0},{6,2},{8,4},{10,6},{12,8},{14,10},{1,13},{3,15... | collective-permute-start | bytes 393224 | tf_op jit(solution)/shard_map/ppermute | solution.py:246
  54.0 11.1 %copy-start.6 = (bf16[8,64,128]{2,1,0:T(8,128)(2,1)}, bf16[8,64,128]{2,1,0:T(8,128)(2,1)S(1)}, u32[]{:S(2)}) copy-start(bf16[8,64,128]{2,1,0:T(8,128)(2,1)S(1)} %collective-permute-done.refs_1_) | copy-start | bytes 393220
  54.1 7.6 %collective-permute-start.5 = (bf16[8,64,128]{2,1,0:T(8,128)(2,1)}, bf16[8,64,128]{2,1,0:T(8,128)(2,1)S(1)}, u32[]{:S(2)}, u32[]{:S(2)}) collective-permute-start(bf16[8,64,128]{2,1,0:T(8,128)(2,1)} %get-tuple-element.27), channel_id=1, source_target_pairs={{0,2},{2,4},{4,6},{6,8},{8,10},{10,12},{12,14},{14,0},{1,3},{3,5},... | collective-permute-start | bytes 393224 | tf_op jit(solution)/shard_map/ppermute | solution.py:246
  56.8 8.3 %copy-start.7 = (bf16[8,64,128]{2,1,0:T(8,128)(2,1)}, bf16[8,64,128]{2,1,0:T(8,128)(2,1)S(1)}, u32[]{:S(2)}) copy-start(bf16[8,64,128]{2,1,0:T(8,128)(2,1)S(1)} %collective-permute-done.1.refs_2_) | copy-start | bytes 393220
  56.8 8.3 %collective-permute-start.6 = (bf16[8,64,128]{2,1,0:T(8,128)(2,1)}, bf16[8,64,128]{2,1,0:T(8,128)(2,1)S(1)}, u32[]{:S(2)}, u32[]{:S(2)}) collective-permute-start(bf16[8,64,128]{2,1,0:T(8,128)(2,1)} %get-tuple-element.28), channel_id=1, source_target_pairs={{0,14},{2,0},{4,2},{6,4},{8,6},{10,8},{12,10},{14,12},{1,15},{3,1}... | collective-permute-start | bytes 393224 | tf_op jit(solution)/shard_map/ppermute | solution.py:246
  61.1 4.0 %copy-start.8 = (bf16[8,64,128]{2,1,0:T(8,128)(2,1)}, bf16[8,64,128]{2,1,0:T(8,128)(2,1)S(1)}, u32[]{:S(2)}) copy-start(bf16[8,64,128]{2,1,0:T(8,128)(2,1)S(1)} %collective-permute-done.2.refs_3_) | copy-start | bytes 393220
  61.1 4.0 %copy-start.9 = (bf16[8,64,128]{2,1,0:T(8,128)(2,1)}, bf16[8,64,128]{2,1,0:T(8,128)(2,1)S(1)}, u32[]{:S(2)}) copy-start(bf16[8,64,128]{2,1,0:T(8,128)(2,1)S(1)} %collective-permute-done.3.refs_4_) | copy-start | bytes 393220
  61.6 3.5 %copy-start.10 = (bf16[8,64,128]{2,1,0:T(8,128)(2,1)}, bf16[8,64,128]{2,1,0:T(8,128)(2,1)S(1)}, u32[]{:S(2)}) copy-start(bf16[8,64,128]{2,1,0:T(8,128)(2,1)S(1)} %collective-permute-done.4.refs_5_) | copy-start | bytes 393220
  61.6 3.5 %copy-start.11 = (bf16[8,64,128]{2,1,0:T(8,128)(2,1)}, bf16[8,64,128]{2,1,0:T(8,128)(2,1)S(1)}, u32[]{:S(2)}) copy-start(bf16[8,64,128]{2,1,0:T(8,128)(2,1)S(1)} %collective-permute-done.5.refs_6_) | copy-start | bytes 393220
  65.1 0.7 copy-start.12
  73.2 9.9 %collective-permute-start.7 = (bf16[64,64,128]{2,1,0:T(8,128)(2,1)}, bf16[64,64,128]{2,1,0:T(8,128)(2,1)S(1)}, u32[]{:S(2)}, u32[]{:S(2)}) collective-permute-start(bf16[64,64,128]{2,1,0:T(8,128)(2,1)} %get-tuple-element.39), channel_id=1, source_target_pairs={{0,1},{1,0},{2,3},{3,2},{4,5},{5,4},{6,7},{7,6},{8,9},{9,8},{10,11... | collective-permute-start | bytes 3145736 | tf_op jit(solution)/shard_map/ppermute | solution.py:259

commit v5 on v4

--- a/solution.py
+++ b/solution.py
@@ -144,7 +144,7 @@
             summed = jnp.dot(left, jnp.concatenate(columns, axis=1), preferred_element_type=jnp.float32)
             for place in range(2):
                 tile = summed[:, place * width : (place + 1) * width]
-                own_ref[start + first + place] = tile[:half]
+                own_ref[start + first + place] = tile[:half].astype(own_ref.dtype)
                 other_ref[start + first + place] = tile[half:].astype(other_ref.dtype)
 
 
@@ -164,7 +164,7 @@
             pl.BlockSpec((GROUP, half, width), lambda g: (g, 0, 0)),
         ],
         out_shape=[
-            jax.ShapeDtypeStruct((items, half, width), jnp.float32),
+            jax.ShapeDtypeStruct((items, half, width), jnp.bfloat16),
             jax.ShapeDtypeStruct((items, half, width), jnp.bfloat16),
         ],
         compiler_params=pltpu.CompilerParams(vmem_limit_bytes=12 << 20),
@@ -199,7 +199,7 @@
     stores = []
     for part in range(SPLITS):
         block = pl.ds(part * share, share)
-        total = own_ref[block] + received_ref[block].astype(jnp.float32)
+        total = own_ref[block].astype(jnp.float32) + received_ref[block].astype(jnp.float32)
         out_ref[block] = total.astype(out_ref.dtype)
         stores.append(pltpu.make_async_copy(out_ref.at[block], out_hbm.at[block], sems.at[part]))
         stores[-1].start()

time: 84.6 us -> 83.7 us (0.989)
  transfers between devices with their start and end apart: 9 -> 9, of which waited for: 3 -> 3; matrix products, arithmetic and copies ran while one was open for 1% -> 1% of each run, Pallas kernels for 7% -> 8%
where the time goes in v5:
time: 83.7 us; the launch traced here: 83.2 us
  starting transfers between devices  59.8 us (71%)
  Pallas kernels  16.8 us (20%)
  waiting for transfers between devices  4.15 us (5%)
  local copies, waits for them, and re-layouts  1.53 us (2%)
  between operations  0.98 us (1%)
    ppermute x7, starting transfers between devices, shards(): parts.append(lax.ppermute(partials[step], 'occ', ring))  37.9 us
    all_to_all x1, starting transfers between devices, shards(): lax.all_to_all(outgoing, 'vir', split_axis=0, concat_axis=0, tiled=True)  14.6 us
    ppermute x1, starting transfers between devices, shards(): received = lax.ppermute(other, 'rep', [(0, 1), (1, 0)])  7.33 us
    pallas_call x1, Pallas kernels, ladder_partials(): pl.pallas_call(ladder_kernel, grid=(items // GROUP,), in_specs=[pl.BlockS...  6.74 us
    pallas_call x1, Pallas kernels, cycle_partials(): pl.pallas_call(cycle_kernel, grid_spec=pltpu.PrefetchScalarGridSpec(num_s...  4.21 us
    ppermute x7, waiting for transfers between devices, shards(): parts.append(lax.ppermute(partials[step], 'occ', ring))  3.96 us
    pallas_call x1, Pallas kernels, gather_tiles(): pl.pallas_call(gather_kernel, in_specs=[pl.BlockSpec(memory_space=pltpu.H...  2.7 us
    pallas_call x1, Pallas kernels, sum_parts(): pl.pallas_call(sum_kernel, in_specs=[pl.BlockSpec(memory_space=pltpu.VMEM...  2.08 us
  transfers between devices with their start and end apart: 9, of which 3 were waited for; matrix products, arithmetic and copies ran while one was open for 1% of the time, Pallas kernels for 8%

profile of v5, /device:TPU:1, one launch (start us, length us, event | category | flops | bytes accessed | tf_op | source)
XLA Modules:
  0.0 83.2 jit_solution(1899238449886119178)
XLA Ops:
  0.6 0.0 copy-start
  0.6 2.7 %outgoing_tiles.1 = bf16[64,2,64,128]{3,2,1,0:T(8,128)(2,1)} custom-call(s32[64]{0:T(128)} %order_hbm.1, s32[2,64]{1,0:T(2,128)} %bitcast.30, bf16[64,64,128]{2,1,0:T(8,128)(2,1)} %bitcast.20), custom_call_target="tpu_custom_call" | custom-call | bytes 4194304 | tf_op jit(solution)/shard_map/outgoing_tiles/pallas_call | solution.py:54
  3.3 0.0 copy-start.1
  3.4 0.0 copy-start.2
  3.4 0.0 copy-start.3
  3.4 0.0 copy-start.4
  3.4 14.6 %all-to-all-start = ((bf16[64,2,64,128]{3,2,1,0:T(8,128)(2,1)}), bf16[64,2,64,128]{3,2,1,0:T(8,128)(2,1)}, u32[]{:S(2)}, u32[]{:S(2)}) async-start(bf16[64,2,64,128]{3,2,1,0:T(8,128)(2,1)} %outgoing_tiles.1), calls=%async_computation | async-start | bytes 4194304 | tf_op jit(solution)/shard_map/all_to_all | solution.py:238
  18.0 4.2 %cycle_partials.1 = (bf16[8,64,128]{2,1,0:T(8,128)(2,1)}, bf16[8,64,128]{2,1,0:T(8,128)(2,1)}, bf16[8,64,128]{2,1,0:T(8,128)(2,1)}, bf16[8,64,128]{2,1,0:T(8,128...) custom-call(s32[1]{0:T(128)} %bitcast.2.me_ref, ...), custom_call_target="tpu_custom_call" | custom-call | flops 268435456 | bytes 4194304 | tf_op jit(solution)/shard_map/cycle_partials/pallas_call | solution.py:98
  22.2 0.0 copy-start.5
  22.2 14.4 %collective-permute-start = (bf16[8,64,128]{2,1,0:T(8,128)(2,1)}, bf16[8,64,128]{2,1,0:T(8,128)(2,1)S(1)}, u32[]{:S(2)}, u32[]{:S(2)}) collective-permute-start(bf16[8,64,128]{2,1,0:T(8,128)(2,1)} %get-tuple-element.22), channel_id=1, source_target_pairs={{0,8},{2,10},{4,12},{6,14},{8,0},{10,2},{12,4},{14,6},{1,9},{3,11}... | collective-permute-start | bytes 393224 | tf_op jit(solution)/shard_map/ppermute | solution.py:246
  36.7 7.6 %collective-permute-start.1 = (bf16[8,64,128]{2,1,0:T(8,128)(2,1)}, bf16[8,64,128]{2,1,0:T(8,128)(2,1)S(1)}, u32[]{:S(2)}, u32[]{:S(2)}) collective-permute-start(bf16[8,64,128]{2,1,0:T(8,128)(2,1)} %get-tuple-element.23), channel_id=1, source_target_pairs={{0,6},{2,8},{4,10},{6,12},{8,14},{10,0},{12,2},{14,4},{1,7},{3,9},... | collective-permute-start | bytes 393224 | tf_op jit(solution)/shard_map/ppermute | solution.py:246
  44.3 1.9 %collective-permute-start.2 = (bf16[8,64,128]{2,1,0:T(8,128)(2,1)}, bf16[8,64,128]{2,1,0:T(8,128)(2,1)S(1)}, u32[]{:S(2)}, u32[]{:S(2)}) collective-permute-start(bf16[8,64,128]{2,1,0:T(8,128)(2,1)} %get-tuple-element.24), channel_id=1, source_target_pairs={{0,10},{2,12},{4,14},{6,0},{8,2},{10,4},{12,6},{14,8},{1,11},{3,13... | collective-permute-start | bytes 393224 | tf_op jit(solution)/shard_map/ppermute | solution.py:246
  46.2 4.6 %collective-permute-start.3 = (bf16[8,64,128]{2,1,0:T(8,128)(2,1)}, bf16[8,64,128]{2,1,0:T(8,128)(2,1)S(1)}, u32[]{:S(2)}, u32[]{:S(2)}) collective-permute-start(bf16[8,64,128]{2,1,0:T(8,128)(2,1)} %get-tuple-element.25), channel_id=1, source_target_pairs={{0,4},{2,6},{4,8},{6,10},{8,12},{10,14},{12,0},{14,2},{1,5},{3,7},... | collective-permute-start | bytes 393224 | tf_op jit(solution)/shard_map/ppermute | solution.py:246
  50.8 2.8 %collective-permute-start.4 = (bf16[8,64,128]{2,1,0:T(8,128)(2,1)}, bf16[8,64,128]{2,1,0:T(8,128)(2,1)S(1)}, u32[]{:S(2)}, u32[]{:S(2)}) collective-permute-start(bf16[8,64,128]{2,1,0:T(8,128)(2,1)} %get-tuple-element.26), channel_id=1, source_target_pairs={{0,12},{2,14},{4,0},{6,2},{8,4},{10,6},{12,8},{14,10},{1,13},{3,15... | collective-permute-start | bytes 393224 | tf_op jit(solution)/shard_map/ppermute | solution.py:246
  53.7 0.2 dynamic-slice_bitcast_fusion
  53.8 0.2 copy.13
  54.0 0.0 collective-permute-done.refs_1_
  54.1 2.7 %collective-permute-start.5 = (bf16[8,64,128]{2,1,0:T(8,128)(2,1)}, bf16[8,64,128]{2,1,0:T(8,128)(2,1)S(1)}, u32[]{:S(2)}, u32[]{:S(2)}) collective-permute-start(bf16[8,64,128]{2,1,0:T(8,128)(2,1)} %get-tuple-element.27), channel_id=1, source_target_pairs={{0,2},{2,4},{4,6},{6,8},{8,10},{10,12},{12,14},{14,0},{1,3},{3,5},... | collective-permute-start | bytes 393224 | tf_op jit(solution)/shard_map/ppermute | solution.py:246
  56.8 3.8 %collective-permute-start.6 = (bf16[8,64,128]{2,1,0:T(8,128)(2,1)}, bf16[8,64,128]{2,1,0:T(8,128)(2,1)S(1)}, u32[]{:S(2)}, u32[]{:S(2)}) collective-permute-start(bf16[8,64,128]{2,1,0:T(8,128)(2,1)} %get-tuple-element.28), channel_id=1, source_target_pairs={{0,14},{2,0},{4,2},{6,4},{8,6},{10,8},{12,10},{14,12},{1,15},{3,1}... | collective-permute-start | bytes 393224 | tf_op jit(solution)/shard_map/ppermute | solution.py:246
  60.6 0.2 constant_dynamic-slice_fusion.1
  60.8 0.1 copy.20
  60.9 0.1 copy.19
  61.1 0.0 collective-permute-done.3.refs_4_
  61.2 0.5 collective-permute-done.4.refs_5_
  61.7 0.0 collective-permute-done.5.refs_6_
  61.7 3.5 %collective-permute-done.6.refs_7_ = bf16[8,64,128]{2,1,0:T(8,128)(2,1)S(1)} collective-permute-done((bf16[8,64,128]{2,1,0:T(8,128)(2,1)}, bf16[8,64,128]{2,1,0:T(8,128)(2,1)S(1)}, u32[]{:S(2)}, u32[]{:S(2)}) %collective-permute-start.6) | collective-permute-done | bytes 131104 | tf_op jit(solution)/shard_map/ppermute | solution.py:246
  65.1 0.6 copy-done.12
  65.8 6.7 %ladder_partials.1 = (bf16[64,64,128]{2,1,0:T(8,128)(2,1)S(1)}, bf16[64,64,128]{2,1,0:T(8,128)(2,1)S(1)}) custom-call(bf16[64,2,64,128]{3,2,1,0:T(8,128)(2,1)} %all-to-all-done.amps_ref, bf16[128,768]{1,0:T(8,128)(2,1)S(1)} %pad_maximum_fusion.left_ref, bf16[2,768,128]{2,1,0:T(8,128)(2,1)S(1)} %bitcast.23), custom_call_target="tpu_custom_call" | custom-call | flops 4294967296 | bytes 6291456 | tf_op jit(solution)/shard_map/ladder_partials/pallas_call | solution.py:154
  72.5 7.3 %collective-permute-start.7 = (bf16[64,64,128]{2,1,0:T(8,128)(2,1)S(1)}, bf16[64,64,128]{2,1,0:T(8,128)(2,1)S(1)}, u32[]{:S(2)}, u32[]{:S(2)}) collective-permute-start(bf16[64,64,128]{2,1,0:T(8,128)(2,1)S(1)} %get-tuple-element.39), channel_id=1, source_target_pairs={{0,1},{1,0},{2,3},{3,2},{4,5},{5,4},{6,7},{7,6},{8,9},{9,8},{10,11... | collective-permute-start | bytes 3145736 | tf_op jit(solution)/shard_map/ppermute | solution.py:259
  79.9 2.1 %sum_parts.1 = bf16[8,64,128]{2,1,0:T(8,128)(2,1)} custom-call(bf16[8,64,128]{2,1,0:T(8,128)(2,1)} %get-tuple-element.29.refs_0_, bf16[8,64,128]{2,1,0:T(8,128)(2,1)} %copy-done.6, bf16[8,64,128]{2,1,0:T(8,128)(2,1)} %copy-done.7, bf16[8,64,128]{2,1,0:T(8,128)(2,1)} %copy-done.8, bf16[8,64,128]{2,1,0:T(8,128)(2,1)} %copy-done.9, ...), custom_call_target="tpu_custom_call" | custom-call | flops 524288 | bytes 1179648 | tf_op jit(solution)/shard_map/sum_parts/pallas_call | solution.py:186
  82.0 0.2 collective-permute-done.7.received_ref
  82.1 1.1 %final_sum.1 = bf16[64,64,128]{2,1,0:T(8,128)(2,1)} custom-call(bf16[64,64,128]{2,1,0:T(8,128)(2,1)S(1)} %get-tuple-element.38.own_ref, bf16[64,64,128]{2,1,0:T(8,128)(2,1)S(1)} %collective-permute-done.7.received_ref), custom_call_target="tpu_custom_call" | custom-call | flops 524288 | bytes 4194304 | tf_op jit(solution)/shard_map/final_sum/pallas_call | solution.py:212
  (24 shorter events, 0.1 us)
Async XLA Ops:
  0.6 53.0 %copy-start = (bf16[6,1,2,128,128]{4,3,2,1,0:T(8,128)(2,1)S(1)}, bf16[6,1,2,128,128]{4,3,2,1,0:T(8,128)(2,1)}, u32[]{:S(2)}) copy-start(bf16[6,1,2,128,128]{4,3,2,1,0:T(8,128)(2,1)} %param.14) | copy-start | bytes 1179652
  3.3 14.6 %copy-start.1 = (bf16[1,1,64,64,128]{4,3,2,1,0:T(8,128)(2,1)S(1)}, bf16[1,1,64,64,128]{4,3,2,1,0:T(8,128)(2,1)}, u32[]{:S(2)}) copy-start(bf16[1,1,64,64,128]{4,3,2,1,0:T(8,128)(2,1)} %param.8) | copy-start | bytes 3145732
  3.4 14.6 %copy-start.2 = (bf16[1,1,64,128,128]{4,3,2,1,0:T(8,128)(2,1)S(1)}, bf16[1,1,64,128,128]{4,3,2,1,0:T(8,128)(2,1)}, u32[]{:S(2)}) copy-start(bf16[1,1,64,128,128]{4,3,2,1,0:T(8,128)(2,1)} %param.9) | copy-start | bytes 6291460
  3.4 14.6 %copy-start.3 = (s32[64,2]{0,1:T(2,128)S(1)}, s32[64,2]{0,1:T(2,128)}, u32[]{:S(2)}) copy-start(s32[64,2]{0,1:T(2,128)} %param.10) | copy-start | bytes 1540
  3.4 14.6 %copy-start.4 = (s32[64,2]{0,1:T(2,128)S(1)}, s32[64,2]{0,1:T(2,128)}, u32[]{:S(2)}) copy-start(s32[64,2]{0,1:T(2,128)} %param.11) | copy-start | bytes 1540
  3.4 61.7 %all-to-all-start = ((bf16[64,2,64,128]{3,2,1,0:T(8,128)(2,1)}), bf16[64,2,64,128]{3,2,1,0:T(8,128)(2,1)}, u32[]{:S(2)}, u32[]{:S(2)}) async-start(bf16[64,2,64,128]{3,2,1,0:T(8,128)(2,1)} %outgoing_tiles.1), calls=%async_computation | async-start | bytes 4194304 | tf_op jit(solution)/shard_map/all_to_all | solution.py:238
  22.2 38.8 %copy-start.5 = (bf16[6,1,2,128,128]{4,3,2,1,0:T(8,128)(2,1)S(1)}, bf16[6,1,2,128,128]{4,3,2,1,0:T(8,128)(2,1)}, u32[]{:S(2)}) copy-start(bf16[6,1,2,128,128]{4,3,2,1,0:T(8,128)(2,1)} %param.15) | copy-start | bytes 1179652
  22.2 31.8 %collective-permute-start = (bf16[8,64,128]{2,1,0:T(8,128)(2,1)}, bf16[8,64,128]{2,1,0:T(8,128)(2,1)S(1)}, u32[]{:S(2)}, u32[]{:S(2)}) collective-permute-start(bf16[8,64,128]{2,1,0:T(8,128)(2,1)} %get-tuple-element.22), channel_id=1, source_target_pairs={{0,8},{2,10},{4,12},{6,14},{8,0},{10,2},{12,4},{14,6},{1,9},{3,11}... | collective-permute-start | bytes 393224 | tf_op jit(solution)/shard_map/ppermute | solution.py:246
  36.7 20.1 %collective-permute-start.1 = (bf16[8,64,128]{2,1,0:T(8,128)(2,1)}, bf16[8,64,128]{2,1,0:T(8,128)(2,1)S(1)}, u32[]{:S(2)}, u32[]{:S(2)}) collective-permute-start(bf16[8,64,128]{2,1,0:T(8,128)(2,1)} %get-tuple-element.23), channel_id=1, source_target_pairs={{0,6},{2,8},{4,10},{6,12},{8,14},{10,0},{12,2},{14,4},{1,7},{3,9},... | collective-permute-start | bytes 393224 | tf_op jit(solution)/shard_map/ppermute | solution.py:246
  44.3 16.8 %collective-permute-start.2 = (bf16[8,64,128]{2,1,0:T(8,128)(2,1)}, bf16[8,64,128]{2,1,0:T(8,128)(2,1)S(1)}, u32[]{:S(2)}, u32[]{:S(2)}) collective-permute-start(bf16[8,64,128]{2,1,0:T(8,128)(2,1)} %get-tuple-element.24), channel_id=1, source_target_pairs={{0,10},{2,12},{4,14},{6,0},{8,2},{10,4},{12,6},{14,8},{1,11},{3,13... | collective-permute-start | bytes 393224 | tf_op jit(solution)/shard_map/ppermute | solution.py:246
  46.2 14.9 %collective-permute-start.3 = (bf16[8,64,128]{2,1,0:T(8,128)(2,1)}, bf16[8,64,128]{2,1,0:T(8,128)(2,1)S(1)}, u32[]{:S(2)}, u32[]{:S(2)}) collective-permute-start(bf16[8,64,128]{2,1,0:T(8,128)(2,1)} %get-tuple-element.25), channel_id=1, source_target_pairs={{0,4},{2,6},{4,8},{6,10},{8,12},{10,14},{12,0},{14,2},{1,5},{3,7},... | collective-permute-start | bytes 393224 | tf_op jit(solution)/shard_map/ppermute | solution.py:246
  50.8 10.8 %collective-permute-start.4 = (bf16[8,64,128]{2,1,0:T(8,128)(2,1)}, bf16[8,64,128]{2,1,0:T(8,128)(2,1)S(1)}, u32[]{:S(2)}, u32[]{:S(2)}) collective-permute-start(bf16[8,64,128]{2,1,0:T(8,128)(2,1)} %get-tuple-element.26), channel_id=1, source_target_pairs={{0,12},{2,14},{4,0},{6,2},{8,4},{10,6},{12,8},{14,10},{1,13},{3,15... | collective-permute-start | bytes 393224 | tf_op jit(solution)/shard_map/ppermute | solution.py:246
  54.0 7.0 %copy-start.6 = (bf16[8,64,128]{2,1,0:T(8,128)(2,1)}, bf16[8,64,128]{2,1,0:T(8,128)(2,1)S(1)}, u32[]{:S(2)}) copy-start(bf16[8,64,128]{2,1,0:T(8,128)(2,1)S(1)} %collective-permute-done.refs_1_) | copy-start | bytes 393220
  54.1 7.6 %collective-permute-start.5 = (bf16[8,64,128]{2,1,0:T(8,128)(2,1)}, bf16[8,64,128]{2,1,0:T(8,128)(2,1)S(1)}, u32[]{:S(2)}, u32[]{:S(2)}) collective-permute-start(bf16[8,64,128]{2,1,0:T(8,128)(2,1)} %get-tuple-element.27), channel_id=1, source_target_pairs={{0,2},{2,4},{4,6},{6,8},{8,10},{10,12},{12,14},{14,0},{1,3},{3,5},... | collective-permute-start | bytes 393224 | tf_op jit(solution)/shard_map/ppermute | solution.py:246
  56.8 4.2 %copy-start.7 = (bf16[8,64,128]{2,1,0:T(8,128)(2,1)}, bf16[8,64,128]{2,1,0:T(8,128)(2,1)S(1)}, u32[]{:S(2)}) copy-start(bf16[8,64,128]{2,1,0:T(8,128)(2,1)S(1)} %collective-permute-done.1.refs_2_) | copy-start | bytes 393220
  56.8 8.3 %collective-permute-start.6 = (bf16[8,64,128]{2,1,0:T(8,128)(2,1)}, bf16[8,64,128]{2,1,0:T(8,128)(2,1)S(1)}, u32[]{:S(2)}, u32[]{:S(2)}) collective-permute-start(bf16[8,64,128]{2,1,0:T(8,128)(2,1)} %get-tuple-element.28), channel_id=1, source_target_pairs={{0,14},{2,0},{4,2},{6,4},{8,6},{10,8},{12,10},{14,12},{1,15},{3,1}... | collective-permute-start | bytes 393224 | tf_op jit(solution)/shard_map/ppermute | solution.py:246
  61.1 11.4 %copy-start.8 = (bf16[8,64,128]{2,1,0:T(8,128)(2,1)}, bf16[8,64,128]{2,1,0:T(8,128)(2,1)S(1)}, u32[]{:S(2)}) copy-start(bf16[8,64,128]{2,1,0:T(8,128)(2,1)S(1)} %collective-permute-done.2.refs_3_) | copy-start | bytes 393220
  61.2 11.4 %copy-start.9 = (bf16[8,64,128]{2,1,0:T(8,128)(2,1)}, bf16[8,64,128]{2,1,0:T(8,128)(2,1)S(1)}, u32[]{:S(2)}) copy-start(bf16[8,64,128]{2,1,0:T(8,128)(2,1)S(1)} %collective-permute-done.3.refs_4_) | copy-start | bytes 393220
  61.7 10.9 %copy-start.10 = (bf16[8,64,128]{2,1,0:T(8,128)(2,1)}, bf16[8,64,128]{2,1,0:T(8,128)(2,1)S(1)}, u32[]{:S(2)}) copy-start(bf16[8,64,128]{2,1,0:T(8,128)(2,1)S(1)} %collective-permute-done.4.refs_5_) | copy-start | bytes 393220
  61.7 3.5 %copy-start.11 = (bf16[8,64,128]{2,1,0:T(8,128)(2,1)}, bf16[8,64,128]{2,1,0:T(8,128)(2,1)S(1)}, u32[]{:S(2)}) copy-start(bf16[8,64,128]{2,1,0:T(8,128)(2,1)S(1)} %collective-permute-done.5.refs_6_) | copy-start | bytes 393220
  65.1 0.7 copy-start.12
  72.5 9.6 %collective-permute-start.7 = (bf16[64,64,128]{2,1,0:T(8,128)(2,1)S(1)}, bf16[64,64,128]{2,1,0:T(8,128)(2,1)S(1)}, u32[]{:S(2)}, u32[]{:S(2)}) collective-permute-start(bf16[64,64,128]{2,1,0:T(8,128)(2,1)S(1)} %get-tuple-element.39), channel_id=1, source_target_pairs={{0,1},{1,0},{2,3},{3,2},{4,5},{5,4},{6,7},{7,6},{8,9},{9,8},{10,11... | collective-permute-start | bytes 3145736 | tf_op jit(solution)/shard_map/ppermute | solution.py:259

commit v6 on v3

--- a/solution.py
+++ b/solution.py
@@ -1,3 +1,5 @@
+import functools
+
 import jax
 import jax.numpy as jnp
 from jax import lax
@@ -114,7 +116,7 @@
     )(me, src, wsel, amps, ints)
 
 
-def ladder_kernel(amps_ref, left_ref, right_ref, own_ref, other_ref):
+def ladder_kernel(amps_ref, left_ref, right_ref, own_ref, early_ref, late_ref, other_ref):
     group, terms, rows, width = amps_ref.shape
     vectors = right_ref.shape[1] // width
     half = own_ref.shape[1]
@@ -144,8 +146,17 @@
             summed = jnp.dot(left, jnp.concatenate(columns, axis=1), preferred_element_type=jnp.float32)
             for place in range(2):
                 tile = summed[:, place * width : (place + 1) * width]
-                own_ref[start + first + place] = tile[:half]
+                own_ref[start + first + place] = tile[:half].astype(own_ref.dtype)
                 other_ref[start + first + place] = tile[half:].astype(other_ref.dtype)
+    last = pl.num_programs(0) - 1
+
+    @pl.when(pl.program_id(0) < last)
+    def _():
+        early_ref[...] = other_ref[...]
+
+    @pl.when(pl.program_id(0) == last)
+    def _():
+        late_ref[...] = other_ref[...]
 
 
 def ladder_partials(amps, left, right):
@@ -161,12 +172,15 @@
         ],
         out_specs=[
             pl.BlockSpec((GROUP, half, width), lambda g: (g, 0, 0)),
-            pl.BlockSpec((GROUP, half, width), lambda g: (g, 0, 0)),
+            pl.BlockSpec((GROUP, half, width), lambda g: (jnp.minimum(g, items // GROUP - 2), 0, 0)),
+            pl.BlockSpec((GROUP, half, width), lambda g: (0, 0, 0)),
         ],
         out_shape=[
-            jax.ShapeDtypeStruct((items, half, width), jnp.float32),
             jax.ShapeDtypeStruct((items, half, width), jnp.bfloat16),
-        ],
+            jax.ShapeDtypeStruct((items - GROUP, half, width), jnp.bfloat16),
+            jax.ShapeDtypeStruct((GROUP, half, width), jnp.bfloat16),
+        ],
+        scratch_shapes=[pltpu.VMEM((GROUP, half, width), jnp.bfloat16)],
         compiler_params=pltpu.CompilerParams(vmem_limit_bytes=12 << 20),
         cost_estimate=pl.CostEstimate(flops=32 << 27, bytes_accessed=6 << 20, transcendentals=0),
         name="ladder_partials",
@@ -191,6 +205,36 @@
         cost_estimate=pl.CostEstimate(flops=8 * size, bytes_accessed=18 * size, transcendentals=0),
         name="sum_parts",
     )(*parts)
+
+
+def final_kernel(first, pieces, own_ref, received_ref, *refs):
+    out_hbm, out_ref, sems = refs[-3:]
+    share = received_ref.shape[0] // pieces
+    stores = []
+    for part in range(pieces):
+        block = pl.ds(part * share, share)
+        place = pl.ds(first + part * share, share)
+        total = own_ref[place].astype(jnp.float32) + received_ref[block].astype(jnp.float32)
+        out_ref[block] = total.astype(out_ref.dtype)
+        stores.append(pltpu.make_async_copy(out_ref.at[block], out_hbm.at[place], sems.at[part]))
+        stores[-1].start()
+    for store in stores:
+        store.wait()
+
+
+def final_sum(first, pieces, own, received, *earlier):
+    vmem, hbm = pl.BlockSpec(memory_space=pltpu.VMEM), pl.BlockSpec(memory_space=pltpu.HBM)
+    return pl.pallas_call(
+        functools.partial(final_kernel, first, pieces),
+        in_specs=[vmem, vmem] + [hbm] * len(earlier),
+        out_specs=hbm,
+        out_shape=pltpu.HBM(own.shape, received.dtype),
+        scratch_shapes=[pltpu.VMEM(received.shape, received.dtype), pltpu.SemaphoreType.DMA((pieces,))],
+        input_output_aliases={2: 0} if earlier else {},
+        compiler_params=pltpu.CompilerParams(vmem_limit_bytes=8 << 20),
+        cost_estimate=pl.CostEstimate(flops=received.size, bytes_accessed=6 * received.size, transcendentals=0),
+        name="final_sum",
+    )(own, received, *earlier)
 
 
 def shards(
@@ -216,8 +260,9 @@
     for step in SENDS:
         ring = [(k, (k + step) % holders) for k in range(holders)]
         parts.append(lax.ppermute(partials[step], "occ", ring))
-    arriving, *parts = lax.optimization_barrier((arriving, *parts))
-    cycle_part = sum_parts(parts)[None, None]
+    cycle_part = sum_parts(parts)
+    arriving, cycle_part = lax.optimization_barrier((arriving, cycle_part))
+    cycle_part = cycle_part[None, None]
 
     replica = lax.axis_index("rep")
     left = lax.dynamic_slice_in_dim(first_integral_blocks[:, 0], replica * row_count, row_count, 3)
@@ -227,9 +272,12 @@
     left = jnp.concatenate([own_rows, other_rows], axis=0)
     right = jnp.transpose(right_ints[:, 0], (1, 0, 2, 3)).reshape(right_ints.shape[2], -1, width)
 
-    own, other = ladder_partials(arriving, left, right)
-    received = lax.ppermute(other, "rep", [(0, 1), (1, 0)])
-    ladder_part = (own + received.astype(jnp.float32)).astype(jnp.bfloat16)[:, None, None]
+    own, early, late = ladder_partials(arriving, left, right)
+    swap = [(0, 1), (1, 0)]
+    early = lax.ppermute(early, "rep", swap)
+    late = lax.ppermute(late, "rep", swap)
+    ladder_part = final_sum(0, 3, own, early)
+    ladder_part = final_sum(early.shape[0], 2, own, late, ladder_part)[:, None, None]
     return (cycle_part, ladder_part)
 
 

time: 86.3 us -> 84.6 us (0.980)
  other arithmetic: 2.54 us -> 0.02 us
  Pallas kernels: 16.4 us -> 17.5 us
    unnamed x1 -> x0, other arithmetic: 2.53 us -> none
    pallas_call x0 -> x2, Pallas kernels: none -> 1.71 us  [final_sum(): pl.pallas_call(functools.partial(final_kernel, first, pieces), in_specs=[...]
    ppermute x1 -> x2, starting transfers between devices: 7.37 us -> 7.17 us  [the longest x1 5.25 us: shards(): early = lax.ppermute(early, 'rep', swap)]
  transfers between devices with their start and end apart: 9 -> 10, of which waited for: 3 -> 3; matrix products, arithmetic and copies ran while one was open for 1% -> 1% of each run, Pallas kernels for 7% -> 9%
where the time goes in v6:
time: 84.6 us; the launch traced here: 84.1 us
  starting transfers between devices  59.6 us (70%)
  Pallas kernels  17.5 us (21%)
  waiting for transfers between devices  4.49 us (5%)
  local copies, waits for them, and re-layouts  1.5 us (2%)
  between operations  0.99 us (1%)
    ppermute x7, starting transfers between devices, shards(): parts.append(lax.ppermute(partials[step], 'occ', ring))  37.9 us
    all_to_all x1, starting transfers between devices, shards(): lax.all_to_all(outgoing, 'vir', split_axis=0, concat_axis=0, tiled=True)  14.6 us
    pallas_call x1, Pallas kernels, ladder_partials(): pl.pallas_call(ladder_kernel, grid=(items // GROUP,), in_specs=[pl.BlockS...  6.79 us
    ppermute x1, starting transfers between devices, shards(): early = lax.ppermute(early, 'rep', swap)  5.25 us
    pallas_call x1, Pallas kernels, cycle_partials(): pl.pallas_call(cycle_kernel, grid_spec=pltpu.PrefetchScalarGridSpec(num_s...  4.21 us
    ppermute x7, waiting for transfers between devices, shards(): parts.append(lax.ppermute(partials[step], 'occ', ring))  3.97 us
    pallas_call x1, Pallas kernels, gather_tiles(): pl.pallas_call(gather_kernel, in_specs=[pl.BlockSpec(memory_space=pltpu.H...  2.69 us
    pallas_call x1, Pallas kernels, sum_parts(): pl.pallas_call(sum_kernel, in_specs=[pl.BlockSpec(memory_space=pltpu.VMEM...  2.07 us
  transfers between devices with their start and end apart: 10, of which 3 were waited for; matrix products, arithmetic and copies ran while one was open for 1% of the time, Pallas kernels for 9%

profile of v6, /device:TPU:1, one launch (start us, length us, event | category | flops | bytes accessed | tf_op | source)
XLA Modules:
  0.0 84.1 jit_solution(992435267223559903)
XLA Ops:
  0.6 0.0 copy-start
  0.6 2.7 %outgoing_tiles.1 = bf16[64,2,64,128]{3,2,1,0:T(8,128)(2,1)} custom-call(s32[64]{0:T(128)} %order_hbm.1, s32[2,64]{1,0:T(2,128)} %bitcast.30, bf16[64,64,128]{2,1,0:T(8,128)(2,1)} %bitcast.20), custom_call_target="tpu_custom_call" | custom-call | bytes 4194304 | tf_op jit(solution)/shard_map/outgoing_tiles/pallas_call | solution.py:56
  3.3 0.0 copy-start.1
  3.4 0.0 copy-start.2
  3.4 0.0 copy-start.3
  3.4 0.0 copy-start.4
  3.4 14.6 %all-to-all-start = ((bf16[64,2,64,128]{3,2,1,0:T(8,128)(2,1)}), bf16[64,2,64,128]{3,2,1,0:T(8,128)(2,1)}, u32[]{:S(2)}, u32[]{:S(2)}) async-start(bf16[64,2,64,128]{3,2,1,0:T(8,128)(2,1)} %outgoing_tiles.1), calls=%async_computation | async-start | bytes 4194304 | tf_op jit(solution)/shard_map/all_to_all | solution.py:254
  18.0 4.2 %cycle_partials.1 = (bf16[8,64,128]{2,1,0:T(8,128)(2,1)}, bf16[8,64,128]{2,1,0:T(8,128)(2,1)}, bf16[8,64,128]{2,1,0:T(8,128)(2,1)}, bf16[8,64,128]{2,1,0:T(8,128...) custom-call(s32[1]{0:T(128)} %bitcast.2.me_ref, ...), custom_call_target="tpu_custom_call" | custom-call | flops 268435456 | bytes 4194304 | tf_op jit(solution)/shard_map/cycle_partials/pallas_call | solution.py:100
  22.2 0.0 copy-start.5
  22.2 14.4 %collective-permute-start = (bf16[8,64,128]{2,1,0:T(8,128)(2,1)}, bf16[8,64,128]{2,1,0:T(8,128)(2,1)S(1)}, u32[]{:S(2)}, u32[]{:S(2)}) collective-permute-start(bf16[8,64,128]{2,1,0:T(8,128)(2,1)} %get-tuple-element.16), channel_id=1, source_target_pairs={{0,8},{2,10},{4,12},{6,14},{8,0},{10,2},{12,4},{14,6},{1,9},{3,11}... | collective-permute-start | bytes 393224 | tf_op jit(solution)/shard_map/ppermute | solution.py:262
  36.7 7.6 %collective-permute-start.1 = (bf16[8,64,128]{2,1,0:T(8,128)(2,1)}, bf16[8,64,128]{2,1,0:T(8,128)(2,1)S(1)}, u32[]{:S(2)}, u32[]{:S(2)}) collective-permute-start(bf16[8,64,128]{2,1,0:T(8,128)(2,1)} %get-tuple-element.17), channel_id=1, source_target_pairs={{0,6},{2,8},{4,10},{6,12},{8,14},{10,0},{12,2},{14,4},{1,7},{3,9},... | collective-permute-start | bytes 393224 | tf_op jit(solution)/shard_map/ppermute | solution.py:262
  44.3 1.9 %collective-permute-start.2 = (bf16[8,64,128]{2,1,0:T(8,128)(2,1)}, bf16[8,64,128]{2,1,0:T(8,128)(2,1)S(1)}, u32[]{:S(2)}, u32[]{:S(2)}) collective-permute-start(bf16[8,64,128]{2,1,0:T(8,128)(2,1)} %get-tuple-element.18), channel_id=1, source_target_pairs={{0,10},{2,12},{4,14},{6,0},{8,2},{10,4},{12,6},{14,8},{1,11},{3,13... | collective-permute-start | bytes 393224 | tf_op jit(solution)/shard_map/ppermute | solution.py:262
  46.2 4.6 %collective-permute-start.3 = (bf16[8,64,128]{2,1,0:T(8,128)(2,1)}, bf16[8,64,128]{2,1,0:T(8,128)(2,1)S(1)}, u32[]{:S(2)}, u32[]{:S(2)}) collective-permute-start(bf16[8,64,128]{2,1,0:T(8,128)(2,1)} %get-tuple-element.19), channel_id=1, source_target_pairs={{0,4},{2,6},{4,8},{6,10},{8,12},{10,14},{12,0},{14,2},{1,5},{3,7},... | collective-permute-start | bytes 393224 | tf_op jit(solution)/shard_map/ppermute | solution.py:262
  50.8 2.8 %collective-permute-start.4 = (bf16[8,64,128]{2,1,0:T(8,128)(2,1)}, bf16[8,64,128]{2,1,0:T(8,128)(2,1)S(1)}, u32[]{:S(2)}, u32[]{:S(2)}) collective-permute-start(bf16[8,64,128]{2,1,0:T(8,128)(2,1)} %get-tuple-element.20), channel_id=1, source_target_pairs={{0,12},{2,14},{4,0},{6,2},{8,4},{10,6},{12,8},{14,10},{1,13},{3,15... | collective-permute-start | bytes 393224 | tf_op jit(solution)/shard_map/ppermute | solution.py:262
  53.7 0.2 dynamic-slice_bitcast_fusion
  53.8 0.2 copy.14
  54.0 0.0 collective-permute-done.refs_1_
  54.0 2.7 %collective-permute-start.5 = (bf16[8,64,128]{2,1,0:T(8,128)(2,1)}, bf16[8,64,128]{2,1,0:T(8,128)(2,1)S(1)}, u32[]{:S(2)}, u32[]{:S(2)}) collective-permute-start(bf16[8,64,128]{2,1,0:T(8,128)(2,1)} %get-tuple-element.21), channel_id=1, source_target_pairs={{0,2},{2,4},{4,6},{6,8},{8,10},{10,12},{12,14},{14,0},{1,3},{3,5},... | collective-permute-start | bytes 393224 | tf_op jit(solution)/shard_map/ppermute | solution.py:262
  56.8 3.8 %collective-permute-start.6 = (bf16[8,64,128]{2,1,0:T(8,128)(2,1)}, bf16[8,64,128]{2,1,0:T(8,128)(2,1)S(1)}, u32[]{:S(2)}, u32[]{:S(2)}) collective-permute-start(bf16[8,64,128]{2,1,0:T(8,128)(2,1)} %get-tuple-element.22), channel_id=1, source_target_pairs={{0,14},{2,0},{4,2},{6,4},{8,6},{10,8},{12,10},{14,12},{1,15},{3,1}... | collective-permute-start | bytes 393224 | tf_op jit(solution)/shard_map/ppermute | solution.py:262
  60.6 0.2 constant_dynamic-slice_fusion.1
  60.8 0.1 copy.21
  60.9 0.1 copy.20
  61.1 0.5 collective-permute-done.4.refs_5_
  61.6 3.5 %collective-permute-done.6.refs_7_ = bf16[8,64,128]{2,1,0:T(8,128)(2,1)S(1)} collective-permute-done((bf16[8,64,128]{2,1,0:T(8,128)(2,1)}, bf16[8,64,128]{2,1,0:T(8,128)(2,1)S(1)}, u32[]{:S(2)}, u32[]{:S(2)}) %collective-permute-start.6) | collective-permute-done | bytes 131104 | tf_op jit(solution)/shard_map/ppermute | solution.py:262
  65.1 0.6 copy-done.12
  65.8 2.1 %sum_parts.1 = bf16[8,64,128]{2,1,0:T(8,128)(2,1)} custom-call(bf16[8,64,128]{2,1,0:T(8,128)(2,1)} %get-tuple-element.15.refs_0_, bf16[8,64,128]{2,1,0:T(8,128)(2,1)} %copy-done.6, bf16[8,64,128]{2,1,0:T(8,128)(2,1)} %copy-done.7, bf16[8,64,128]{2,1,0:T(8,128)(2,1)} %copy-done.8, bf16[8,64,128]{2,1,0:T(8,128)(2,1)} %copy-done.9, ...), custom_call_target="tpu_custom_call" | custom-call | flops 524288 | bytes 1179648 | tf_op jit(solution)/shard_map/sum_parts/pallas_call | solution.py:200
  67.8 6.8 %ladder_partials.1 = (bf16[64,64,128]{2,1,0:T(8,128)(2,1)S(1)}, bf16[48,64,128]{2,1,0:T(8,128)(2,1)S(1)}, bf16[16,64,128]{2,1,0:T(8,128)(2,1)S(1)}) custom-call(bf16[64,2,64,128]{3,2,1,0:T(8,128)(2,1)} %all-to-all-done.amps_ref, bf16[128,768]{1,0:T(8,128)(2,1)S(1)} %pad_maximum_fusion.left_ref, bf16[2,768,128]{2,1,0:T(8,128)(2,1)S(1)} %bitcast.23), custom_call_target="tpu_custom_call" | custom-call | flops 4294967296 | bytes 6291456 | tf_op jit(solution)/shard_map/ladder_partials/pallas_call | solution.py:165
  74.6 5.3 %collective-permute-start.8 = (bf16[48,64,128]{2,1,0:T(8,128)(2,1)S(1)}, bf16[48,64,128]{2,1,0:T(8,128)(2,1)S(1)}, u32[]{:S(2)}, u32[]{:S(2)}) collective-permute-start(bf16[48,64,128]{2,1,0:T(8,128)(2,1)S(1)} %get-tuple-element.27), channel_id=1, source_target_pairs={{0,1},{1,0},{2,3},{3,2},{4,5},{5,4},{6,7},{7,6},{8,9},{9,8},{10,11... | collective-permute-start | bytes 2359304 | tf_op jit(solution)/shard_map/ppermute | solution.py:277
  79.9 1.9 %collective-permute-start.7 = (bf16[16,64,128]{2,1,0:T(8,128)(2,1)S(1)}, bf16[16,64,128]{2,1,0:T(8,128)(2,1)S(1)}, u32[]{:S(2)}, u32[]{:S(2)}) collective-permute-start(bf16[16,64,128]{2,1,0:T(8,128)(2,1)S(1)} %get-tuple-element.26), channel_id=1, source_target_pairs={{0,1},{1,0},{2,3},{3,2},{4,5},{5,4},{6,7},{7,6},{8,9},{9,8},{10,11... | collective-permute-start | bytes 786440 | tf_op jit(solution)/shard_map/ppermute | solution.py:278
  81.8 1.0 %final_sum.2.refs_0_ = bf16[64,64,128]{2,1,0:T(8,128)(2,1)} custom-call(bf16[64,64,128]{2,1,0:T(8,128)(2,1)S(1)} %get-tuple-element.25.own_ref, bf16[48,64,128]{2,1,0:T(8,128)(2,1)S(1)} %collective-permute-done.8.received_ref), custom_call_target="tpu_custom_call" | custom-call | flops 393216 | bytes 2359296 | tf_op jit(solution)/shard_map/final_sum/pallas_call | solution.py:227
  82.8 0.5 collective-permute-done.7.received_ref
  83.3 0.7 final_sum.3
  (27 shorter events, 0.1 us)
Async XLA Ops:
  0.6 53.0 %copy-start = (bf16[6,1,2,128,128]{4,3,2,1,0:T(8,128)(2,1)S(1)}, bf16[6,1,2,128,128]{4,3,2,1,0:T(8,128)(2,1)}, u32[]{:S(2)}) copy-start(bf16[6,1,2,128,128]{4,3,2,1,0:T(8,128)(2,1)} %param.14) | copy-start | bytes 1179652
  3.3 14.6 %copy-start.1 = (bf16[1,1,64,64,128]{4,3,2,1,0:T(8,128)(2,1)S(1)}, bf16[1,1,64,64,128]{4,3,2,1,0:T(8,128)(2,1)}, u32[]{:S(2)}) copy-start(bf16[1,1,64,64,128]{4,3,2,1,0:T(8,128)(2,1)} %param.8) | copy-start | bytes 3145732
  3.4 14.6 %copy-start.2 = (bf16[1,1,64,128,128]{4,3,2,1,0:T(8,128)(2,1)S(1)}, bf16[1,1,64,128,128]{4,3,2,1,0:T(8,128)(2,1)}, u32[]{:S(2)}) copy-start(bf16[1,1,64,128,128]{4,3,2,1,0:T(8,128)(2,1)} %param.9) | copy-start | bytes 6291460
  3.4 14.6 %copy-start.3 = (s32[64,2]{0,1:T(2,128)S(1)}, s32[64,2]{0,1:T(2,128)}, u32[]{:S(2)}) copy-start(s32[64,2]{0,1:T(2,128)} %param.10) | copy-start | bytes 1540
  3.4 14.6 %copy-start.4 = (s32[64,2]{0,1:T(2,128)S(1)}, s32[64,2]{0,1:T(2,128)}, u32[]{:S(2)}) copy-start(s32[64,2]{0,1:T(2,128)} %param.11) | copy-start | bytes 1540
  3.4 64.4 %all-to-all-start = ((bf16[64,2,64,128]{3,2,1,0:T(8,128)(2,1)}), bf16[64,2,64,128]{3,2,1,0:T(8,128)(2,1)}, u32[]{:S(2)}, u32[]{:S(2)}) async-start(bf16[64,2,64,128]{3,2,1,0:T(8,128)(2,1)} %outgoing_tiles.1), calls=%async_computation | async-start | bytes 4194304 | tf_op jit(solution)/shard_map/all_to_all | solution.py:254
  22.2 38.8 %copy-start.5 = (bf16[6,1,2,128,128]{4,3,2,1,0:T(8,128)(2,1)S(1)}, bf16[6,1,2,128,128]{4,3,2,1,0:T(8,128)(2,1)}, u32[]{:S(2)}) copy-start(bf16[6,1,2,128,128]{4,3,2,1,0:T(8,128)(2,1)} %param.15) | copy-start | bytes 1179652
  22.2 31.8 %collective-permute-start = (bf16[8,64,128]{2,1,0:T(8,128)(2,1)}, bf16[8,64,128]{2,1,0:T(8,128)(2,1)S(1)}, u32[]{:S(2)}, u32[]{:S(2)}) collective-permute-start(bf16[8,64,128]{2,1,0:T(8,128)(2,1)} %get-tuple-element.16), channel_id=1, source_target_pairs={{0,8},{2,10},{4,12},{6,14},{8,0},{10,2},{12,4},{14,6},{1,9},{3,11}... | collective-permute-start | bytes 393224 | tf_op jit(solution)/shard_map/ppermute | solution.py:262
  36.7 20.1 %collective-permute-start.1 = (bf16[8,64,128]{2,1,0:T(8,128)(2,1)}, bf16[8,64,128]{2,1,0:T(8,128)(2,1)S(1)}, u32[]{:S(2)}, u32[]{:S(2)}) collective-permute-start(bf16[8,64,128]{2,1,0:T(8,128)(2,1)} %get-tuple-element.17), channel_id=1, source_target_pairs={{0,6},{2,8},{4,10},{6,12},{8,14},{10,0},{12,2},{14,4},{1,7},{3,9},... | collective-permute-start | bytes 393224 | tf_op jit(solution)/shard_map/ppermute | solution.py:262
  44.3 16.8 %collective-permute-start.2 = (bf16[8,64,128]{2,1,0:T(8,128)(2,1)}, bf16[8,64,128]{2,1,0:T(8,128)(2,1)S(1)}, u32[]{:S(2)}, u32[]{:S(2)}) collective-permute-start(bf16[8,64,128]{2,1,0:T(8,128)(2,1)} %get-tuple-element.18), channel_id=1, source_target_pairs={{0,10},{2,12},{4,14},{6,0},{8,2},{10,4},{12,6},{14,8},{1,11},{3,13... | collective-permute-start | bytes 393224 | tf_op jit(solution)/shard_map/ppermute | solution.py:262
  46.2 14.9 %collective-permute-start.3 = (bf16[8,64,128]{2,1,0:T(8,128)(2,1)}, bf16[8,64,128]{2,1,0:T(8,128)(2,1)S(1)}, u32[]{:S(2)}, u32[]{:S(2)}) collective-permute-start(bf16[8,64,128]{2,1,0:T(8,128)(2,1)} %get-tuple-element.19), channel_id=1, source_target_pairs={{0,4},{2,6},{4,8},{6,10},{8,12},{10,14},{12,0},{14,2},{1,5},{3,7},... | collective-permute-start | bytes 393224 | tf_op jit(solution)/shard_map/ppermute | solution.py:262
  50.8 10.8 %collective-permute-start.4 = (bf16[8,64,128]{2,1,0:T(8,128)(2,1)}, bf16[8,64,128]{2,1,0:T(8,128)(2,1)S(1)}, u32[]{:S(2)}, u32[]{:S(2)}) collective-permute-start(bf16[8,64,128]{2,1,0:T(8,128)(2,1)} %get-tuple-element.20), channel_id=1, source_target_pairs={{0,12},{2,14},{4,0},{6,2},{8,4},{10,6},{12,8},{14,10},{1,13},{3,15... | collective-permute-start | bytes 393224 | tf_op jit(solution)/shard_map/ppermute | solution.py:262
  54.0 11.1 %copy-start.6 = (bf16[8,64,128]{2,1,0:T(8,128)(2,1)}, bf16[8,64,128]{2,1,0:T(8,128)(2,1)S(1)}, u32[]{:S(2)}) copy-start(bf16[8,64,128]{2,1,0:T(8,128)(2,1)S(1)} %collective-permute-done.refs_1_) | copy-start | bytes 393220
  54.0 7.6 %collective-permute-start.5 = (bf16[8,64,128]{2,1,0:T(8,128)(2,1)}, bf16[8,64,128]{2,1,0:T(8,128)(2,1)S(1)}, u32[]{:S(2)}, u32[]{:S(2)}) collective-permute-start(bf16[8,64,128]{2,1,0:T(8,128)(2,1)} %get-tuple-element.21), channel_id=1, source_target_pairs={{0,2},{2,4},{4,6},{6,8},{8,10},{10,12},{12,14},{14,0},{1,3},{3,5},... | collective-permute-start | bytes 393224 | tf_op jit(solution)/shard_map/ppermute | solution.py:262
  56.8 8.3 %copy-start.7 = (bf16[8,64,128]{2,1,0:T(8,128)(2,1)}, bf16[8,64,128]{2,1,0:T(8,128)(2,1)S(1)}, u32[]{:S(2)}) copy-start(bf16[8,64,128]{2,1,0:T(8,128)(2,1)S(1)} %collective-permute-done.1.refs_2_) | copy-start | bytes 393220
  56.8 8.3 %collective-permute-start.6 = (bf16[8,64,128]{2,1,0:T(8,128)(2,1)}, bf16[8,64,128]{2,1,0:T(8,128)(2,1)S(1)}, u32[]{:S(2)}, u32[]{:S(2)}) collective-permute-start(bf16[8,64,128]{2,1,0:T(8,128)(2,1)} %get-tuple-element.22), channel_id=1, source_target_pairs={{0,14},{2,0},{4,2},{6,4},{8,6},{10,8},{12,10},{14,12},{1,15},{3,1}... | collective-permute-start | bytes 393224 | tf_op jit(solution)/shard_map/ppermute | solution.py:262
  61.1 4.0 %copy-start.8 = (bf16[8,64,128]{2,1,0:T(8,128)(2,1)}, bf16[8,64,128]{2,1,0:T(8,128)(2,1)S(1)}, u32[]{:S(2)}) copy-start(bf16[8,64,128]{2,1,0:T(8,128)(2,1)S(1)} %collective-permute-done.2.refs_3_) | copy-start | bytes 393220
  61.1 4.0 %copy-start.9 = (bf16[8,64,128]{2,1,0:T(8,128)(2,1)}, bf16[8,64,128]{2,1,0:T(8,128)(2,1)S(1)}, u32[]{:S(2)}) copy-start(bf16[8,64,128]{2,1,0:T(8,128)(2,1)S(1)} %collective-permute-done.3.refs_4_) | copy-start | bytes 393220
  61.6 3.5 %copy-start.10 = (bf16[8,64,128]{2,1,0:T(8,128)(2,1)}, bf16[8,64,128]{2,1,0:T(8,128)(2,1)S(1)}, u32[]{:S(2)}) copy-start(bf16[8,64,128]{2,1,0:T(8,128)(2,1)S(1)} %collective-permute-done.4.refs_5_) | copy-start | bytes 393220
  61.6 3.5 %copy-start.11 = (bf16[8,64,128]{2,1,0:T(8,128)(2,1)}, bf16[8,64,128]{2,1,0:T(8,128)(2,1)S(1)}, u32[]{:S(2)}) copy-start(bf16[8,64,128]{2,1,0:T(8,128)(2,1)S(1)} %collective-permute-done.5.refs_6_) | copy-start | bytes 393220
  65.1 0.7 copy-start.12
  74.6 7.2 %collective-permute-start.8 = (bf16[48,64,128]{2,1,0:T(8,128)(2,1)S(1)}, bf16[48,64,128]{2,1,0:T(8,128)(2,1)S(1)}, u32[]{:S(2)}, u32[]{:S(2)}) collective-permute-start(bf16[48,64,128]{2,1,0:T(8,128)(2,1)S(1)} %get-tuple-element.27), channel_id=1, source_target_pairs={{0,1},{1,0},{2,3},{3,2},{4,5},{5,4},{6,7},{7,6},{8,9},{9,8},{10,11... | collective-permute-start | bytes 2359304 | tf_op jit(solution)/shard_map/ppermute | solution.py:277
  79.9 3.4 %collective-permute-start.7 = (bf16[16,64,128]{2,1,0:T(8,128)(2,1)S(1)}, bf16[16,64,128]{2,1,0:T(8,128)(2,1)S(1)}, u32[]{:S(2)}, u32[]{:S(2)}) collective-permute-start(bf16[16,64,128]{2,1,0:T(8,128)(2,1)S(1)} %get-tuple-element.26), channel_id=1, source_target_pairs={{0,1},{1,0},{2,3},{3,2},{4,5},{5,4},{6,7},{7,6},{8,9},{9,8},{10,11... | collective-permute-start | bytes 786440 | tf_op jit(solution)/shard_map/ppermute | solution.py:278

commit v7 on v5

--- a/solution.py
+++ b/solution.py
@@ -5,7 +5,7 @@
 from jax.experimental.pallas import tpu as pltpu
 from jax.sharding import PartitionSpec as P
 
-GROUP = 16
+GROUP = 32
 TOGETHER = 8
 SENDS = (4, 3, 5, 2, 6, 1, 7)
 SPLITS = 4

time: 83.7 us -> 83.5 us (level)
  no operation moved by 1% of the time
where the time goes in v7:
time: 83.5 us; the launch traced here: 83 us
  starting transfers between devices  59.8 us (72%)
  Pallas kernels  16.6 us (20%)
  waiting for transfers between devices  4.15 us (5%)
  local copies, waits for them, and re-layouts  1.53 us (2%)
  between operations  0.98 us (1%)
    ppermute x7, starting transfers between devices, shards(): parts.append(lax.ppermute(partials[step], 'occ', ring))  37.9 us
    all_to_all x1, starting transfers between devices, shards(): lax.all_to_all(outgoing, 'vir', split_axis=0, concat_axis=0, tiled=True)  14.6 us
    ppermute x1, starting transfers between devices, shards(): received = lax.ppermute(other, 'rep', [(0, 1), (1, 0)])  7.33 us
    pallas_call x1, Pallas kernels, ladder_partials(): pl.pallas_call(ladder_kernel, grid=(items // GROUP,), in_specs=[pl.BlockS...  6.55 us
    pallas_call x1, Pallas kernels, cycle_partials(): pl.pallas_call(cycle_kernel, grid_spec=pltpu.PrefetchScalarGridSpec(num_s...  4.21 us
    ppermute x7, waiting for transfers between devices, shards(): parts.append(lax.ppermute(partials[step], 'occ', ring))  3.96 us
    pallas_call x1, Pallas kernels, gather_tiles(): pl.pallas_call(gather_kernel, in_specs=[pl.BlockSpec(memory_space=pltpu.H...  2.7 us
    pallas_call x1, Pallas kernels, sum_parts(): pl.pallas_call(sum_kernel, in_specs=[pl.BlockSpec(memory_space=pltpu.VMEM...  2.08 us
  transfers between devices with their start and end apart: 9, of which 3 were waited for; matrix products, arithmetic and copies ran while one was open for 1% of the time, Pallas kernels for 8%

profile of v7, /device:TPU:1, one launch (start us, length us, event | category | flops | bytes accessed | tf_op | source)
XLA Modules:
  0.0 83.0 jit_solution(7150371344367964737)
XLA Ops:
  0.6 0.0 copy-start
  0.6 2.7 %outgoing_tiles.1 = bf16[64,2,64,128]{3,2,1,0:T(8,128)(2,1)} custom-call(s32[64]{0:T(128)} %order_hbm.1, s32[2,64]{1,0:T(2,128)} %bitcast.30, bf16[64,64,128]{2,1,0:T(8,128)(2,1)} %bitcast.20), custom_call_target="tpu_custom_call" | custom-call | bytes 4194304 | tf_op jit(solution)/shard_map/outgoing_tiles/pallas_call | solution.py:54
  3.3 0.0 copy-start.1
  3.4 0.0 copy-start.2
  3.4 0.0 copy-start.3
  3.4 0.0 copy-start.4
  3.4 14.6 %all-to-all-start = ((bf16[64,2,64,128]{3,2,1,0:T(8,128)(2,1)}), bf16[64,2,64,128]{3,2,1,0:T(8,128)(2,1)}, u32[]{:S(2)}, u32[]{:S(2)}) async-start(bf16[64,2,64,128]{3,2,1,0:T(8,128)(2,1)} %outgoing_tiles.1), calls=%async_computation | async-start | bytes 4194304 | tf_op jit(solution)/shard_map/all_to_all | solution.py:238
  18.0 4.2 %cycle_partials.1 = (bf16[8,64,128]{2,1,0:T(8,128)(2,1)}, bf16[8,64,128]{2,1,0:T(8,128)(2,1)}, bf16[8,64,128]{2,1,0:T(8,128)(2,1)}, bf16[8,64,128]{2,1,0:T(8,128...) custom-call(s32[1]{0:T(128)} %bitcast.2.me_ref, ...), custom_call_target="tpu_custom_call" | custom-call | flops 268435456 | bytes 4194304 | tf_op jit(solution)/shard_map/cycle_partials/pallas_call | solution.py:98
  22.2 0.0 copy-start.5
  22.2 14.4 %collective-permute-start = (bf16[8,64,128]{2,1,0:T(8,128)(2,1)}, bf16[8,64,128]{2,1,0:T(8,128)(2,1)S(1)}, u32[]{:S(2)}, u32[]{:S(2)}) collective-permute-start(bf16[8,64,128]{2,1,0:T(8,128)(2,1)} %get-tuple-element.22), channel_id=1, source_target_pairs={{0,8},{2,10},{4,12},{6,14},{8,0},{10,2},{12,4},{14,6},{1,9},{3,11}... | collective-permute-start | bytes 393224 | tf_op jit(solution)/shard_map/ppermute | solution.py:246
  36.7 7.6 %collective-permute-start.1 = (bf16[8,64,128]{2,1,0:T(8,128)(2,1)}, bf16[8,64,128]{2,1,0:T(8,128)(2,1)S(1)}, u32[]{:S(2)}, u32[]{:S(2)}) collective-permute-start(bf16[8,64,128]{2,1,0:T(8,128)(2,1)} %get-tuple-element.23), channel_id=1, source_target_pairs={{0,6},{2,8},{4,10},{6,12},{8,14},{10,0},{12,2},{14,4},{1,7},{3,9},... | collective-permute-start | bytes 393224 | tf_op jit(solution)/shard_map/ppermute | solution.py:246
  44.3 1.9 %collective-permute-start.2 = (bf16[8,64,128]{2,1,0:T(8,128)(2,1)}, bf16[8,64,128]{2,1,0:T(8,128)(2,1)S(1)}, u32[]{:S(2)}, u32[]{:S(2)}) collective-permute-start(bf16[8,64,128]{2,1,0:T(8,128)(2,1)} %get-tuple-element.24), channel_id=1, source_target_pairs={{0,10},{2,12},{4,14},{6,0},{8,2},{10,4},{12,6},{14,8},{1,11},{3,13... | collective-permute-start | bytes 393224 | tf_op jit(solution)/shard_map/ppermute | solution.py:246
  46.2 4.6 %collective-permute-start.3 = (bf16[8,64,128]{2,1,0:T(8,128)(2,1)}, bf16[8,64,128]{2,1,0:T(8,128)(2,1)S(1)}, u32[]{:S(2)}, u32[]{:S(2)}) collective-permute-start(bf16[8,64,128]{2,1,0:T(8,128)(2,1)} %get-tuple-element.25), channel_id=1, source_target_pairs={{0,4},{2,6},{4,8},{6,10},{8,12},{10,14},{12,0},{14,2},{1,5},{3,7},... | collective-permute-start | bytes 393224 | tf_op jit(solution)/shard_map/ppermute | solution.py:246
  50.8 2.8 %collective-permute-start.4 = (bf16[8,64,128]{2,1,0:T(8,128)(2,1)}, bf16[8,64,128]{2,1,0:T(8,128)(2,1)S(1)}, u32[]{:S(2)}, u32[]{:S(2)}) collective-permute-start(bf16[8,64,128]{2,1,0:T(8,128)(2,1)} %get-tuple-element.26), channel_id=1, source_target_pairs={{0,12},{2,14},{4,0},{6,2},{8,4},{10,6},{12,8},{14,10},{1,13},{3,15... | collective-permute-start | bytes 393224 | tf_op jit(solution)/shard_map/ppermute | solution.py:246
  53.7 0.2 dynamic-slice_bitcast_fusion
  53.8 0.2 copy.13
  54.1 2.7 %collective-permute-start.5 = (bf16[8,64,128]{2,1,0:T(8,128)(2,1)}, bf16[8,64,128]{2,1,0:T(8,128)(2,1)S(1)}, u32[]{:S(2)}, u32[]{:S(2)}) collective-permute-start(bf16[8,64,128]{2,1,0:T(8,128)(2,1)} %get-tuple-element.27), channel_id=1, source_target_pairs={{0,2},{2,4},{4,6},{6,8},{8,10},{10,12},{12,14},{14,0},{1,3},{3,5},... | collective-permute-start | bytes 393224 | tf_op jit(solution)/shard_map/ppermute | solution.py:246
  56.8 0.0 collective-permute-done.1.refs_2_
  56.8 3.8 %collective-permute-start.6 = (bf16[8,64,128]{2,1,0:T(8,128)(2,1)}, bf16[8,64,128]{2,1,0:T(8,128)(2,1)S(1)}, u32[]{:S(2)}, u32[]{:S(2)}) collective-permute-start(bf16[8,64,128]{2,1,0:T(8,128)(2,1)} %get-tuple-element.28), channel_id=1, source_target_pairs={{0,14},{2,0},{4,2},{6,4},{8,6},{10,8},{12,10},{14,12},{1,15},{3,1}... | collective-permute-start | bytes 393224 | tf_op jit(solution)/shard_map/ppermute | solution.py:246
  60.6 0.2 constant_dynamic-slice_fusion.1
  60.8 0.1 copy.20
  60.9 0.1 copy.19
  61.1 0.0 collective-permute-done.2.refs_3_
  61.2 0.5 collective-permute-done.4.refs_5_
  61.7 3.5 %collective-permute-done.6.refs_7_ = bf16[8,64,128]{2,1,0:T(8,128)(2,1)S(1)} collective-permute-done((bf16[8,64,128]{2,1,0:T(8,128)(2,1)}, bf16[8,64,128]{2,1,0:T(8,128)(2,1)S(1)}, u32[]{:S(2)}, u32[]{:S(2)}) %collective-permute-start.6) | collective-permute-done | bytes 131104 | tf_op jit(solution)/shard_map/ppermute | solution.py:246
  65.1 0.0 all-to-all-done.amps_ref
  65.1 0.6 copy-done.12
  65.8 6.5 %ladder_partials.1 = (bf16[64,64,128]{2,1,0:T(8,128)(2,1)S(1)}, bf16[64,64,128]{2,1,0:T(8,128)(2,1)S(1)}) custom-call(bf16[64,2,64,128]{3,2,1,0:T(8,128)(2,1)} %all-to-all-done.amps_ref, bf16[128,768]{1,0:T(8,128)(2,1)S(1)} %pad_maximum_fusion.left_ref, bf16[2,768,128]{2,1,0:T(8,128)(2,1)S(1)} %bitcast.23), custom_call_target="tpu_custom_call" | custom-call | flops 4294967296 | bytes 6291456 | tf_op jit(solution)/shard_map/ladder_partials/pallas_call | solution.py:154
  72.4 7.3 %collective-permute-start.7 = (bf16[64,64,128]{2,1,0:T(8,128)(2,1)S(1)}, bf16[64,64,128]{2,1,0:T(8,128)(2,1)S(1)}, u32[]{:S(2)}, u32[]{:S(2)}) collective-permute-start(bf16[64,64,128]{2,1,0:T(8,128)(2,1)S(1)} %get-tuple-element.39), channel_id=1, source_target_pairs={{0,1},{1,0},{2,3},{3,2},{4,5},{5,4},{6,7},{7,6},{8,9},{9,8},{10,11... | collective-permute-start | bytes 3145736 | tf_op jit(solution)/shard_map/ppermute | solution.py:259
  79.7 2.1 %sum_parts.1 = bf16[8,64,128]{2,1,0:T(8,128)(2,1)} custom-call(bf16[8,64,128]{2,1,0:T(8,128)(2,1)} %get-tuple-element.29.refs_0_, bf16[8,64,128]{2,1,0:T(8,128)(2,1)} %copy-done.6, bf16[8,64,128]{2,1,0:T(8,128)(2,1)} %copy-done.7, bf16[8,64,128]{2,1,0:T(8,128)(2,1)} %copy-done.8, bf16[8,64,128]{2,1,0:T(8,128)(2,1)} %copy-done.9, ...), custom_call_target="tpu_custom_call" | custom-call | flops 524288 | bytes 1179648 | tf_op jit(solution)/shard_map/sum_parts/pallas_call | solution.py:186
  81.8 0.2 collective-permute-done.7.received_ref
  82.0 1.1 %final_sum.1 = bf16[64,64,128]{2,1,0:T(8,128)(2,1)} custom-call(bf16[64,64,128]{2,1,0:T(8,128)(2,1)S(1)} %get-tuple-element.38.own_ref, bf16[64,64,128]{2,1,0:T(8,128)(2,1)S(1)} %collective-permute-done.7.received_ref), custom_call_target="tpu_custom_call" | custom-call | flops 524288 | bytes 4194304 | tf_op jit(solution)/shard_map/final_sum/pallas_call | solution.py:212
  (24 shorter events, 0.1 us)
Async XLA Ops:
  0.6 53.0 %copy-start = (bf16[6,1,2,128,128]{4,3,2,1,0:T(8,128)(2,1)S(1)}, bf16[6,1,2,128,128]{4,3,2,1,0:T(8,128)(2,1)}, u32[]{:S(2)}) copy-start(bf16[6,1,2,128,128]{4,3,2,1,0:T(8,128)(2,1)} %param.14) | copy-start | bytes 1179652
  3.3 14.6 %copy-start.1 = (bf16[1,1,64,64,128]{4,3,2,1,0:T(8,128)(2,1)S(1)}, bf16[1,1,64,64,128]{4,3,2,1,0:T(8,128)(2,1)}, u32[]{:S(2)}) copy-start(bf16[1,1,64,64,128]{4,3,2,1,0:T(8,128)(2,1)} %param.8) | copy-start | bytes 3145732
  3.4 14.6 %copy-start.2 = (bf16[1,1,64,128,128]{4,3,2,1,0:T(8,128)(2,1)S(1)}, bf16[1,1,64,128,128]{4,3,2,1,0:T(8,128)(2,1)}, u32[]{:S(2)}) copy-start(bf16[1,1,64,128,128]{4,3,2,1,0:T(8,128)(2,1)} %param.9) | copy-start | bytes 6291460
  3.4 14.6 %copy-start.3 = (s32[64,2]{0,1:T(2,128)S(1)}, s32[64,2]{0,1:T(2,128)}, u32[]{:S(2)}) copy-start(s32[64,2]{0,1:T(2,128)} %param.10) | copy-start | bytes 1540
  3.4 14.6 %copy-start.4 = (s32[64,2]{0,1:T(2,128)S(1)}, s32[64,2]{0,1:T(2,128)}, u32[]{:S(2)}) copy-start(s32[64,2]{0,1:T(2,128)} %param.11) | copy-start | bytes 1540
  3.4 61.7 %all-to-all-start = ((bf16[64,2,64,128]{3,2,1,0:T(8,128)(2,1)}), bf16[64,2,64,128]{3,2,1,0:T(8,128)(2,1)}, u32[]{:S(2)}, u32[]{:S(2)}) async-start(bf16[64,2,64,128]{3,2,1,0:T(8,128)(2,1)} %outgoing_tiles.1), calls=%async_computation | async-start | bytes 4194304 | tf_op jit(solution)/shard_map/all_to_all | solution.py:238
  22.2 38.8 %copy-start.5 = (bf16[6,1,2,128,128]{4,3,2,1,0:T(8,128)(2,1)S(1)}, bf16[6,1,2,128,128]{4,3,2,1,0:T(8,128)(2,1)}, u32[]{:S(2)}) copy-start(bf16[6,1,2,128,128]{4,3,2,1,0:T(8,128)(2,1)} %param.15) | copy-start | bytes 1179652
  22.2 31.8 %collective-permute-start = (bf16[8,64,128]{2,1,0:T(8,128)(2,1)}, bf16[8,64,128]{2,1,0:T(8,128)(2,1)S(1)}, u32[]{:S(2)}, u32[]{:S(2)}) collective-permute-start(bf16[8,64,128]{2,1,0:T(8,128)(2,1)} %get-tuple-element.22), channel_id=1, source_target_pairs={{0,8},{2,10},{4,12},{6,14},{8,0},{10,2},{12,4},{14,6},{1,9},{3,11}... | collective-permute-start | bytes 393224 | tf_op jit(solution)/shard_map/ppermute | solution.py:246
  36.7 20.1 %collective-permute-start.1 = (bf16[8,64,128]{2,1,0:T(8,128)(2,1)}, bf16[8,64,128]{2,1,0:T(8,128)(2,1)S(1)}, u32[]{:S(2)}, u32[]{:S(2)}) collective-permute-start(bf16[8,64,128]{2,1,0:T(8,128)(2,1)} %get-tuple-element.23), channel_id=1, source_target_pairs={{0,6},{2,8},{4,10},{6,12},{8,14},{10,0},{12,2},{14,4},{1,7},{3,9},... | collective-permute-start | bytes 393224 | tf_op jit(solution)/shard_map/ppermute | solution.py:246
  44.3 16.8 %collective-permute-start.2 = (bf16[8,64,128]{2,1,0:T(8,128)(2,1)}, bf16[8,64,128]{2,1,0:T(8,128)(2,1)S(1)}, u32[]{:S(2)}, u32[]{:S(2)}) collective-permute-start(bf16[8,64,128]{2,1,0:T(8,128)(2,1)} %get-tuple-element.24), channel_id=1, source_target_pairs={{0,10},{2,12},{4,14},{6,0},{8,2},{10,4},{12,6},{14,8},{1,11},{3,13... | collective-permute-start | bytes 393224 | tf_op jit(solution)/shard_map/ppermute | solution.py:246
  46.2 14.9 %collective-permute-start.3 = (bf16[8,64,128]{2,1,0:T(8,128)(2,1)}, bf16[8,64,128]{2,1,0:T(8,128)(2,1)S(1)}, u32[]{:S(2)}, u32[]{:S(2)}) collective-permute-start(bf16[8,64,128]{2,1,0:T(8,128)(2,1)} %get-tuple-element.25), channel_id=1, source_target_pairs={{0,4},{2,6},{4,8},{6,10},{8,12},{10,14},{12,0},{14,2},{1,5},{3,7},... | collective-permute-start | bytes 393224 | tf_op jit(solution)/shard_map/ppermute | solution.py:246
  50.8 10.8 %collective-permute-start.4 = (bf16[8,64,128]{2,1,0:T(8,128)(2,1)}, bf16[8,64,128]{2,1,0:T(8,128)(2,1)S(1)}, u32[]{:S(2)}, u32[]{:S(2)}) collective-permute-start(bf16[8,64,128]{2,1,0:T(8,128)(2,1)} %get-tuple-element.26), channel_id=1, source_target_pairs={{0,12},{2,14},{4,0},{6,2},{8,4},{10,6},{12,8},{14,10},{1,13},{3,15... | collective-permute-start | bytes 393224 | tf_op jit(solution)/shard_map/ppermute | solution.py:246
  54.0 7.0 %copy-start.6 = (bf16[8,64,128]{2,1,0:T(8,128)(2,1)}, bf16[8,64,128]{2,1,0:T(8,128)(2,1)S(1)}, u32[]{:S(2)}) copy-start(bf16[8,64,128]{2,1,0:T(8,128)(2,1)S(1)} %collective-permute-done.refs_1_) | copy-start | bytes 393220
  54.1 7.6 %collective-permute-start.5 = (bf16[8,64,128]{2,1,0:T(8,128)(2,1)}, bf16[8,64,128]{2,1,0:T(8,128)(2,1)S(1)}, u32[]{:S(2)}, u32[]{:S(2)}) collective-permute-start(bf16[8,64,128]{2,1,0:T(8,128)(2,1)} %get-tuple-element.27), channel_id=1, source_target_pairs={{0,2},{2,4},{4,6},{6,8},{8,10},{10,12},{12,14},{14,0},{1,3},{3,5},... | collective-permute-start | bytes 393224 | tf_op jit(solution)/shard_map/ppermute | solution.py:246
  56.8 4.2 %copy-start.7 = (bf16[8,64,128]{2,1,0:T(8,128)(2,1)}, bf16[8,64,128]{2,1,0:T(8,128)(2,1)S(1)}, u32[]{:S(2)}) copy-start(bf16[8,64,128]{2,1,0:T(8,128)(2,1)S(1)} %collective-permute-done.1.refs_2_) | copy-start | bytes 393220
  56.8 8.3 %collective-permute-start.6 = (bf16[8,64,128]{2,1,0:T(8,128)(2,1)}, bf16[8,64,128]{2,1,0:T(8,128)(2,1)S(1)}, u32[]{:S(2)}, u32[]{:S(2)}) collective-permute-start(bf16[8,64,128]{2,1,0:T(8,128)(2,1)} %get-tuple-element.28), channel_id=1, source_target_pairs={{0,14},{2,0},{4,2},{6,4},{8,6},{10,8},{12,10},{14,12},{1,15},{3,1}... | collective-permute-start | bytes 393224 | tf_op jit(solution)/shard_map/ppermute | solution.py:246
  61.1 11.2 %copy-start.8 = (bf16[8,64,128]{2,1,0:T(8,128)(2,1)}, bf16[8,64,128]{2,1,0:T(8,128)(2,1)S(1)}, u32[]{:S(2)}) copy-start(bf16[8,64,128]{2,1,0:T(8,128)(2,1)S(1)} %collective-permute-done.2.refs_3_) | copy-start | bytes 393220
  61.2 11.2 %copy-start.9 = (bf16[8,64,128]{2,1,0:T(8,128)(2,1)}, bf16[8,64,128]{2,1,0:T(8,128)(2,1)S(1)}, u32[]{:S(2)}) copy-start(bf16[8,64,128]{2,1,0:T(8,128)(2,1)S(1)} %collective-permute-done.3.refs_4_) | copy-start | bytes 393220
  61.7 10.7 %copy-start.10 = (bf16[8,64,128]{2,1,0:T(8,128)(2,1)}, bf16[8,64,128]{2,1,0:T(8,128)(2,1)S(1)}, u32[]{:S(2)}) copy-start(bf16[8,64,128]{2,1,0:T(8,128)(2,1)S(1)} %collective-permute-done.4.refs_5_) | copy-start | bytes 393220
  61.7 3.5 %copy-start.11 = (bf16[8,64,128]{2,1,0:T(8,128)(2,1)}, bf16[8,64,128]{2,1,0:T(8,128)(2,1)S(1)}, u32[]{:S(2)}) copy-start(bf16[8,64,128]{2,1,0:T(8,128)(2,1)S(1)} %collective-permute-done.5.refs_6_) | copy-start | bytes 393220
  65.1 0.7 copy-start.12
  72.4 9.6 %collective-permute-start.7 = (bf16[64,64,128]{2,1,0:T(8,128)(2,1)S(1)}, bf16[64,64,128]{2,1,0:T(8,128)(2,1)S(1)}, u32[]{:S(2)}, u32[]{:S(2)}) collective-permute-start(bf16[64,64,128]{2,1,0:T(8,128)(2,1)S(1)} %get-tuple-element.39), channel_id=1, source_target_pairs={{0,1},{1,0},{2,3},{3,2},{4,5},{5,4},{6,7},{7,6},{8,9},{9,8},{10,11... | collective-permute-start | bytes 3145736 | tf_op jit(solution)/shard_map/ppermute | solution.py:259
